TPU v7x, 256 devices: a whole 4x4x8 slice. The times are simulated.
256 devices in a mesh: clip: 4 (over x), vid: 16 (over z, core), aud: 4 (over y).
Axes of the slice: x: 4, y: 4, z: 8, core: 2. Of those that a mesh axis runs over, the one named last changes fastest.
Arguments:
- video_query: bfloat16 [4, 32768, 1536], P('clip', ('vid', 'aud')), may hold values from -100 to 100
- audio_key: bfloat16 [4, 8192, 1536], P('clip', ('vid', 'aud')), may hold values from -4 to 4
- audio_value: bfloat16 [4, 8192, 1536], P('clip', ('vid', 'aud')), may hold values from -6 to 6
- cross_gate: float32 [1536], replicated, may hold values from 0.5 to 1.5
- grad_out: bfloat16 [4, 32768, 1536], P('clip', ('vid', 'aud')), may hold values from -6 to 6
- pair_blocks: int32 [4, 256, 4], P('clip', ('vid', 'aud')), may hold values from 0 to 63, as said below
- pair_count: int32 [4, 256], P('clip', ('vid', 'aud')), may hold values from 1 to 4
Outputs:
- cross_out: bfloat16 [4, 32768, 1536], P('clip', ('vid', 'aud'))
- query_grad: bfloat16 [4, 32768, 1536], P('clip', ('vid', 'aud'))
- key_grad: bfloat16 [4, 8192, 1536], P('clip', ('vid', 'aud'))
- value_grad: bfloat16 [4, 8192, 1536], P('clip', ('vid', 'aud'))
- gate_grad: float32 [1536], replicated
Inputs may be any that keep to these rules, and one draw needn't show every extreme that they name: pair_blocks[c, b, 0] is b // 4, the time-aligned audio block; every entry lies within 2 blocks of it; entries 1 and later of a row are distinct before they are clipped to the clip's blocks.
All inputs are finite; a program needn't handle non-finite values.
Results may differ from a plain program's by a relative error of at most 0.03.
Values may be sent and summed in bfloat16 or wider, within the bound.
No kernel may reach another device: no remote copies, remote signals or barrier semaphores. Data moves between devices by JAX's collectives and lax.ppermute only.
A program may use at most 128 MiB of HBM per device.

v0:
```python
import math

import jax
import jax.numpy as jnp
from jax import lax
from jax.experimental import pallas as pl
from jax.experimental.pallas import tpu as pltpu
from jax.sharding import PartitionSpec as P

HEADS = 12
HEAD_DIM = 128
BLOCK = 128
REACH = 2
MAXP = 4
WINDOW = 2 * REACH + 1
SCALE = HEAD_DIM**-0.5
LOG2E = math.log2(math.e)
F32 = jnp.float32
BF16 = jnp.bfloat16
TIME = ("vid", "aud")


def nn(a, b):
    return lax.dot_general(a, b, (((1,), (0,)), ((), ())), preferred_element_type=F32)


def nt(a, b):
    return lax.dot_general(a, b, (((1,), (1,)), ((), ())), preferred_element_type=F32)


def tn(a, b):
    return lax.dot_general(a, b, (((0,), (0,)), ((), ())), preferred_element_type=F32)


def weigh(pairs, counts, slot, block):
    times = jnp.int32(0)
    for s in range(MAXP):
        named = pairs[0, block, s] - pairs[0, block, 0] + REACH == slot
        times = times + jnp.where(jnp.logical_and(named, s < counts[0, block]), 1, 0)
    several = jnp.where(times == 2, 1.0, jnp.where(times == 3, math.log2(3.0), 2.0))
    return jnp.where(times == 0, -1e30, jnp.where(times == 1, 0.0, several))


def one_head(queries, upstream, gate, keys, values, bias):
    upf = upstream.astype(F32)
    dattend = (upf * gate).astype(BF16)
    dattend_t = dattend.T
    scores = [nt(k, queries) for k in keys]
    fold = SCALE * LOG2E
    tops = [
        jnp.max(s, axis=0, keepdims=True) * fold + b for s, b in zip(scores, bias)
    ]
    top = tops[0]
    for other in tops[1:]:
        top = jnp.maximum(top, other)
    expo = [jnp.exp2(s * fold + (b - top)) for s, b in zip(scores, bias)]
    total = sum(jnp.sum(e, axis=0, keepdims=True) for e in expo)
    inverse = 1.0 / total
    prob = [e * inverse for e in expo]
    prob16 = [p.astype(BF16) for p in prob]
    attend_t = sum(tn(v, p) for v, p in zip(values, prob16))
    delta = jnp.sum(attend_t * dattend_t.astype(F32), axis=0, keepdims=True)
    attend = attend_t.T
    out = (attend * gate).astype(BF16)
    gate_part = jnp.sum(attend * upf, axis=0, keepdims=True)
    dscore = [
        (p * (nn(v, dattend_t) - delta)).astype(BF16) for p, v in zip(prob, values)
    ]
    qgrad_t = sum(tn(k, d) for k, d in zip(keys, dscore)) * SCALE
    qgrad = qgrad_t.astype(BF16).T
    kparts = [nn(d, queries) * SCALE for d in dscore]
    vparts = [nn(p, dattend) for p in prob16]
    return out, qgrad, gate_part, kparts, vparts


def pair_kernel(
    pairs, counts, q_ref, up_ref, gate_ref,
    k0, v0, kvm1, kvp1, km2, vm2, kp2, vp2,
    out_ref, qgrad_ref, gpart_ref, own_ref, dm1, dp1, dkm2, dvm2, dkp2, dvp2, bias_ref,
):
    @pl.when(pl.program_id(0) == 0)
    def _():
        for slot in range(WINDOW):
            for block in range(4):
                bias_ref[slot : slot + 1, block * BLOCK : (block + 1) * BLOCK] = jnp.full(
                    (1, BLOCK), weigh(pairs, counts, slot, block), F32
                )

    bias = [bias_ref[slot : slot + 1, :] for slot in range(WINDOW)]
    keys = [km2[...], kvm1[0], k0[0], kvp1[0], kp2[...]]
    values = [vm2[...], kvm1[1], v0[0], kvp1[1], vp2[...]]
    out, qgrad, gate_part, kparts, vparts = one_head(
        q_ref[0], up_ref[0], gate_ref[...], keys, values, bias
    )
    out_ref[0] = out
    qgrad_ref[0] = qgrad
    gpart_ref[...] = gate_part
    own_ref[0] = kparts[2]
    own_ref[1] = vparts[2]
    dm1[0] = kparts[1].astype(BF16)
    dm1[1] = vparts[1].astype(BF16)
    dp1[0] = kparts[3].astype(BF16)
    dp1[1] = vparts[3].astype(BF16)
    dkm2[...] = kparts[0].astype(BF16)
    dvm2[...] = vparts[0].astype(BF16)
    dkp2[...] = kparts[4].astype(BF16)
    dvp2[...] = vparts[4].astype(BF16)


def attend_pairs(pairs, counts, queries, upstream, gate, k0, v0, kvm1, kvp1, km2, vm2, kp2, vp2):
    vrows, width = queries.shape[1:]
    smem = pl.BlockSpec(memory_space=pltpu.SMEM)
    video = pl.BlockSpec((1, vrows, HEAD_DIM), lambda h: (0, 0, h))
    own = pl.BlockSpec((1, BLOCK, HEAD_DIM), lambda h: (0, 0, h))
    both = pl.BlockSpec((2, BLOCK, HEAD_DIM), lambda h: (0, 0, h))
    one = pl.BlockSpec((BLOCK, HEAD_DIM), lambda h: (0, h))
    row = pl.BlockSpec((1, HEAD_DIM), lambda h: (0, h))
    shape = jax.ShapeDtypeStruct
    return pl.pallas_call(
        pair_kernel,
        grid=(HEADS,),
        in_specs=[smem, smem, video, video, row, own, own, both, both, one, one, one, one],
        out_specs=[video, video, row, both, both, both, one, one, one, one],
        out_shape=[
            shape((1, vrows, width), BF16),
            shape((1, vrows, width), BF16),
            shape((1, width), F32),
            shape((2, BLOCK, width), F32),
            shape((2, BLOCK, width), BF16),
            shape((2, BLOCK, width), BF16),
        ]
        + [shape((BLOCK, width), BF16)] * 4,
        scratch_shapes=[pltpu.VMEM((8, vrows), F32)],
        compiler_params=pltpu.CompilerParams(
            vmem_limit_bytes=48 * 2**20, dimension_semantics=("arbitrary",)
        ),
        cost_estimate=pl.CostEstimate(
            flops=6 * 10**9, bytes_accessed=16 * 10**6, transcendentals=4 * 10**6
        ),
        name="pairs",
    )(pairs, counts, queries, upstream, gate, k0, v0, kvm1, kvp1, km2, vm2, kp2, vp2)


def moved(shard, by):
    count = lax.axis_size(TIME)
    return lax.ppermute(shard, TIME, [(i, (i + by) % count) for i in range(count)])


def summed(part, axis, masks):
    count = lax.axis_size(axis)
    a, b, c = (
        lax.ppermute(part, axis, [(i, i ^ mask) for i in range(count)]) for mask in masks
    )
    return (part + a) + (b + c)


def shards(video_query, audio_key, audio_value, cross_gate, grad_out, pair_blocks, pair_count):
    width = cross_gate.shape[0]
    key = audio_key[0]
    value = audio_value[0]
    km2 = moved(key, 2)
    vp2 = moved(value, -2)
    both = jnp.stack([key, value])
    kvm1 = moved(both, 1)
    kvp1 = moved(both, -1)
    kp2 = moved(km2, -4)
    vm2 = moved(vp2, 4)
    out, qgrad, gate_part, own, dm1, dp1, dkm2, dvm2, dkp2, dvp2 = attend_pairs(
        pair_blocks, pair_count, video_query, grad_out, cross_gate.reshape(1, width),
        audio_key, audio_value, kvm1, kvp1, km2, vm2, kp2, vp2,
    )
    after = moved(dm1, -1)
    before = moved(dp1, 1)
    kfar = moved(dkp2, 4)
    vfar = moved(dvm2, -4)
    gate_part, kfar, vfar = lax.optimization_barrier((gate_part, kfar, vfar))
    gate_part = summed(gate_part, "clip", (1, 2, 3))
    gate_part, after, before, kfar, vfar = lax.optimization_barrier(
        (gate_part, after, before, kfar, vfar)
    )
    kfar = moved((dkm2.astype(F32) + kfar.astype(F32)).astype(BF16), -2)
    vfar = moved((dvp2.astype(F32) + vfar.astype(F32)).astype(BF16), 2)
    gate_part = summed(gate_part, "vid", (1, 2, 3))
    gate_part = summed(gate_part, "vid", (4, 8, 12))
    gate_part = summed(gate_part, "aud", (1, 2, 3))
    near = own + after.astype(F32) + before.astype(F32)
    key_grad = (near[0] + kfar.astype(F32)).astype(BF16)[None]
    value_grad = (near[1] + vfar.astype(F32)).astype(BF16)[None]
    return (out, qgrad, key_grad, value_grad, gate_part.reshape(width))


def solution(mesh):
    tokens = P("clip", TIME, None)
    in_specs = (tokens, tokens, tokens, P(), tokens, tokens, P("clip", TIME))
    out_specs = (tokens, tokens, tokens, tokens, P())
    return jax.shard_map(shards, mesh=mesh, in_specs=in_specs, out_specs=out_specs, check_vma=False)
```

profile of v0, /device:TPU:2, one launch (start us, length us, event | category | flops | bytes accessed | tf_op | source)
XLA Modules:
  0.0 121.2 jit_solution(5703395056902500417)
XLA Ops:
  0.6 0.0 copy-start.1
  0.6 0.0 copy-start
  0.7 0.0 copy-start.5
  0.7 0.0 copy-start.3
  0.7 0.0 copy-start.2
  0.7 8.0 %collective-permute-start.3 = (bf16[128,1536]{1,0:T(8,128)(2,1)}, bf16[128,1536]{1,0:T(8,128)(2,1)S(1)}, u32[]{:S(2)}, u32[]{:S(2)}) collective-permute-start(bf16[128,1536]{1,0:T(8,128)(2,1)} %bitcast.23), channel_id=1, source_target_pairs={{0,62},{1,63},{2,0},{3,1},{4,2},{5,3},{6,4},{7,5},{8,6},{9,7},{10,... | collective-permute-start | bytes 1179656 | tf_op jit(solution)/shard_map/ppermute | solution.py:146
  8.7 0.0 collective-permute-start.2
  8.7 1.1 constant_dynamic-update-slice_fusion.1
  9.8 1.0 constant_dynamic-update-slice_fusion
  10.8 5.3 %collective-permute-start.1 = (bf16[2,128,1536]{2,1,0:T(8,128)(2,1)S(1)}, bf16[2,128,1536]{2,1,0:T(8,128)(2,1)S(1)}, u32[]{:S(2)}, u32[]{:S(2)}) collective-permute-start(bf16[2,128,1536]{2,1,0:T(8,128)(2,1)S(1)} %constant_dynamic-update-slice_fusion), channel_id=1, source_target_pairs={{0,63},{1,0},{2,1},{3,2},{4,3},{5,4},{6,5},{7,6},{8,7},{9,8},{10,9... | collective-permute-start | bytes 2359304 | tf_op jit(solution)/shard_map/ppermute | solution.py:146
  16.0 0.0 collective-permute-start
  16.0 0.0 collective-permute-done.3.vp2
  16.0 0.4 collective-permute-start.4
  16.4 3.5 %collective-permute-done.2.km2 = bf16[128,1536]{1,0:T(8,128)(2,1)S(1)} collective-permute-done((bf16[128,1536]{1,0:T(8,128)(2,1)}, bf16[128,1536]{1,0:T(8,128)(2,1)S(1)}, u32[]{:S(2)}, u32[]{:S(2)}) %collective-permute-start.2) | collective-permute-done | bytes 393248 | tf_op jit(solution)/shard_map/ppermute | solution.py:146
  19.9 14.0 %collective-permute-start.5 = (bf16[128,1536]{1,0:T(8,128)(2,1)S(1)}, bf16[128,1536]{1,0:T(8,128)(2,1)S(1)}, u32[]{:S(2)}, u32[]{:S(2)}) collective-permute-start(bf16[128,1536]{1,0:T(8,128)(2,1)S(1)} %collective-permute-done.2.km2), channel_id=1, source_target_pairs={{0,60},{1,61},{2,62},{3,63},{4,0},{5,1},{6,2},{7,3},{8,4},{9,5},{1... | collective-permute-start | bytes 1179656 | tf_op jit(solution)/shard_map/ppermute | solution.py:146
  33.9 0.0 collective-permute-done.4.vm2
  33.9 5.3 %collective-permute-done.5.kp2 = bf16[128,1536]{1,0:T(8,128)(2,1)S(1)} collective-permute-done((bf16[128,1536]{1,0:T(8,128)(2,1)S(1)}, bf16[128,1536]{1,0:T(8,128)(2,1)S(1)}, u32[]{:S(2)}, u32[]{:S(2)}) %collective-permute-start.5) | collective-permute-done | bytes 393248 | tf_op jit(solution)/shard_map/ppermute | solution.py:146
  39.2 3.5 %collective-permute-done.1.kvp1 = bf16[2,128,1536]{2,1,0:T(8,128)(2,1)S(1)} collective-permute-done((bf16[2,128,1536]{2,1,0:T(8,128)(2,1)S(1)}, bf16[2,128,1536]{2,1,0:T(8,128)(2,1)S(1)}, u32[]{:S(2)}, u32[]{:S(2)}) %collective-permute-start.1) | collective-permute-done | bytes 786464 | tf_op jit(solution)/shard_map/ppermute | solution.py:146
  42.7 0.0 collective-permute-done.kvm1
  42.7 0.9 copy-done.6
  43.5 0.9 copy-done.7
  44.5 0.0 copy-done.3
  44.5 24.2 %pairs.2 = (bf16[1,512,1536]{2,1,0:T(8,128)(2,1)}, bf16[1,512,1536]{2,1,0:T(8,128)(2,1)}, f32[1,1536]{1,0:T(1,128)S(1)}, f32[2,128,1536]{2,1,0:T(8,128)}, bf16[2...) custom-call(s32[1,4,4]{2,1,0:T(4,128)S(1)} %copy-done.2, ...), custom_call_target="tpu_custom_call" | custom-call | flops 6000000000 | bytes 16000000 | tf_op jit(solution)/shard_map/pairs/pallas_call | solution.py:119
  68.7 2.9 %collective-permute-start.6 = (bf16[128,1536]{1,0:T(8,128)(2,1)S(1)}, bf16[128,1536]{1,0:T(8,128)(2,1)S(1)}, u32[]{:S(2)}, u32[]{:S(2)}) collective-permute-start(bf16[128,1536]{1,0:T(8,128)(2,1)S(1)} %get-tuple-element.27), channel_id=1, source_target_pairs={{0,4},{1,5},{2,6},{3,7},{4,8},{5,9},{6,10},{7,11},{8,12},{9,13},{1... | collective-permute-start | bytes 1179656 | tf_op jit(solution)/shard_map/ppermute | solution.py:146
  71.5 6.4 %collective-permute-start.7 = (bf16[128,1536]{1,0:T(8,128)(2,1)S(1)}, bf16[128,1536]{1,0:T(8,128)(2,1)S(1)}, u32[]{:S(2)}, u32[]{:S(2)}) collective-permute-start(bf16[128,1536]{1,0:T(8,128)(2,1)S(1)} %get-tuple-element.28), channel_id=1, source_target_pairs={{0,60},{1,61},{2,62},{3,63},{4,0},{5,1},{6,2},{7,3},{8,4},{9,5},{1... | collective-permute-start | bytes 1179656 | tf_op jit(solution)/shard_map/ppermute | solution.py:146
  78.0 0.0 collective-permute-start.11
  78.0 2.0 %collective-permute-start.12 = (bf16[2,128,1536]{2,1,0:T(8,128)(2,1)S(1)}, bf16[2,128,1536]{2,1,0:T(8,128)(2,1)S(1)}, u32[]{:S(2)}, u32[]{:S(2)}) collective-permute-start(bf16[2,128,1536]{2,1,0:T(8,128)(2,1)S(1)} %get-tuple-element.31), channel_id=1, source_target_pairs={{0,1},{1,2},{2,3},{3,4},{4,5},{5,6},{6,7},{7,8},{8,9},{9,10},{10,1... | collective-permute-start | bytes 2359304 | tf_op jit(solution)/shard_map/ppermute | solution.py:146
  80.0 3.4 %collective-permute-done.6 = bf16[128,1536]{1,0:T(8,128)(2,1)S(1)} collective-permute-done((bf16[128,1536]{1,0:T(8,128)(2,1)S(1)}, bf16[128,1536]{1,0:T(8,128)(2,1)S(1)}, u32[]{:S(2)}, u32[]{:S(2)}) %collective-permute-start.6) | collective-permute-done | bytes 393248 | tf_op jit(solution)/shard_map/ppermute | solution.py:146
  83.4 0.0 collective-permute-done.7
  83.4 1.5 %collective-permute-start.10 = (f32[1,1536]{1,0:T(1,128)S(1)}, f32[1,1536]{1,0:T(1,128)S(1)}, u32[]{:S(2)}, u32[]{:S(2)}) collective-permute-start(f32[1,1536]{1,0:T(1,128)S(1)} %get-tuple-element.29), channel_id=1, source_target_pairs={{0,192},{64,128},{128,64},{192,0},{1,193},{65,129},{129,65},{193,1... | collective-permute-start | bytes 18440 | tf_op jit(solution)/shard_map/ppermute | solution.py:152
  84.9 1.1 collective-permute-start.9
  86.0 1.5 %collective-permute-start.8 = (f32[1,1536]{1,0:T(1,128)S(1)}, f32[1,1536]{1,0:T(1,128)S(1)}, u32[]{:S(2)}, u32[]{:S(2)}) collective-permute-start(f32[1,1536]{1,0:T(1,128)S(1)} %get-tuple-element.29), channel_id=1, source_target_pairs={{0,64},{64,0},{128,192},{192,128},{1,65},{65,1},{129,193},{193,129... | collective-permute-start | bytes 18440 | tf_op jit(solution)/shard_map/ppermute | solution.py:152
  87.5 0.0 collective-permute-done.10
  87.5 2.5 %collective-permute-done.9 = f32[1,1536]{1,0:T(1,128)S(1)} collective-permute-done((f32[1,1536]{1,0:T(1,128)S(1)}, f32[1,1536]{1,0:T(1,128)S(1)}, u32[]{:S(2)}, u32[]{:S(2)}) %collective-permute-start.9) | collective-permute-done | bytes 6176 | tf_op jit(solution)/shard_map/ppermute | solution.py:152
  90.0 0.0 collective-permute-done.8
  90.0 1.7 %collective-permute-done.11 = bf16[2,128,1536]{2,1,0:T(8,128)(2,1)S(1)} collective-permute-done((bf16[2,128,1536]{2,1,0:T(8,128)(2,1)S(1)}, bf16[2,128,1536]{2,1,0:T(8,128)(2,1)S(1)}, u32[]{:S(2)}, u32[]{:S(2)}) %collective-permute-start.11) | collective-permute-done | bytes 786464 | tf_op jit(solution)/shard_map/ppermute | solution.py:146
  91.7 1.1 collective-permute-done.12
  92.8 1.7 %collective-permute-start.17 = (f32[1,1536]{1,0:T(1,128)S(1)}, f32[1,1536]{1,0:T(1,128)S(1)}, u32[]{:S(2)}, u32[]{:S(2)}) collective-permute-start(f32[1,1536]{1,0:T(1,128)S(1)} %add_add_fusion.2), channel_id=1, source_target_pairs={{0,12},{4,8},{8,4},{12,0},{16,28},{20,24},{24,20},{28,16},{32,44},... | collective-permute-start | bytes 18440 | tf_op jit(solution)/shard_map/ppermute | solution.py:152
  94.5 2.8 %collective-permute-start.16 = (f32[1,1536]{1,0:T(1,128)S(1)}, f32[1,1536]{1,0:T(1,128)S(1)}, u32[]{:S(2)}, u32[]{:S(2)}) collective-permute-start(f32[1,1536]{1,0:T(1,128)S(1)} %add_add_fusion.2), channel_id=1, source_target_pairs={{0,8},{4,12},{8,0},{12,4},{16,24},{20,28},{24,16},{28,20},{32,40},... | collective-permute-start | bytes 18440 | tf_op jit(solution)/shard_map/ppermute | solution.py:152
  97.3 0.0 collective-permute-start.15
  97.3 0.1 add_convert_fusion.1
  97.4 4.0 %collective-permute-start.13 = (bf16[128,1536]{1,0:T(8,128)(2,1)S(1)}, bf16[128,1536]{1,0:T(8,128)(2,1)S(1)}, u32[]{:S(2)}, u32[]{:S(2)}) collective-permute-start(bf16[128,1536]{1,0:T(8,128)(2,1)S(1)} %add_convert_fusion.1), channel_id=1, source_target_pairs={{0,62},{1,63},{2,0},{3,1},{4,2},{5,3},{6,4},{7,5},{8,6},{9,7},{10,... | collective-permute-start | bytes 1179656 | tf_op jit(solution)/shard_map/ppermute | solution.py:146
  101.4 0.0 collective-permute-done.17
  101.4 0.0 collective-permute-done.16
  101.4 0.0 collective-permute-done.15
  101.5 3.4 %collective-permute-start.20 = (f32[1,1536]{1,0:T(1,128)S(1)}, f32[1,1536]{1,0:T(1,128)S(1)}, u32[]{:S(2)}, u32[]{:S(2)}) collective-permute-start(f32[1,1536]{1,0:T(1,128)S(1)} %add_add_fusion.1), channel_id=1, source_target_pairs={{0,48},{4,52},{8,56},{12,60},{16,32},{20,36},{24,40},{28,44},{32,1... | collective-permute-start | bytes 18440 | tf_op jit(solution)/shard_map/ppermute | solution.py:152
  104.9 1.4 %collective-permute-start.19 = (f32[1,1536]{1,0:T(1,128)S(1)}, f32[1,1536]{1,0:T(1,128)S(1)}, u32[]{:S(2)}, u32[]{:S(2)}) collective-permute-start(f32[1,1536]{1,0:T(1,128)S(1)} %add_add_fusion.1), channel_id=1, source_target_pairs={{0,32},{4,36},{8,40},{12,44},{16,48},{20,52},{24,56},{28,60},{32,0... | collective-permute-start | bytes 18440 | tf_op jit(solution)/shard_map/ppermute | solution.py:152
  106.3 1.9 %collective-permute-start.18 = (f32[1,1536]{1,0:T(1,128)S(1)}, f32[1,1536]{1,0:T(1,128)S(1)}, u32[]{:S(2)}, u32[]{:S(2)}) collective-permute-start(f32[1,1536]{1,0:T(1,128)S(1)} %add_add_fusion.1), channel_id=1, source_target_pairs={{0,16},{4,20},{8,24},{12,28},{16,0},{20,4},{24,8},{28,12},{32,48},... | collective-permute-start | bytes 18440 | tf_op jit(solution)/shard_map/ppermute | solution.py:152
  108.2 0.1 add_convert_fusion
  108.3 0.1 collective-permute-start.14
  108.4 0.0 collective-permute-done.20
  108.5 4.0 %collective-permute-done.19 = f32[1,1536]{1,0:T(1,128)S(1)} collective-permute-done((f32[1,1536]{1,0:T(1,128)S(1)}, f32[1,1536]{1,0:T(1,128)S(1)}, u32[]{:S(2)}, u32[]{:S(2)}) %collective-permute-start.19) | collective-permute-done | bytes 6176 | tf_op jit(solution)/shard_map/ppermute | solution.py:152
  112.5 0.0 collective-permute-done.18
  112.5 0.1 collective-permute-start.23
  112.6 1.6 %collective-permute-start.22 = (f32[1,1536]{1,0:T(1,128)S(1)}, f32[1,1536]{1,0:T(1,128)S(1)}, u32[]{:S(2)}, u32[]{:S(2)}) collective-permute-start(f32[1,1536]{1,0:T(1,128)S(1)} %add_add_fusion), channel_id=1, source_target_pairs={{0,2},{1,3},{2,0},{3,1},{4,6},{5,7},{6,4},{7,5},{8,10},{9,11},{10,... | collective-permute-start | bytes 18440 | tf_op jit(solution)/shard_map/ppermute | solution.py:152
  114.1 2.5 %collective-permute-start.21 = (f32[1,1536]{1,0:T(1,128)S(1)}, f32[1,1536]{1,0:T(1,128)S(1)}, u32[]{:S(2)}, u32[]{:S(2)}) collective-permute-start(f32[1,1536]{1,0:T(1,128)S(1)} %add_add_fusion), channel_id=1, source_target_pairs={{0,1},{1,0},{2,3},{3,2},{4,5},{5,4},{6,7},{7,6},{8,9},{9,8},{10,11... | collective-permute-start | bytes 18440 | tf_op jit(solution)/shard_map/ppermute | solution.py:152
  116.7 0.3 convert_add_fusion
  117.0 2.5 %collective-permute-done.23 = f32[1,1536]{1,0:T(1,128)S(1)} collective-permute-done((f32[1,1536]{1,0:T(1,128)S(1)}, f32[1,1536]{1,0:T(1,128)S(1)}, u32[]{:S(2)}, u32[]{:S(2)}) %collective-permute-start.23) | collective-permute-done | bytes 6176 | tf_op jit(solution)/shard_map/ppermute | solution.py:152
  119.4 0.0 collective-permute-done.22
  119.4 0.0 collective-permute-done.21
  119.4 0.6 add_reduce_fusion
  120.1 0.0 collective-permute-done.13
  120.1 0.0 collective-permute-done.14
  120.1 1.1 fusion.5
  (12 shorter events, 0.1 us)
Async XLA Ops:
  0.6 43.8 %copy-start.1 = (bf16[1,128,1536]{2,1,0:T(8,128)(2,1)S(1)}, bf16[1,128,1536]{2,1,0:T(8,128)(2,1)}, u32[]{:S(2)}) copy-start(bf16[1,128,1536]{2,1,0:T(8,128)(2,1)} %v0.1) | copy-start | bytes 1179652
  0.6 43.8 %copy-start = (bf16[1,128,1536]{2,1,0:T(8,128)(2,1)S(1)}, bf16[1,128,1536]{2,1,0:T(8,128)(2,1)}, u32[]{:S(2)}) copy-start(bf16[1,128,1536]{2,1,0:T(8,128)(2,1)} %k0.1) | copy-start | bytes 1179652
  0.7 33.2 %copy-start.5 = (f32[1536]{0:T(1024)S(1)}, f32[1536]{0:T(1024)}, u32[]{:S(2)}) copy-start(f32[1536]{0:T(1024)} %param.10) | copy-start | bytes 18436
  0.7 43.8 %copy-start.3 = (s32[1,4]{1,0:T(1,128)S(1)}, s32[1,4]{1,0:T(1,128)}, u32[]{:S(2)}) copy-start(s32[1,4]{1,0:T(1,128)} %counts.1) | copy-start | bytes 52
  0.7 43.8 %copy-start.2 = (s32[1,4,4]{2,1,0:T(4,128)S(1)}, s32[1,4,4]{2,1,0:T(4,128)}, u32[]{:S(2)}) copy-start(s32[1,4,4]{2,1,0:T(4,128)} %pairs.3) | copy-start | bytes 196
  0.7 15.4 %collective-permute-start.3 = (bf16[128,1536]{1,0:T(8,128)(2,1)}, bf16[128,1536]{1,0:T(8,128)(2,1)S(1)}, u32[]{:S(2)}, u32[]{:S(2)}) collective-permute-start(bf16[128,1536]{1,0:T(8,128)(2,1)} %bitcast.23), channel_id=1, source_target_pairs={{0,62},{1,63},{2,0},{3,1},{4,2},{5,3},{6,4},{7,5},{8,6},{9,7},{10,... | collective-permute-start | bytes 1179656 | tf_op jit(solution)/shard_map/ppermute | solution.py:146
  8.7 11.2 %collective-permute-start.2 = (bf16[128,1536]{1,0:T(8,128)(2,1)}, bf16[128,1536]{1,0:T(8,128)(2,1)S(1)}, u32[]{:S(2)}, u32[]{:S(2)}) collective-permute-start(bf16[128,1536]{1,0:T(8,128)(2,1)} %bitcast.22), channel_id=1, source_target_pairs={{0,2},{1,3},{2,4},{3,5},{4,6},{5,7},{6,8},{7,9},{8,10},{9,11},{10,... | collective-permute-start | bytes 1179656 | tf_op jit(solution)/shard_map/ppermute | solution.py:146
  10.8 31.9 %collective-permute-start.1 = (bf16[2,128,1536]{2,1,0:T(8,128)(2,1)S(1)}, bf16[2,128,1536]{2,1,0:T(8,128)(2,1)S(1)}, u32[]{:S(2)}, u32[]{:S(2)}) collective-permute-start(bf16[2,128,1536]{2,1,0:T(8,128)(2,1)S(1)} %constant_dynamic-update-slice_fusion), channel_id=1, source_target_pairs={{0,63},{1,0},{2,1},{3,2},{4,3},{5,4},{6,5},{7,6},{8,7},{9,8},{10,9... | collective-permute-start | bytes 2359304 | tf_op jit(solution)/shard_map/ppermute | solution.py:146
  16.0 26.6 %collective-permute-start = (bf16[2,128,1536]{2,1,0:T(8,128)(2,1)S(1)}, bf16[2,128,1536]{2,1,0:T(8,128)(2,1)S(1)}, u32[]{:S(2)}, u32[]{:S(2)}) collective-permute-start(bf16[2,128,1536]{2,1,0:T(8,128)(2,1)S(1)} %constant_dynamic-update-slice_fusion), channel_id=1, source_target_pairs={{0,1},{1,2},{2,3},{3,4},{4,5},{5,6},{6,7},{7,8},{8,9},{9,10},{10,1... | collective-permute-start | bytes 2359304 | tf_op jit(solution)/shard_map/ppermute | solution.py:146
  16.0 17.8 %collective-permute-start.4 = (bf16[128,1536]{1,0:T(8,128)(2,1)S(1)}, bf16[128,1536]{1,0:T(8,128)(2,1)S(1)}, u32[]{:S(2)}, u32[]{:S(2)}) collective-permute-start(bf16[128,1536]{1,0:T(8,128)(2,1)S(1)} %collective-permute-done.3.vp2), channel_id=1, source_target_pairs={{0,4},{1,5},{2,6},{3,7},{4,8},{5,9},{6,10},{7,11},{8,12},{9,13},{1... | collective-permute-start | bytes 1179656 | tf_op jit(solution)/shard_map/ppermute | solution.py:146
  19.9 19.3 %collective-permute-start.5 = (bf16[128,1536]{1,0:T(8,128)(2,1)S(1)}, bf16[128,1536]{1,0:T(8,128)(2,1)S(1)}, u32[]{:S(2)}, u32[]{:S(2)}) collective-permute-start(bf16[128,1536]{1,0:T(8,128)(2,1)S(1)} %collective-permute-done.2.km2), channel_id=1, source_target_pairs={{0,60},{1,61},{2,62},{3,63},{4,0},{5,1},{6,2},{7,3},{8,4},{9,5},{1... | collective-permute-start | bytes 1179656 | tf_op jit(solution)/shard_map/ppermute | solution.py:146
  42.7 0.9 copy-start.6
  43.5 0.9 copy-start.7
  68.6 48.0 %copy-start.4 = (f32[2,128,1536]{2,1,0:T(8,128)S(1)}, f32[2,128,1536]{2,1,0:T(8,128)}, u32[]{:S(2)}) copy-start(f32[2,128,1536]{2,1,0:T(8,128)} %get-tuple-element.25) | copy-start | bytes 4718596
  68.7 14.7 %collective-permute-start.6 = (bf16[128,1536]{1,0:T(8,128)(2,1)S(1)}, bf16[128,1536]{1,0:T(8,128)(2,1)S(1)}, u32[]{:S(2)}, u32[]{:S(2)}) collective-permute-start(bf16[128,1536]{1,0:T(8,128)(2,1)S(1)} %get-tuple-element.27), channel_id=1, source_target_pairs={{0,4},{1,5},{2,6},{3,7},{4,8},{5,9},{6,10},{7,11},{8,12},{9,13},{1... | collective-permute-start | bytes 1179656 | tf_op jit(solution)/shard_map/ppermute | solution.py:146
  71.5 11.9 %collective-permute-start.7 = (bf16[128,1536]{1,0:T(8,128)(2,1)S(1)}, bf16[128,1536]{1,0:T(8,128)(2,1)S(1)}, u32[]{:S(2)}, u32[]{:S(2)}) collective-permute-start(bf16[128,1536]{1,0:T(8,128)(2,1)S(1)} %get-tuple-element.28), channel_id=1, source_target_pairs={{0,60},{1,61},{2,62},{3,63},{4,0},{5,1},{6,2},{7,3},{8,4},{9,5},{1... | collective-permute-start | bytes 1179656 | tf_op jit(solution)/shard_map/ppermute | solution.py:146
  78.0 13.8 %collective-permute-start.11 = (bf16[2,128,1536]{2,1,0:T(8,128)(2,1)S(1)}, bf16[2,128,1536]{2,1,0:T(8,128)(2,1)S(1)}, u32[]{:S(2)}, u32[]{:S(2)}) collective-permute-start(bf16[2,128,1536]{2,1,0:T(8,128)(2,1)S(1)} %get-tuple-element.30), channel_id=1, source_target_pairs={{0,63},{1,0},{2,1},{3,2},{4,3},{5,4},{6,5},{7,6},{8,7},{9,8},{10,9... | collective-permute-start | bytes 2359304 | tf_op jit(solution)/shard_map/ppermute | solution.py:146
  78.0 14.8 %collective-permute-start.12 = (bf16[2,128,1536]{2,1,0:T(8,128)(2,1)S(1)}, bf16[2,128,1536]{2,1,0:T(8,128)(2,1)S(1)}, u32[]{:S(2)}, u32[]{:S(2)}) collective-permute-start(bf16[2,128,1536]{2,1,0:T(8,128)(2,1)S(1)} %get-tuple-element.31), channel_id=1, source_target_pairs={{0,1},{1,2},{2,3},{3,4},{4,5},{5,6},{6,7},{7,8},{8,9},{9,10},{10,1... | collective-permute-start | bytes 2359304 | tf_op jit(solution)/shard_map/ppermute | solution.py:146
  83.4 4.1 %collective-permute-start.10 = (f32[1,1536]{1,0:T(1,128)S(1)}, f32[1,1536]{1,0:T(1,128)S(1)}, u32[]{:S(2)}, u32[]{:S(2)}) collective-permute-start(f32[1,1536]{1,0:T(1,128)S(1)} %get-tuple-element.29), channel_id=1, source_target_pairs={{0,192},{64,128},{128,64},{192,0},{1,193},{65,129},{129,65},{193,1... | collective-permute-start | bytes 18440 | tf_op jit(solution)/shard_map/ppermute | solution.py:152
  84.9 5.1 %collective-permute-start.9 = (f32[1,1536]{1,0:T(1,128)S(1)}, f32[1,1536]{1,0:T(1,128)S(1)}, u32[]{:S(2)}, u32[]{:S(2)}) collective-permute-start(f32[1,1536]{1,0:T(1,128)S(1)} %get-tuple-element.29), channel_id=1, source_target_pairs={{0,128},{64,192},{128,0},{192,64},{1,129},{65,193},{129,1},{193,65... | collective-permute-start | bytes 18440 | tf_op jit(solution)/shard_map/ppermute | solution.py:152
  86.0 4.0 %collective-permute-start.8 = (f32[1,1536]{1,0:T(1,128)S(1)}, f32[1,1536]{1,0:T(1,128)S(1)}, u32[]{:S(2)}, u32[]{:S(2)}) collective-permute-start(f32[1,1536]{1,0:T(1,128)S(1)} %get-tuple-element.29), channel_id=1, source_target_pairs={{0,64},{64,0},{128,192},{192,128},{1,65},{65,1},{129,193},{193,129... | collective-permute-start | bytes 18440 | tf_op jit(solution)/shard_map/ppermute | solution.py:152
  92.8 8.6 %collective-permute-start.17 = (f32[1,1536]{1,0:T(1,128)S(1)}, f32[1,1536]{1,0:T(1,128)S(1)}, u32[]{:S(2)}, u32[]{:S(2)}) collective-permute-start(f32[1,1536]{1,0:T(1,128)S(1)} %add_add_fusion.2), channel_id=1, source_target_pairs={{0,12},{4,8},{8,4},{12,0},{16,28},{20,24},{24,20},{28,16},{32,44},... | collective-permute-start | bytes 18440 | tf_op jit(solution)/shard_map/ppermute | solution.py:152
  94.5 6.9 %collective-permute-start.16 = (f32[1,1536]{1,0:T(1,128)S(1)}, f32[1,1536]{1,0:T(1,128)S(1)}, u32[]{:S(2)}, u32[]{:S(2)}) collective-permute-start(f32[1,1536]{1,0:T(1,128)S(1)} %add_add_fusion.2), channel_id=1, source_target_pairs={{0,8},{4,12},{8,0},{12,4},{16,24},{20,28},{24,16},{28,20},{32,40},... | collective-permute-start | bytes 18440 | tf_op jit(solution)/shard_map/ppermute | solution.py:152
  97.3 4.1 %collective-permute-start.15 = (f32[1,1536]{1,0:T(1,128)S(1)}, f32[1,1536]{1,0:T(1,128)S(1)}, u32[]{:S(2)}, u32[]{:S(2)}) collective-permute-start(f32[1,1536]{1,0:T(1,128)S(1)} %add_add_fusion.2), channel_id=1, source_target_pairs={{0,4},{4,0},{8,12},{12,8},{16,20},{20,16},{24,28},{28,24},{32,36},... | collective-permute-start | bytes 18440 | tf_op jit(solution)/shard_map/ppermute | solution.py:152
  97.4 22.7 %collective-permute-start.13 = (bf16[128,1536]{1,0:T(8,128)(2,1)S(1)}, bf16[128,1536]{1,0:T(8,128)(2,1)S(1)}, u32[]{:S(2)}, u32[]{:S(2)}) collective-permute-start(bf16[128,1536]{1,0:T(8,128)(2,1)S(1)} %add_convert_fusion.1), channel_id=1, source_target_pairs={{0,62},{1,63},{2,0},{3,1},{4,2},{5,3},{6,4},{7,5},{8,6},{9,7},{10,... | collective-permute-start | bytes 1179656 | tf_op jit(solution)/shard_map/ppermute | solution.py:146
  101.5 7.0 %collective-permute-start.20 = (f32[1,1536]{1,0:T(1,128)S(1)}, f32[1,1536]{1,0:T(1,128)S(1)}, u32[]{:S(2)}, u32[]{:S(2)}) collective-permute-start(f32[1,1536]{1,0:T(1,128)S(1)} %add_add_fusion.1), channel_id=1, source_target_pairs={{0,48},{4,52},{8,56},{12,60},{16,32},{20,36},{24,40},{28,44},{32,1... | collective-permute-start | bytes 18440 | tf_op jit(solution)/shard_map/ppermute | solution.py:152
  104.9 7.6 %collective-permute-start.19 = (f32[1,1536]{1,0:T(1,128)S(1)}, f32[1,1536]{1,0:T(1,128)S(1)}, u32[]{:S(2)}, u32[]{:S(2)}) collective-permute-start(f32[1,1536]{1,0:T(1,128)S(1)} %add_add_fusion.1), channel_id=1, source_target_pairs={{0,32},{4,36},{8,40},{12,44},{16,48},{20,52},{24,56},{28,60},{32,0... | collective-permute-start | bytes 18440 | tf_op jit(solution)/shard_map/ppermute | solution.py:152
  106.3 6.1 %collective-permute-start.18 = (f32[1,1536]{1,0:T(1,128)S(1)}, f32[1,1536]{1,0:T(1,128)S(1)}, u32[]{:S(2)}, u32[]{:S(2)}) collective-permute-start(f32[1,1536]{1,0:T(1,128)S(1)} %add_add_fusion.1), channel_id=1, source_target_pairs={{0,16},{4,20},{8,24},{12,28},{16,0},{20,4},{24,8},{28,12},{32,48},... | collective-permute-start | bytes 18440 | tf_op jit(solution)/shard_map/ppermute | solution.py:152
  108.3 11.7 %collective-permute-start.14 = (bf16[128,1536]{1,0:T(8,128)(2,1)S(1)}, bf16[128,1536]{1,0:T(8,128)(2,1)S(1)}, u32[]{:S(2)}, u32[]{:S(2)}) collective-permute-start(bf16[128,1536]{1,0:T(8,128)(2,1)S(1)} %add_convert_fusion), channel_id=1, source_target_pairs={{0,2},{1,3},{2,4},{3,5},{4,6},{5,7},{6,8},{7,9},{8,10},{9,11},{10,... | collective-permute-start | bytes 1179656 | tf_op jit(solution)/shard_map/ppermute | solution.py:146
  112.5 7.0 %collective-permute-start.23 = (f32[1,1536]{1,0:T(1,128)S(1)}, f32[1,1536]{1,0:T(1,128)S(1)}, u32[]{:S(2)}, u32[]{:S(2)}) collective-permute-start(f32[1,1536]{1,0:T(1,128)S(1)} %add_add_fusion), channel_id=1, source_target_pairs={{0,3},{1,2},{2,1},{3,0},{4,7},{5,6},{6,5},{7,4},{8,11},{9,10},{10,... | collective-permute-start | bytes 18440 | tf_op jit(solution)/shard_map/ppermute | solution.py:152
  112.6 6.9 %collective-permute-start.22 = (f32[1,1536]{1,0:T(1,128)S(1)}, f32[1,1536]{1,0:T(1,128)S(1)}, u32[]{:S(2)}, u32[]{:S(2)}) collective-permute-start(f32[1,1536]{1,0:T(1,128)S(1)} %add_add_fusion), channel_id=1, source_target_pairs={{0,2},{1,3},{2,0},{3,1},{4,6},{5,7},{6,4},{7,5},{8,10},{9,11},{10,... | collective-permute-start | bytes 18440 | tf_op jit(solution)/shard_map/ppermute | solution.py:152
  114.1 5.3 %collective-permute-start.21 = (f32[1,1536]{1,0:T(1,128)S(1)}, f32[1,1536]{1,0:T(1,128)S(1)}, u32[]{:S(2)}, u32[]{:S(2)}) collective-permute-start(f32[1,1536]{1,0:T(1,128)S(1)} %add_add_fusion), channel_id=1, source_target_pairs={{0,1},{1,0},{2,3},{3,2},{4,5},{5,4},{6,7},{7,6},{8,9},{9,8},{10,11... | collective-permute-start | bytes 18440 | tf_op jit(solution)/shard_map/ppermute | solution.py:152
where the time goes:
time: 121 us
  starting transfers between devices  62.6 us (52%)
  waiting for transfers between devices  27.4 us (23%)
  Pallas kernels  24.2 us (20%)
  local copies, waits for them, and re-layouts  3.89 us (3%)
  other arithmetic  2.24 us (2%)
    ppermute x12, starting transfers between devices, moved(): lax.ppermute(shard, TIME, [(i, (i + by) % count) for i in range(count)])  43.1 us
    pallas_call x1, Pallas kernels, attend_pairs(): pl.pallas_call(pair_kernel, grid=(HEADS,), in_specs=[smem, smem, video, v...  24.2 us
    ppermute x12, starting transfers between devices, summed(): lax.ppermute(part, axis, [(i, i ^ mask) for i in range(count)])  19.6 us
    ppermute x12, waiting for transfers between devices, moved(): lax.ppermute(shard, TIME, [(i, (i + by) % count) for i in range(count)])  18.4 us
    ppermute x12, waiting for transfers between devices, summed(): lax.ppermute(part, axis, [(i, i ^ mask) for i in range(count)])  9.04 us
    unnamed x17, local copies, waits for them, and re-layouts  2.86 us
  transfers between devices with their start and end apart: 24, of which 9 were waited for; matrix products, arithmetic and copies ran while one was open for 3% of the time, Pallas kernels for 0%

commit v1 on v0

v1 whole, which is shorter than its diff:
```python
import math

import jax
import jax.numpy as jnp
from jax import lax
from jax.experimental import pallas as pl
from jax.experimental.pallas import tpu as pltpu
from jax.sharding import PartitionSpec as P

HEADS = 12
HEAD_DIM = 128
BLOCK = 128
REACH = 2
MAXP = 4
WINDOW = 2 * REACH + 1
GROUP = 2
LANES = 256
ROWS = 64
SCALE = HEAD_DIM**-0.5
LOG2E = math.log2(math.e)
F32 = jnp.float32
BF16 = jnp.bfloat16
TIME = ("vid", "aud")


def nn(a, b):
    return lax.dot_general(a, b, (((1,), (0,)), ((), ())), preferred_element_type=F32)


def nt(a, b):
    return lax.dot_general(a, b, (((1,), (1,)), ((), ())), preferred_element_type=F32)


def tn(a, b):
    return lax.dot_general(a, b, (((0,), (0,)), ((), ())), preferred_element_type=F32)


def weigh(pairs, counts, slot, block):
    times = jnp.int32(0)
    for s in range(MAXP):
        named = pairs[0, block, s] - pairs[0, block, 0] + REACH == slot
        times = times + jnp.where(jnp.logical_and(named, s < counts[0, block]), 1, 0)
    several = jnp.where(times == 2, 1.0, jnp.where(times == 3, math.log2(3.0), 2.0))
    return jnp.where(times == 0, -1e30, jnp.where(times == 1, 0.0, several))


def pair_kernel(pairs, counts, q_ref, up_ref, gate_ref, *refs):
    k_refs, v_refs = refs[:WINDOW], refs[WINDOW : 2 * WINDOW]
    out_ref, qgrad_ref, gpart_ref = refs[2 * WINDOW : 2 * WINDOW + 3]
    grad_refs = refs[2 * WINDOW + 3 : 3 * WINDOW + 3]
    bias_ref, expo_ref = refs[3 * WINDOW + 3 :]

    def hand_out(grads, which, cols):
        for w, ref in enumerate(grad_refs):
            ref[which, :, cols] = grads[w * BLOCK : (w + 1) * BLOCK].astype(ref.dtype)

    @pl.when(pl.program_id(0) == 0)
    def _():
        for slot in range(WINDOW):
            for block in range(4):
                bias_ref[slot : slot + 1, block * BLOCK : (block + 1) * BLOCK] = jnp.full(
                    (1, BLOCK), weigh(pairs, counts, slot, block), F32
                )

    fold = SCALE * LOG2E
    vrows = q_ref.shape[1]
    for head in range(GROUP):
        cols = slice(head * HEAD_DIM, (head + 1) * HEAD_DIM)

        keys = jnp.concatenate([r[:, cols] for r in k_refs], axis=0)
        values = jnp.concatenate([r[:, cols] for r in v_refs], axis=0)
        gate = gate_ref[:, cols]
        dattend_t = (up_ref[0, :, cols].astype(F32) * gate).astype(BF16).T
        scaled = []
        inverses = []
        for at in range(0, vrows, LANES):
            lanes = slice(at, at + LANES)
            scores = nt(keys, q_ref[0, lanes, cols])
            bias = [bias_ref[slot : slot + 1, lanes] for slot in range(WINDOW)]
            top = None
            for slot in range(WINDOW):
                part = scores[slot * BLOCK : (slot + 1) * BLOCK]
                part = jnp.max(part, axis=0, keepdims=True) * fold + bias[slot]
                top = part if top is None else jnp.maximum(top, part)
            total = jnp.zeros((8, LANES), F32)
            for slot in range(WINDOW):
                shift = jnp.broadcast_to(bias[slot] - top, (ROWS, LANES))
                for row in range(slot * BLOCK, (slot + 1) * BLOCK, ROWS):
                    expo = jnp.exp2(scores[row : row + ROWS] * fold + shift)
                    for i in range(0, ROWS, 8):
                        total = total + expo[i : i + 8]
                    expo_ref[head, row : row + ROWS, lanes] = expo.astype(BF16)
            inverse = 1.0 / jnp.sum(total, axis=0, keepdims=True)
            inverses.append(inverse)
            scaled.append((dattend_t[:, lanes].astype(F32) * inverse).astype(BF16))
        scaled = jnp.concatenate(scaled, axis=1)
        attend_t = tn(values, expo_ref[head]) * jnp.concatenate(inverses, axis=1)
        attend = attend_t.T
        out_ref[0, :, cols] = (attend * gate).astype(BF16)
        gpart_ref[:, cols] = jnp.sum(
            attend * up_ref[0, :, cols].astype(F32), axis=0, keepdims=True
        )
        hand_out(nt(expo_ref[head], scaled), 1, cols)
        dscore = []
        for at in range(0, vrows, LANES):
            lanes = slice(at, at + LANES)
            dat = scaled[:, lanes]
            delta = jnp.sum(attend_t[:, lanes] * dat.astype(F32), axis=0, keepdims=True)
            dprob = nn(values, dat)
            dscore.append(
                jnp.concatenate(
                    [
                        (
                            expo_ref[head, row : row + ROWS, lanes].astype(F32)
                            * (dprob[row : row + ROWS] - delta)
                        ).astype(BF16)
                        for row in range(0, WINDOW * BLOCK, ROWS)
                    ],
                    axis=0,
                )
            )
        dscore = jnp.concatenate(dscore, axis=1)
        qgrad_ref[0, :, cols] = (tn(keys, dscore) * SCALE).astype(BF16).T
        hand_out(nn(dscore, q_ref[0, :, cols]) * SCALE, 0, cols)


def attend_pairs(pairs, counts, queries, upstream, gate, keys, values):
    vrows, width = queries.shape[1:]
    cols = GROUP * HEAD_DIM
    smem = pl.BlockSpec(memory_space=pltpu.SMEM)
    video = pl.BlockSpec((1, vrows, cols), lambda h: (0, 0, h))
    one = pl.BlockSpec((BLOCK, cols), lambda h: (0, h))
    both = pl.BlockSpec((2, BLOCK, cols), lambda h: (0, 0, h))
    row = pl.BlockSpec((1, cols), lambda h: (0, h))
    shape = jax.ShapeDtypeStruct
    return pl.pallas_call(
        pair_kernel,
        grid=(HEADS // GROUP,),
        in_specs=[smem, smem, video, video, row] + [one] * (2 * WINDOW),
        out_specs=[video, video, row] + [both] * WINDOW,
        out_shape=[
            shape((1, vrows, width), BF16),
            shape((1, vrows, width), BF16),
            shape((1, width), F32),
        ]
        + [shape((2, BLOCK, width), F32 if w == REACH else BF16) for w in range(WINDOW)],
        scratch_shapes=[
            pltpu.VMEM((8, vrows), F32),
            pltpu.VMEM((GROUP, WINDOW * BLOCK, vrows), BF16),
        ],
        compiler_params=pltpu.CompilerParams(
            vmem_limit_bytes=60 * 2**20, dimension_semantics=("arbitrary",)
        ),
        cost_estimate=pl.CostEstimate(
            flops=6 * 10**9, bytes_accessed=16 * 10**6, transcendentals=4 * 10**6
        ),
        name="pairs",
    )(pairs, counts, queries, upstream, gate, *keys, *values)


def moved(shard, by):
    count = lax.axis_size(TIME)
    return lax.ppermute(shard, TIME, [(i, (i + by) % count) for i in range(count)])


def joined(part, arrived):
    return (part.astype(F32) + arrived.astype(F32)).astype(BF16)


def summed(part, axis, masks):
    count = lax.axis_size(axis)
    a, b, c = (
        lax.ppermute(part, axis, [(i, i ^ mask) for i in range(count)]) for mask in masks
    )
    return (part + a) + (b + c)


def shards(video_query, audio_key, audio_value, cross_gate, grad_out, pair_blocks, pair_count):
    width = cross_gate.shape[0]
    key, value = audio_key[0], audio_value[0]
    km1, kp1 = moved(key, 1), moved(key, -1)
    vm1, vp1 = moved(value, 1), moved(value, -1)
    km2, kp2 = moved(km1, 1), moved(kp1, -1)
    vm2, vp2 = moved(vm1, 1), moved(vp1, -1)
    out, qgrad, gate_part, m2, m1, own, p1, p2 = attend_pairs(
        pair_blocks, pair_count, video_query, grad_out, cross_gate.reshape(1, width),
        (km2, km1, key, kp1, kp2), (vm2, vm1, value, vp1, vp2),
    )
    m2, p2 = moved(m2, -1), moved(p2, 1)
    gate_part = summed(gate_part, "clip", (1, 2, 3))
    gate_part = summed(gate_part, "vid", (1, 2, 3))
    gate_part, m2, p2 = lax.optimization_barrier((gate_part, m2, p2))
    m1, p1 = moved(joined(m1, m2), -1), moved(joined(p1, p2), 1)
    gate_part = summed(gate_part, "vid", (4, 8, 12))
    gate_part = summed(gate_part, "aud", (1, 2, 3))
    grads = (own + m1.astype(F32) + p1.astype(F32)).astype(BF16)
    return (out, qgrad, grads[:1], grads[1:], gate_part.reshape(width))


def solution(mesh):
    tokens = P("clip", TIME, None)
    in_specs = (tokens, tokens, tokens, P(), tokens, tokens, P("clip", TIME))
    out_specs = (tokens, tokens, tokens, tokens, P())
    return jax.shard_map(shards, mesh=mesh, in_specs=in_specs, out_specs=out_specs, check_vma=False)
```

time: 121 us -> 110 us (0.909); the launches traced: 121 us -> 108 us
  starting transfers between devices: 62.6 us -> 54 us
  Pallas kernels: 24.2 us -> 18.9 us
    ppermute x12, starting transfers between devices: 43.1 us -> 33.5 us  [moved(): lax.ppermute(shard, TIME, [(i, (i + by) % count) for i in range(count)])]
    pallas_call x1, Pallas kernels: 24.2 us -> 18.9 us  [attend_pairs(): pl.pallas_call(pair_kernel, grid=(HEADS // GROUP,), in_specs=[smem, smem,...]
    ppermute x12, waiting for transfers between devices: 9.04 us -> 12.1 us  [summed(): lax.ppermute(part, axis, [(i, i ^ mask) for i in range(count)])]
    unnamed x17 -> x20, local copies, waits for them, and re-layouts: 2.86 us -> 0.77 us
    ppermute x12, waiting for transfers between devices: 18.4 us -> 16.6 us  [moved(): lax.ppermute(shard, TIME, [(i, (i + by) % count) for i in range(count)])]
    convert_element_type x2 -> x3, other arithmetic: 0.18 us -> 1.82 us  [the longest x2 1.51 us: joined(): return (part.astype(F32) + arrived.astype(F32)).astype(BF16)]
    reshape x1, local copies, waits for them, and re-layouts: 0.01 us -> 1.32 us  [shards(): cross_gate.reshape(1, width)]
  transfers between devices with their start and end apart: 24 -> 24, of which waited for: 9 -> 13; matrix products, arithmetic and copies ran while one was open for 3% -> 3% of each run, Pallas kernels for 0% -> 0%
where the time goes in v1:
time: 110 us; the launch traced here: 108 us
  starting transfers between devices  54 us (49%)
  waiting for transfers between devices  28.6 us (26%)
  Pallas kernels  18.9 us (17%)
  other arithmetic  3.17 us (3%)
  local copies, waits for them, and re-layouts  3.01 us (3%)
    ppermute x12, starting transfers between devices, moved(): lax.ppermute(shard, TIME, [(i, (i + by) % count) for i in range(count)])  33.5 us
    ppermute x12, starting transfers between devices, summed(): lax.ppermute(part, axis, [(i, i ^ mask) for i in range(count)])  20.5 us
    pallas_call x1, Pallas kernels, attend_pairs(): pl.pallas_call(pair_kernel, grid=(HEADS // GROUP,), in_specs=[smem, smem,...  18.9 us
    ppermute x12, waiting for transfers between devices, moved(): lax.ppermute(shard, TIME, [(i, (i + by) % count) for i in range(count)])  16.6 us
    ppermute x12, waiting for transfers between devices, summed(): lax.ppermute(part, axis, [(i, i ^ mask) for i in range(count)])  12.1 us
  transfers between devices with their start and end apart: 24, of which 13 were waited for; matrix products, arithmetic and copies ran while one was open for 3% of the time, Pallas kernels for 0%

profile of v1, /device:TPU:2, one launch (start us, length us, event | category | flops | bytes accessed | tf_op | source)
XLA Modules:
  0.0 108.4 jit_solution(2632664250981961560)
XLA Ops:
  0.6 7.8 %collective-permute-start.2 = (bf16[128,1536]{1,0:T(8,128)(2,1)}, bf16[128,1536]{1,0:T(8,128)(2,1)S(1)}, u32[]{:S(2)}, u32[]{:S(2)}) collective-permute-start(bf16[128,1536]{1,0:T(8,128)(2,1)} %bitcast.2), channel_id=1, source_target_pairs={{0,63},{1,0},{2,1},{3,2},{4,3},{5,4},{6,5},{7,6},{8,7},{9,8},{10,9... | collective-permute-start | bytes 1179656 | tf_op jit(solution)/shard_map/ppermute | solution.py:163
  8.5 0.0 collective-permute-start
  8.5 5.1 %collective-permute-start.6 = (bf16[128,1536]{1,0:T(8,128)(2,1)}, bf16[128,1536]{1,0:T(8,128)(2,1)S(1)}, u32[]{:S(2)}, u32[]{:S(2)}) collective-permute-start(bf16[128,1536]{1,0:T(8,128)(2,1)} %bitcast.5), channel_id=1, source_target_pairs={{0,63},{1,0},{2,1},{3,2},{4,3},{5,4},{6,5},{7,6},{8,7},{9,8},{10,9... | collective-permute-start | bytes 1179656 | tf_op jit(solution)/shard_map/ppermute | solution.py:163
  13.5 0.0 collective-permute-start.4
  13.5 0.6 collective-permute-done.2.refs_3_
  14.1 5.2 %collective-permute-start.3 = (bf16[128,1536]{1,0:T(8,128)(2,1)S(1)}, bf16[128,1536]{1,0:T(8,128)(2,1)S(1)}, u32[]{:S(2)}, u32[]{:S(2)}) collective-permute-start(bf16[128,1536]{1,0:T(8,128)(2,1)S(1)} %collective-permute-done.2.refs_3_), channel_id=1, source_target_pairs={{0,63},{1,0},{2,1},{3,2},{4,3},{5,4},{6,5},{7,6},{8,7},{9,8},{10,9... | collective-permute-start | bytes 1179656 | tf_op jit(solution)/shard_map/ppermute | solution.py:163
  19.3 0.0 collective-permute-done.refs_1_
  19.3 0.3 collective-permute-start.1
  19.6 0.6 collective-permute-done.6.refs_8_
  20.2 5.2 %collective-permute-start.7 = (bf16[128,1536]{1,0:T(8,128)(2,1)S(1)}, bf16[128,1536]{1,0:T(8,128)(2,1)S(1)}, u32[]{:S(2)}, u32[]{:S(2)}) collective-permute-start(bf16[128,1536]{1,0:T(8,128)(2,1)S(1)} %collective-permute-done.6.refs_8_), channel_id=1, source_target_pairs={{0,63},{1,0},{2,1},{3,2},{4,3},{5,4},{6,5},{7,6},{8,7},{9,8},{10,9... | collective-permute-start | bytes 1179656 | tf_op jit(solution)/shard_map/ppermute | solution.py:163
  25.5 0.0 collective-permute-done.4.refs_6_
  25.5 0.0 collective-permute-start.5
  25.5 1.3 %reshape.16.gate_ref = f32[1,1536]{1,0:T(1,128)} reshape(f32[1536]{0:T(1024)} %param.10) | data formatting | bytes 12288 | tf_op jit(solution)/shard_map/reshape | solution.py:186
  26.8 0.0 collective-permute-done.3.refs_4_
  26.8 3.1 %collective-permute-done.1.refs_0_ = bf16[128,1536]{1,0:T(8,128)(2,1)S(1)} collective-permute-done((bf16[128,1536]{1,0:T(8,128)(2,1)S(1)}, bf16[128,1536]{1,0:T(8,128)(2,1)S(1)}, u32[]{:S(2)}, u32[]{:S(2)}) %collective-permute-start.1) | collective-permute-done | bytes 393248 | tf_op jit(solution)/shard_map/ppermute | solution.py:163
  29.9 3.2 %collective-permute-done.7.refs_9_ = bf16[128,1536]{1,0:T(8,128)(2,1)S(1)} collective-permute-done((bf16[128,1536]{1,0:T(8,128)(2,1)S(1)}, bf16[128,1536]{1,0:T(8,128)(2,1)S(1)}, u32[]{:S(2)}, u32[]{:S(2)}) %collective-permute-start.7) | collective-permute-done | bytes 393248 | tf_op jit(solution)/shard_map/ppermute | solution.py:163
  33.1 3.0 %collective-permute-done.5.refs_5_ = bf16[128,1536]{1,0:T(8,128)(2,1)S(1)} collective-permute-done((bf16[128,1536]{1,0:T(8,128)(2,1)S(1)}, bf16[128,1536]{1,0:T(8,128)(2,1)S(1)}, u32[]{:S(2)}, u32[]{:S(2)}) %collective-permute-start.5) | collective-permute-done | bytes 393248 | tf_op jit(solution)/shard_map/ppermute | solution.py:163
  36.1 0.0 copy-done.2
  36.1 0.0 copy-done.3
  36.1 0.0 copy-done.4
  36.1 0.0 copy-done.5
  36.1 0.0 copy-done.6
  36.1 0.7 copy-done.9
  36.9 18.9 %pairs.2 = (bf16[1,512,1536]{2,1,0:T(8,128)(2,1)}, bf16[1,512,1536]{2,1,0:T(8,128)(2,1)}, f32[1,1536]{1,0:T(1,128)}, bf16[2,128,1536]{2,1,0:T(8,128)(2,1)}, bf16...) custom-call(s32[1,4,4]{2,1,0:T(4,128)} %pairs.3, ...), custom_call_target="tpu_custom_call" | custom-call | flops 6000000000 | bytes 16000000 | tf_op jit(solution)/shard_map/pairs/pallas_call | solution.py:136
  55.7 0.0 copy-start.1
  55.7 1.6 %collective-permute-start.10 = (f32[1,1536]{1,0:T(1,128)}, f32[1,1536]{1,0:T(1,128)S(1)}, u32[]{:S(2)}, u32[]{:S(2)}) collective-permute-start(f32[1,1536]{1,0:T(1,128)} %get-tuple-element.20), channel_id=1, source_target_pairs={{0,192},{64,128},{128,64},{192,0},{1,193},{65,129},{129,65},{193,1... | collective-permute-start | bytes 18440 | tf_op jit(solution)/shard_map/ppermute | solution.py:173
  57.3 1.1 %collective-permute-start.9 = (f32[1,1536]{1,0:T(1,128)}, f32[1,1536]{1,0:T(1,128)S(1)}, u32[]{:S(2)}, u32[]{:S(2)}) collective-permute-start(f32[1,1536]{1,0:T(1,128)} %get-tuple-element.20), channel_id=1, source_target_pairs={{0,128},{64,192},{128,0},{192,64},{1,129},{65,193},{129,1},{193,65... | collective-permute-start | bytes 18440 | tf_op jit(solution)/shard_map/ppermute | solution.py:173
  58.4 1.5 %collective-permute-start.8 = (f32[1,1536]{1,0:T(1,128)}, f32[1,1536]{1,0:T(1,128)S(1)}, u32[]{:S(2)}, u32[]{:S(2)}) collective-permute-start(f32[1,1536]{1,0:T(1,128)} %get-tuple-element.20), channel_id=1, source_target_pairs={{0,64},{64,0},{128,192},{192,128},{1,65},{65,1},{129,193},{193,129... | collective-permute-start | bytes 18440 | tf_op jit(solution)/shard_map/ppermute | solution.py:173
  59.9 3.7 %collective-permute-start.14 = (bf16[2,128,1536]{2,1,0:T(8,128)(2,1)}, bf16[2,128,1536]{2,1,0:T(8,128)(2,1)S(1)}, u32[]{:S(2)}, u32[]{:S(2)}) collective-permute-start(bf16[2,128,1536]{2,1,0:T(8,128)(2,1)} %get-tuple-element.21), channel_id=1, source_target_pairs={{0,63},{1,0},{2,1},{3,2},{4,3},{5,4},{6,5},{7,6},{8,7},{9,8},{10,9... | collective-permute-start | bytes 2359304 | tf_op jit(solution)/shard_map/ppermute | solution.py:163
  63.7 0.0 collective-permute-start.15
  63.7 0.0 collective-permute-done.10
  63.7 0.0 collective-permute-done.9
  63.7 0.0 collective-permute-done.8
  63.7 0.7 add_add_fusion.2
  64.4 5.3 %collective-permute-start.13 = (f32[1,1536]{1,0:T(1,128)S(1)}, f32[1,1536]{1,0:T(1,128)S(1)}, u32[]{:S(2)}, u32[]{:S(2)}) collective-permute-start(f32[1,1536]{1,0:T(1,128)S(1)} %add_add_fusion.2), channel_id=1, source_target_pairs={{0,12},{4,8},{8,4},{12,0},{16,28},{20,24},{24,20},{28,16},{32,44},... | collective-permute-start | bytes 18440 | tf_op jit(solution)/shard_map/ppermute | solution.py:173
  69.7 0.2 collective-permute-start.12
  69.9 0.1 collective-permute-start.11
  69.9 1.1 %collective-permute-done.13 = f32[1,1536]{1,0:T(1,128)S(1)} collective-permute-done((f32[1,1536]{1,0:T(1,128)S(1)}, f32[1,1536]{1,0:T(1,128)S(1)}, u32[]{:S(2)}, u32[]{:S(2)}) %collective-permute-start.13) | collective-permute-done | bytes 6176 | tf_op jit(solution)/shard_map/ppermute | solution.py:173
  71.1 2.3 %collective-permute-done.12 = f32[1,1536]{1,0:T(1,128)S(1)} collective-permute-done((f32[1,1536]{1,0:T(1,128)S(1)}, f32[1,1536]{1,0:T(1,128)S(1)}, u32[]{:S(2)}, u32[]{:S(2)}) %collective-permute-start.12) | collective-permute-done | bytes 6176 | tf_op jit(solution)/shard_map/ppermute | solution.py:173
  73.4 0.0 collective-permute-done.11
  73.4 5.2 %collective-permute-done.14 = bf16[2,128,1536]{2,1,0:T(8,128)(2,1)S(1)} collective-permute-done((bf16[2,128,1536]{2,1,0:T(8,128)(2,1)}, bf16[2,128,1536]{2,1,0:T(8,128)(2,1)S(1)}, u32[]{:S(2)}, u32[]{:S(2)}) %collective-permute-start.14) | collective-permute-done | bytes 786464 | tf_op jit(solution)/shard_map/ppermute | solution.py:163
  78.5 0.9 collective-permute-done.15
  79.4 1.3 %add_convert_fusion.1 = bf16[2,128,1536]{2,1,0:T(8,128)(2,1)S(1)} fusion(bf16[2,128,1536]{2,1,0:T(8,128)(2,1)S(1)} %collective-permute-done.15, bf16[2,128,1536]{2,1,0:T(8,128)(2,1)} %get-tuple-element.24), kind=kLoop, calls=%fused_computation.1 | loop fusion | flops 1572864 | bytes 2359296 | tf_op jit(solution)/shard_map/convert_element_type | solution.py:167
  80.8 3.8 %collective-permute-start.17 = (bf16[2,128,1536]{2,1,0:T(8,128)(2,1)S(1)}, bf16[2,128,1536]{2,1,0:T(8,128)(2,1)S(1)}, u32[]{:S(2)}, u32[]{:S(2)}) collective-permute-start(bf16[2,128,1536]{2,1,0:T(8,128)(2,1)S(1)} %add_convert_fusion.1), channel_id=1, source_target_pairs={{0,1},{1,2},{2,3},{3,4},{4,5},{5,6},{6,7},{7,8},{8,9},{9,10},{10,1... | collective-permute-start | bytes 2359304 | tf_op jit(solution)/shard_map/ppermute | solution.py:163
  84.6 0.0 copy-done.1
  84.6 0.2 add_convert_fusion.2
  84.8 2.4 %collective-permute-start.16 = (bf16[2,128,1536]{2,1,0:T(8,128)(2,1)S(1)}, bf16[2,128,1536]{2,1,0:T(8,128)(2,1)S(1)}, u32[]{:S(2)}, u32[]{:S(2)}) collective-permute-start(bf16[2,128,1536]{2,1,0:T(8,128)(2,1)S(1)} %add_convert_fusion.2), channel_id=1, source_target_pairs={{0,63},{1,0},{2,1},{3,2},{4,3},{5,4},{6,5},{7,6},{8,7},{9,8},{10,9... | collective-permute-start | bytes 2359304 | tf_op jit(solution)/shard_map/ppermute | solution.py:163
  87.2 4.1 %collective-permute-start.20 = (f32[1,1536]{1,0:T(1,128)S(1)}, f32[1,1536]{1,0:T(1,128)S(1)}, u32[]{:S(2)}, u32[]{:S(2)}) collective-permute-start(f32[1,1536]{1,0:T(1,128)S(1)} %add_add_fusion.1), channel_id=1, source_target_pairs={{0,48},{4,52},{8,56},{12,60},{16,32},{20,36},{24,40},{28,44},{32,1... | collective-permute-start | bytes 18440 | tf_op jit(solution)/shard_map/ppermute | solution.py:173
  91.3 1.6 %collective-permute-start.19 = (f32[1,1536]{1,0:T(1,128)S(1)}, f32[1,1536]{1,0:T(1,128)S(1)}, u32[]{:S(2)}, u32[]{:S(2)}) collective-permute-start(f32[1,1536]{1,0:T(1,128)S(1)} %add_add_fusion.1), channel_id=1, source_target_pairs={{0,32},{4,36},{8,40},{12,44},{16,48},{20,52},{24,56},{28,60},{32,0... | collective-permute-start | bytes 18440 | tf_op jit(solution)/shard_map/ppermute | solution.py:173
  92.8 0.9 collective-permute-start.18
  93.7 3.5 %collective-permute-done.20 = f32[1,1536]{1,0:T(1,128)S(1)} collective-permute-done((f32[1,1536]{1,0:T(1,128)S(1)}, f32[1,1536]{1,0:T(1,128)S(1)}, u32[]{:S(2)}, u32[]{:S(2)}) %collective-permute-start.20) | collective-permute-done | bytes 6176 | tf_op jit(solution)/shard_map/ppermute | solution.py:173
  97.2 1.6 %collective-permute-done.19 = f32[1,1536]{1,0:T(1,128)S(1)} collective-permute-done((f32[1,1536]{1,0:T(1,128)S(1)}, f32[1,1536]{1,0:T(1,128)S(1)}, u32[]{:S(2)}, u32[]{:S(2)}) %collective-permute-start.19) | collective-permute-done | bytes 6176 | tf_op jit(solution)/shard_map/ppermute | solution.py:173
  98.8 0.0 collective-permute-done.18
  98.8 2.6 %collective-permute-start.23 = (f32[1,1536]{1,0:T(1,128)S(1)}, f32[1,1536]{1,0:T(1,128)S(1)}, u32[]{:S(2)}, u32[]{:S(2)}) collective-permute-start(f32[1,1536]{1,0:T(1,128)S(1)} %add_add_fusion), channel_id=1, source_target_pairs={{0,3},{1,2},{2,1},{3,0},{4,7},{5,6},{6,5},{7,4},{8,11},{9,10},{10,... | collective-permute-start | bytes 18440 | tf_op jit(solution)/shard_map/ppermute | solution.py:173
  101.4 1.5 %collective-permute-start.22 = (f32[1,1536]{1,0:T(1,128)S(1)}, f32[1,1536]{1,0:T(1,128)S(1)}, u32[]{:S(2)}, u32[]{:S(2)}) collective-permute-start(f32[1,1536]{1,0:T(1,128)S(1)} %add_add_fusion), channel_id=1, source_target_pairs={{0,2},{1,3},{2,0},{3,1},{4,6},{5,7},{6,4},{7,5},{8,10},{9,11},{10,... | collective-permute-start | bytes 18440 | tf_op jit(solution)/shard_map/ppermute | solution.py:173
  102.9 0.1 collective-permute-start.21
  103.0 2.2 %collective-permute-done.23 = f32[1,1536]{1,0:T(1,128)S(1)} collective-permute-done((f32[1,1536]{1,0:T(1,128)S(1)}, f32[1,1536]{1,0:T(1,128)S(1)}, u32[]{:S(2)}, u32[]{:S(2)}) %collective-permute-start.23) | collective-permute-done | bytes 6176 | tf_op jit(solution)/shard_map/ppermute | solution.py:173
  105.2 1.4 %collective-permute-done.22 = f32[1,1536]{1,0:T(1,128)S(1)} collective-permute-done((f32[1,1536]{1,0:T(1,128)S(1)}, f32[1,1536]{1,0:T(1,128)S(1)}, u32[]{:S(2)}, u32[]{:S(2)}) %collective-permute-start.22) | collective-permute-done | bytes 6176 | tf_op jit(solution)/shard_map/ppermute | solution.py:173
  106.6 0.0 collective-permute-done.21
  106.6 0.6 add_reduce_fusion
  107.2 0.0 collective-permute-done.17
  107.2 0.0 collective-permute-done.16
  107.2 0.3 add_convert_fusion
  107.5 0.9 fusion
  (14 shorter events, 0.0 us)
Async XLA Ops:
  0.6 13.5 %collective-permute-start.2 = (bf16[128,1536]{1,0:T(8,128)(2,1)}, bf16[128,1536]{1,0:T(8,128)(2,1)S(1)}, u32[]{:S(2)}, u32[]{:S(2)}) collective-permute-start(bf16[128,1536]{1,0:T(8,128)(2,1)} %bitcast.2), channel_id=1, source_target_pairs={{0,63},{1,0},{2,1},{3,2},{4,3},{5,4},{6,5},{7,6},{8,7},{9,8},{10,9... | collective-permute-start | bytes 1179656 | tf_op jit(solution)/shard_map/ppermute | solution.py:163
  8.5 10.8 %collective-permute-start = (bf16[128,1536]{1,0:T(8,128)(2,1)}, bf16[128,1536]{1,0:T(8,128)(2,1)S(1)}, u32[]{:S(2)}, u32[]{:S(2)}) collective-permute-start(bf16[128,1536]{1,0:T(8,128)(2,1)} %bitcast.3), channel_id=1, source_target_pairs={{0,1},{1,2},{2,3},{3,4},{4,5},{5,6},{6,7},{7,8},{8,9},{9,10},{10,1... | collective-permute-start | bytes 1179656 | tf_op jit(solution)/shard_map/ppermute | solution.py:163
  8.5 11.7 %collective-permute-start.6 = (bf16[128,1536]{1,0:T(8,128)(2,1)}, bf16[128,1536]{1,0:T(8,128)(2,1)S(1)}, u32[]{:S(2)}, u32[]{:S(2)}) collective-permute-start(bf16[128,1536]{1,0:T(8,128)(2,1)} %bitcast.5), channel_id=1, source_target_pairs={{0,63},{1,0},{2,1},{3,2},{4,3},{5,4},{6,5},{7,6},{8,7},{9,8},{10,9... | collective-permute-start | bytes 1179656 | tf_op jit(solution)/shard_map/ppermute | solution.py:163
  13.5 11.9 %collective-permute-start.4 = (bf16[128,1536]{1,0:T(8,128)(2,1)}, bf16[128,1536]{1,0:T(8,128)(2,1)S(1)}, u32[]{:S(2)}, u32[]{:S(2)}) collective-permute-start(bf16[128,1536]{1,0:T(8,128)(2,1)} %bitcast.6), channel_id=1, source_target_pairs={{0,1},{1,2},{2,3},{3,4},{4,5},{5,6},{6,7},{7,8},{8,9},{9,10},{10,1... | collective-permute-start | bytes 1179656 | tf_op jit(solution)/shard_map/ppermute | solution.py:163
  14.1 22.0 %copy-start.2 = (bf16[128,1536]{1,0:T(8,128)(2,1)}, bf16[128,1536]{1,0:T(8,128)(2,1)S(1)}, u32[]{:S(2)}) copy-start(bf16[128,1536]{1,0:T(8,128)(2,1)S(1)} %collective-permute-done.2.refs_3_) | copy-start | bytes 1179652
  14.1 12.7 %collective-permute-start.3 = (bf16[128,1536]{1,0:T(8,128)(2,1)S(1)}, bf16[128,1536]{1,0:T(8,128)(2,1)S(1)}, u32[]{:S(2)}, u32[]{:S(2)}) collective-permute-start(bf16[128,1536]{1,0:T(8,128)(2,1)S(1)} %collective-permute-done.2.refs_3_), channel_id=1, source_target_pairs={{0,63},{1,0},{2,1},{3,2},{4,3},{5,4},{6,5},{7,6},{8,7},{9,8},{10,9... | collective-permute-start | bytes 1179656 | tf_op jit(solution)/shard_map/ppermute | solution.py:163
  19.3 16.8 %copy-start.3 = (bf16[128,1536]{1,0:T(8,128)(2,1)}, bf16[128,1536]{1,0:T(8,128)(2,1)S(1)}, u32[]{:S(2)}) copy-start(bf16[128,1536]{1,0:T(8,128)(2,1)S(1)} %collective-permute-done.refs_1_) | copy-start | bytes 1179652
  19.3 10.6 %collective-permute-start.1 = (bf16[128,1536]{1,0:T(8,128)(2,1)S(1)}, bf16[128,1536]{1,0:T(8,128)(2,1)S(1)}, u32[]{:S(2)}, u32[]{:S(2)}) collective-permute-start(bf16[128,1536]{1,0:T(8,128)(2,1)S(1)} %collective-permute-done.refs_1_), channel_id=1, source_target_pairs={{0,1},{1,2},{2,3},{3,4},{4,5},{5,6},{6,7},{7,8},{8,9},{9,10},{10,1... | collective-permute-start | bytes 1179656 | tf_op jit(solution)/shard_map/ppermute | solution.py:163
  20.2 15.9 %copy-start.4 = (bf16[128,1536]{1,0:T(8,128)(2,1)}, bf16[128,1536]{1,0:T(8,128)(2,1)S(1)}, u32[]{:S(2)}) copy-start(bf16[128,1536]{1,0:T(8,128)(2,1)S(1)} %collective-permute-done.6.refs_8_) | copy-start | bytes 1179652
  20.2 12.9 %collective-permute-start.7 = (bf16[128,1536]{1,0:T(8,128)(2,1)S(1)}, bf16[128,1536]{1,0:T(8,128)(2,1)S(1)}, u32[]{:S(2)}, u32[]{:S(2)}) collective-permute-start(bf16[128,1536]{1,0:T(8,128)(2,1)S(1)} %collective-permute-done.6.refs_8_), channel_id=1, source_target_pairs={{0,63},{1,0},{2,1},{3,2},{4,3},{5,4},{6,5},{7,6},{8,7},{9,8},{10,9... | collective-permute-start | bytes 1179656 | tf_op jit(solution)/shard_map/ppermute | solution.py:163
  25.5 10.6 %copy-start.5 = (bf16[128,1536]{1,0:T(8,128)(2,1)}, bf16[128,1536]{1,0:T(8,128)(2,1)S(1)}, u32[]{:S(2)}) copy-start(bf16[128,1536]{1,0:T(8,128)(2,1)S(1)} %collective-permute-done.4.refs_6_) | copy-start | bytes 1179652
  25.5 10.6 %collective-permute-start.5 = (bf16[128,1536]{1,0:T(8,128)(2,1)S(1)}, bf16[128,1536]{1,0:T(8,128)(2,1)S(1)}, u32[]{:S(2)}, u32[]{:S(2)}) collective-permute-start(bf16[128,1536]{1,0:T(8,128)(2,1)S(1)} %collective-permute-done.4.refs_6_), channel_id=1, source_target_pairs={{0,1},{1,2},{2,3},{3,4},{4,5},{5,6},{6,7},{7,8},{8,9},{9,10},{10,1... | collective-permute-start | bytes 1179656 | tf_op jit(solution)/shard_map/ppermute | solution.py:163
  26.8 9.3 %copy-start.6 = (bf16[128,1536]{1,0:T(8,128)(2,1)}, bf16[128,1536]{1,0:T(8,128)(2,1)S(1)}, u32[]{:S(2)}) copy-start(bf16[128,1536]{1,0:T(8,128)(2,1)S(1)} %collective-permute-done.3.refs_4_) | copy-start | bytes 1179652
  29.9 6.3 %copy-start.7 = (bf16[128,1536]{1,0:T(8,128)(2,1)}, bf16[128,1536]{1,0:T(8,128)(2,1)S(1)}, u32[]{:S(2)}) copy-start(bf16[128,1536]{1,0:T(8,128)(2,1)S(1)} %collective-permute-done.1.refs_0_) | copy-start | bytes 1179652
  33.1 3.0 %copy-start.8 = (bf16[128,1536]{1,0:T(8,128)(2,1)}, bf16[128,1536]{1,0:T(8,128)(2,1)S(1)}, u32[]{:S(2)}) copy-start(bf16[128,1536]{1,0:T(8,128)(2,1)S(1)} %collective-permute-done.7.refs_9_) | copy-start | bytes 1179652
  36.1 0.7 copy-start.9
  55.7 28.8 %copy-start.1 = (bf16[2,128,1536]{2,1,0:T(8,128)(2,1)S(1)}, bf16[2,128,1536]{2,1,0:T(8,128)(2,1)}, u32[]{:S(2)}) copy-start(bf16[2,128,1536]{2,1,0:T(8,128)(2,1)} %get-tuple-element.19) | copy-start | bytes 2359300
  55.7 7.9 %collective-permute-start.10 = (f32[1,1536]{1,0:T(1,128)}, f32[1,1536]{1,0:T(1,128)S(1)}, u32[]{:S(2)}, u32[]{:S(2)}) collective-permute-start(f32[1,1536]{1,0:T(1,128)} %get-tuple-element.20), channel_id=1, source_target_pairs={{0,192},{64,128},{128,64},{192,0},{1,193},{65,129},{129,65},{193,1... | collective-permute-start | bytes 18440 | tf_op jit(solution)/shard_map/ppermute | solution.py:173
  57.3 6.3 %collective-permute-start.9 = (f32[1,1536]{1,0:T(1,128)}, f32[1,1536]{1,0:T(1,128)S(1)}, u32[]{:S(2)}, u32[]{:S(2)}) collective-permute-start(f32[1,1536]{1,0:T(1,128)} %get-tuple-element.20), channel_id=1, source_target_pairs={{0,128},{64,192},{128,0},{192,64},{1,129},{65,193},{129,1},{193,65... | collective-permute-start | bytes 18440 | tf_op jit(solution)/shard_map/ppermute | solution.py:173
  58.4 5.2 %collective-permute-start.8 = (f32[1,1536]{1,0:T(1,128)}, f32[1,1536]{1,0:T(1,128)S(1)}, u32[]{:S(2)}, u32[]{:S(2)}) collective-permute-start(f32[1,1536]{1,0:T(1,128)} %get-tuple-element.20), channel_id=1, source_target_pairs={{0,64},{64,0},{128,192},{192,128},{1,65},{65,1},{129,193},{193,129... | collective-permute-start | bytes 18440 | tf_op jit(solution)/shard_map/ppermute | solution.py:173
  59.9 18.6 %collective-permute-start.14 = (bf16[2,128,1536]{2,1,0:T(8,128)(2,1)}, bf16[2,128,1536]{2,1,0:T(8,128)(2,1)S(1)}, u32[]{:S(2)}, u32[]{:S(2)}) collective-permute-start(bf16[2,128,1536]{2,1,0:T(8,128)(2,1)} %get-tuple-element.21), channel_id=1, source_target_pairs={{0,63},{1,0},{2,1},{3,2},{4,3},{5,4},{6,5},{7,6},{8,7},{9,8},{10,9... | collective-permute-start | bytes 2359304 | tf_op jit(solution)/shard_map/ppermute | solution.py:163
  63.7 15.8 %collective-permute-start.15 = (bf16[2,128,1536]{2,1,0:T(8,128)(2,1)}, bf16[2,128,1536]{2,1,0:T(8,128)(2,1)S(1)}, u32[]{:S(2)}, u32[]{:S(2)}) collective-permute-start(bf16[2,128,1536]{2,1,0:T(8,128)(2,1)} %get-tuple-element.22), channel_id=1, source_target_pairs={{0,1},{1,2},{2,3},{3,4},{4,5},{5,6},{6,7},{7,8},{8,9},{9,10},{10,1... | collective-permute-start | bytes 2359304 | tf_op jit(solution)/shard_map/ppermute | solution.py:163
  64.4 6.7 %collective-permute-start.13 = (f32[1,1536]{1,0:T(1,128)S(1)}, f32[1,1536]{1,0:T(1,128)S(1)}, u32[]{:S(2)}, u32[]{:S(2)}) collective-permute-start(f32[1,1536]{1,0:T(1,128)S(1)} %add_add_fusion.2), channel_id=1, source_target_pairs={{0,12},{4,8},{8,4},{12,0},{16,28},{20,24},{24,20},{28,16},{32,44},... | collective-permute-start | bytes 18440 | tf_op jit(solution)/shard_map/ppermute | solution.py:173
  69.7 3.6 %collective-permute-start.12 = (f32[1,1536]{1,0:T(1,128)S(1)}, f32[1,1536]{1,0:T(1,128)S(1)}, u32[]{:S(2)}, u32[]{:S(2)}) collective-permute-start(f32[1,1536]{1,0:T(1,128)S(1)} %add_add_fusion.2), channel_id=1, source_target_pairs={{0,8},{4,12},{8,0},{12,4},{16,24},{20,28},{24,16},{28,20},{32,40},... | collective-permute-start | bytes 18440 | tf_op jit(solution)/shard_map/ppermute | solution.py:173
  69.9 3.5 %collective-permute-start.11 = (f32[1,1536]{1,0:T(1,128)S(1)}, f32[1,1536]{1,0:T(1,128)S(1)}, u32[]{:S(2)}, u32[]{:S(2)}) collective-permute-start(f32[1,1536]{1,0:T(1,128)S(1)} %add_add_fusion.2), channel_id=1, source_target_pairs={{0,4},{4,0},{8,12},{12,8},{16,20},{20,16},{24,28},{28,24},{32,36},... | collective-permute-start | bytes 18440 | tf_op jit(solution)/shard_map/ppermute | solution.py:173
  80.8 26.4 %copy-start = (f32[2,128,1536]{2,1,0:T(8,128)S(1)}, f32[2,128,1536]{2,1,0:T(8,128)}, u32[]{:S(2)}) copy-start(f32[2,128,1536]{2,1,0:T(8,128)} %get-tuple-element.18) | copy-start | bytes 4718596
  80.8 26.4 %collective-permute-start.17 = (bf16[2,128,1536]{2,1,0:T(8,128)(2,1)S(1)}, bf16[2,128,1536]{2,1,0:T(8,128)(2,1)S(1)}, u32[]{:S(2)}, u32[]{:S(2)}) collective-permute-start(bf16[2,128,1536]{2,1,0:T(8,128)(2,1)S(1)} %add_convert_fusion.1), channel_id=1, source_target_pairs={{0,1},{1,2},{2,3},{3,4},{4,5},{5,6},{6,7},{7,8},{8,9},{9,10},{10,1... | collective-permute-start | bytes 2359304 | tf_op jit(solution)/shard_map/ppermute | solution.py:163
  84.8 22.4 %collective-permute-start.16 = (bf16[2,128,1536]{2,1,0:T(8,128)(2,1)S(1)}, bf16[2,128,1536]{2,1,0:T(8,128)(2,1)S(1)}, u32[]{:S(2)}, u32[]{:S(2)}) collective-permute-start(bf16[2,128,1536]{2,1,0:T(8,128)(2,1)S(1)} %add_convert_fusion.2), channel_id=1, source_target_pairs={{0,63},{1,0},{2,1},{3,2},{4,3},{5,4},{6,5},{7,6},{8,7},{9,8},{10,9... | collective-permute-start | bytes 2359304 | tf_op jit(solution)/shard_map/ppermute | solution.py:163
  87.2 10.0 %collective-permute-start.20 = (f32[1,1536]{1,0:T(1,128)S(1)}, f32[1,1536]{1,0:T(1,128)S(1)}, u32[]{:S(2)}, u32[]{:S(2)}) collective-permute-start(f32[1,1536]{1,0:T(1,128)S(1)} %add_add_fusion.1), channel_id=1, source_target_pairs={{0,48},{4,52},{8,56},{12,60},{16,32},{20,36},{24,40},{28,44},{32,1... | collective-permute-start | bytes 18440 | tf_op jit(solution)/shard_map/ppermute | solution.py:173
  91.3 7.5 %collective-permute-start.19 = (f32[1,1536]{1,0:T(1,128)S(1)}, f32[1,1536]{1,0:T(1,128)S(1)}, u32[]{:S(2)}, u32[]{:S(2)}) collective-permute-start(f32[1,1536]{1,0:T(1,128)S(1)} %add_add_fusion.1), channel_id=1, source_target_pairs={{0,32},{4,36},{8,40},{12,44},{16,48},{20,52},{24,56},{28,60},{32,0... | collective-permute-start | bytes 18440 | tf_op jit(solution)/shard_map/ppermute | solution.py:173
  92.8 6.0 %collective-permute-start.18 = (f32[1,1536]{1,0:T(1,128)S(1)}, f32[1,1536]{1,0:T(1,128)S(1)}, u32[]{:S(2)}, u32[]{:S(2)}) collective-permute-start(f32[1,1536]{1,0:T(1,128)S(1)} %add_add_fusion.1), channel_id=1, source_target_pairs={{0,16},{4,20},{8,24},{12,28},{16,0},{20,4},{24,8},{28,12},{32,48},... | collective-permute-start | bytes 18440 | tf_op jit(solution)/shard_map/ppermute | solution.py:173
  98.8 6.3 %collective-permute-start.23 = (f32[1,1536]{1,0:T(1,128)S(1)}, f32[1,1536]{1,0:T(1,128)S(1)}, u32[]{:S(2)}, u32[]{:S(2)}) collective-permute-start(f32[1,1536]{1,0:T(1,128)S(1)} %add_add_fusion), channel_id=1, source_target_pairs={{0,3},{1,2},{2,1},{3,0},{4,7},{5,6},{6,5},{7,4},{8,11},{9,10},{10,... | collective-permute-start | bytes 18440 | tf_op jit(solution)/shard_map/ppermute | solution.py:173
  101.4 5.1 %collective-permute-start.22 = (f32[1,1536]{1,0:T(1,128)S(1)}, f32[1,1536]{1,0:T(1,128)S(1)}, u32[]{:S(2)}, u32[]{:S(2)}) collective-permute-start(f32[1,1536]{1,0:T(1,128)S(1)} %add_add_fusion), channel_id=1, source_target_pairs={{0,2},{1,3},{2,0},{3,1},{4,6},{5,7},{6,4},{7,5},{8,10},{9,11},{10,... | collective-permute-start | bytes 18440 | tf_op jit(solution)/shard_map/ppermute | solution.py:173
  102.9 3.7 %collective-permute-start.21 = (f32[1,1536]{1,0:T(1,128)S(1)}, f32[1,1536]{1,0:T(1,128)S(1)}, u32[]{:S(2)}, u32[]{:S(2)}) collective-permute-start(f32[1,1536]{1,0:T(1,128)S(1)} %add_add_fusion), channel_id=1, source_target_pairs={{0,1},{1,0},{2,3},{3,2},{4,5},{5,4},{6,7},{7,6},{8,9},{9,8},{10,11... | collective-permute-start | bytes 18440 | tf_op jit(solution)/shard_map/ppermute | solution.py:173

commit v2 on v1

--- a/solution.py
+++ b/solution.py
@@ -13,7 +13,8 @@
 REACH = 2
 MAXP = 4
 WINDOW = 2 * REACH + 1
-GROUP = 2
+GROUP = 4
+LAG = 2
 LANES = 256
 ROWS = 64
 SCALE = HEAD_DIM**-0.5
@@ -64,18 +65,18 @@
 
     fold = SCALE * LOG2E
     vrows = q_ref.shape[1]
-    for head in range(GROUP):
+    def work(head):
         cols = slice(head * HEAD_DIM, (head + 1) * HEAD_DIM)
-
         keys = jnp.concatenate([r[:, cols] for r in k_refs], axis=0)
         values = jnp.concatenate([r[:, cols] for r in v_refs], axis=0)
         gate = gate_ref[:, cols]
         dattend_t = (up_ref[0, :, cols].astype(F32) * gate).astype(BF16).T
+        chunks = [slice(at, at + LANES) for at in range(0, vrows, LANES)]
         scaled = []
         inverses = []
-        for at in range(0, vrows, LANES):
-            lanes = slice(at, at + LANES)
+        for lanes in chunks:
             scores = nt(keys, q_ref[0, lanes, cols])
+            yield
             bias = [bias_ref[slot : slot + 1, lanes] for slot in range(WINDOW)]
             top = None
             for slot in range(WINDOW):
@@ -93,20 +94,16 @@
             inverse = 1.0 / jnp.sum(total, axis=0, keepdims=True)
             inverses.append(inverse)
             scaled.append((dattend_t[:, lanes].astype(F32) * inverse).astype(BF16))
-        scaled = jnp.concatenate(scaled, axis=1)
+            yield
         attend_t = tn(values, expo_ref[head]) * jnp.concatenate(inverses, axis=1)
-        attend = attend_t.T
-        out_ref[0, :, cols] = (attend * gate).astype(BF16)
-        gpart_ref[:, cols] = jnp.sum(
-            attend * up_ref[0, :, cols].astype(F32), axis=0, keepdims=True
-        )
-        hand_out(nt(expo_ref[head], scaled), 1, cols)
+        yield
+        hand_out(nt(expo_ref[head], jnp.concatenate(scaled, axis=1)), 1, cols)
+        yield
         dscore = []
-        for at in range(0, vrows, LANES):
-            lanes = slice(at, at + LANES)
-            dat = scaled[:, lanes]
+        for lanes, dat in zip(chunks, scaled):
             delta = jnp.sum(attend_t[:, lanes] * dat.astype(F32), axis=0, keepdims=True)
             dprob = nn(values, dat)
+            yield
             dscore.append(
                 jnp.concatenate(
                     [
@@ -119,9 +116,25 @@
                     axis=0,
                 )
             )
+            yield
         dscore = jnp.concatenate(dscore, axis=1)
+        attend = attend_t.T
+        out_ref[0, :, cols] = (attend * gate).astype(BF16)
+        gpart_ref[:, cols] = jnp.sum(
+            attend * up_ref[0, :, cols].astype(F32), axis=0, keepdims=True
+        )
+        yield
         qgrad_ref[0, :, cols] = (tn(keys, dscore) * SCALE).astype(BF16).T
+        yield
         hand_out(nn(dscore, q_ref[0, :, cols]) * SCALE, 0, cols)
+
+    heads = [work(head) for head in range(GROUP)]
+    turn = 0
+    while any(h is not None for h in heads):
+        for i, h in enumerate(heads):
+            if h is not None and turn >= i * LAG and next(h, 0) == 0:
+                heads[i] = None
+        turn += 1
 
 
 def attend_pairs(pairs, counts, queries, upstream, gate, keys, values):
@@ -188,10 +201,10 @@
     )
     m2, p2 = moved(m2, -1), moved(p2, 1)
     gate_part = summed(gate_part, "clip", (1, 2, 3))
-    gate_part = summed(gate_part, "vid", (1, 2, 3))
+    gate_part = summed(gate_part, "vid", (4, 8, 12))
     gate_part, m2, p2 = lax.optimization_barrier((gate_part, m2, p2))
     m1, p1 = moved(joined(m1, m2), -1), moved(joined(p1, p2), 1)
-    gate_part = summed(gate_part, "vid", (4, 8, 12))
+    gate_part = summed(gate_part, "vid", (1, 2, 3))
     gate_part = summed(gate_part, "aud", (1, 2, 3))
     grads = (own + m1.astype(F32) + p1.astype(F32)).astype(BF16)
     return (out, qgrad, grads[:1], grads[1:], gate_part.reshape(width))

time: 110 us -> 107 us (0.973)
  waiting for transfers between devices: 28.6 us -> 25.1 us
  starting transfers between devices: 54 us -> 56.4 us
  Pallas kernels: 18.9 us -> 16.8 us
    ppermute x12, waiting for transfers between devices: 16.6 us -> 12.1 us  [moved(): lax.ppermute(shard, TIME, [(i, (i + by) % count) for i in range(count)])]
    ppermute x12, starting transfers between devices: 20.5 us -> 22.9 us  [summed(): lax.ppermute(part, axis, [(i, i ^ mask) for i in range(count)])]
    pallas_call x1, Pallas kernels: 18.9 us -> 16.8 us  [attend_pairs(): pl.pallas_call(pair_kernel, grid=(HEADS // GROUP,), in_specs=[smem, smem,...]
  transfers between devices with their start and end apart: 24 -> 24, of which waited for: 13 -> 11; matrix products, arithmetic and copies ran while one was open for 3% -> 3% of each run, Pallas kernels for 0% -> 0%
where the time goes in v2:
time: 107 us; the launch traced here: 105 us
  starting transfers between devices  56.4 us (53%)
  waiting for transfers between devices  25.1 us (23%)
  Pallas kernels  16.8 us (16%)
  other arithmetic  3.18 us (3%)
  local copies, waits for them, and re-layouts  3.01 us (3%)
    ppermute x12, starting transfers between devices, moved(): lax.ppermute(shard, TIME, [(i, (i + by) % count) for i in range(count)])  33.5 us
    ppermute x12, starting transfers between devices, summed(): lax.ppermute(part, axis, [(i, i ^ mask) for i in range(count)])  22.9 us
    pallas_call x1, Pallas kernels, attend_pairs(): pl.pallas_call(pair_kernel, grid=(HEADS // GROUP,), in_specs=[smem, smem,...  16.8 us
    ppermute x12, waiting for transfers between devices, summed(): lax.ppermute(part, axis, [(i, i ^ mask) for i in range(count)])  13 us
    ppermute x12, waiting for transfers between devices, moved(): lax.ppermute(shard, TIME, [(i, (i + by) % count) for i in range(count)])  12.1 us
  transfers between devices with their start and end apart: 24, of which 11 were waited for; matrix products, arithmetic and copies ran while one was open for 3% of the time, Pallas kernels for 0%

profile of v2, /device:TPU:2, one launch (start us, length us, event | category | flops | bytes accessed | tf_op | source)
XLA Modules:
  0.0 105.2 jit_solution(11366032560835902099)
XLA Ops:
  0.6 7.8 %collective-permute-start.2 = (bf16[128,1536]{1,0:T(8,128)(2,1)}, bf16[128,1536]{1,0:T(8,128)(2,1)S(1)}, u32[]{:S(2)}, u32[]{:S(2)}) collective-permute-start(bf16[128,1536]{1,0:T(8,128)(2,1)} %bitcast.2), channel_id=1, source_target_pairs={{0,63},{1,0},{2,1},{3,2},{4,3},{5,4},{6,5},{7,6},{8,7},{9,8},{10,9... | collective-permute-start | bytes 1179656 | tf_op jit(solution)/shard_map/ppermute | solution.py:176
  8.5 0.0 collective-permute-start
  8.5 5.1 %collective-permute-start.6 = (bf16[128,1536]{1,0:T(8,128)(2,1)}, bf16[128,1536]{1,0:T(8,128)(2,1)S(1)}, u32[]{:S(2)}, u32[]{:S(2)}) collective-permute-start(bf16[128,1536]{1,0:T(8,128)(2,1)} %bitcast.5), channel_id=1, source_target_pairs={{0,63},{1,0},{2,1},{3,2},{4,3},{5,4},{6,5},{7,6},{8,7},{9,8},{10,9... | collective-permute-start | bytes 1179656 | tf_op jit(solution)/shard_map/ppermute | solution.py:176
  13.5 0.0 collective-permute-start.4
  13.5 0.6 collective-permute-done.2.refs_3_
  14.1 5.2 %collective-permute-start.3 = (bf16[128,1536]{1,0:T(8,128)(2,1)S(1)}, bf16[128,1536]{1,0:T(8,128)(2,1)S(1)}, u32[]{:S(2)}, u32[]{:S(2)}) collective-permute-start(bf16[128,1536]{1,0:T(8,128)(2,1)S(1)} %collective-permute-done.2.refs_3_), channel_id=1, source_target_pairs={{0,63},{1,0},{2,1},{3,2},{4,3},{5,4},{6,5},{7,6},{8,7},{9,8},{10,9... | collective-permute-start | bytes 1179656 | tf_op jit(solution)/shard_map/ppermute | solution.py:176
  19.3 0.0 collective-permute-done.refs_1_
  19.3 0.3 collective-permute-start.1
  19.6 0.6 collective-permute-done.6.refs_8_
  20.2 5.2 %collective-permute-start.7 = (bf16[128,1536]{1,0:T(8,128)(2,1)S(1)}, bf16[128,1536]{1,0:T(8,128)(2,1)S(1)}, u32[]{:S(2)}, u32[]{:S(2)}) collective-permute-start(bf16[128,1536]{1,0:T(8,128)(2,1)S(1)} %collective-permute-done.6.refs_8_), channel_id=1, source_target_pairs={{0,63},{1,0},{2,1},{3,2},{4,3},{5,4},{6,5},{7,6},{8,7},{9,8},{10,9... | collective-permute-start | bytes 1179656 | tf_op jit(solution)/shard_map/ppermute | solution.py:176
  25.5 0.0 collective-permute-done.4.refs_6_
  25.5 0.0 collective-permute-start.5
  25.5 1.3 %reshape.16.gate_ref = f32[1,1536]{1,0:T(1,128)} reshape(f32[1536]{0:T(1024)} %param.10) | data formatting | bytes 12288 | tf_op jit(solution)/shard_map/reshape | solution.py:199
  26.8 0.0 collective-permute-done.3.refs_4_
  26.8 3.1 %collective-permute-done.1.refs_0_ = bf16[128,1536]{1,0:T(8,128)(2,1)S(1)} collective-permute-done((bf16[128,1536]{1,0:T(8,128)(2,1)S(1)}, bf16[128,1536]{1,0:T(8,128)(2,1)S(1)}, u32[]{:S(2)}, u32[]{:S(2)}) %collective-permute-start.1) | collective-permute-done | bytes 393248 | tf_op jit(solution)/shard_map/ppermute | solution.py:176
  29.9 3.2 %collective-permute-done.7.refs_9_ = bf16[128,1536]{1,0:T(8,128)(2,1)S(1)} collective-permute-done((bf16[128,1536]{1,0:T(8,128)(2,1)S(1)}, bf16[128,1536]{1,0:T(8,128)(2,1)S(1)}, u32[]{:S(2)}, u32[]{:S(2)}) %collective-permute-start.7) | collective-permute-done | bytes 393248 | tf_op jit(solution)/shard_map/ppermute | solution.py:176
  33.1 3.0 %collective-permute-done.5.refs_5_ = bf16[128,1536]{1,0:T(8,128)(2,1)S(1)} collective-permute-done((bf16[128,1536]{1,0:T(8,128)(2,1)S(1)}, bf16[128,1536]{1,0:T(8,128)(2,1)S(1)}, u32[]{:S(2)}, u32[]{:S(2)}) %collective-permute-start.5) | collective-permute-done | bytes 393248 | tf_op jit(solution)/shard_map/ppermute | solution.py:176
  36.1 0.0 copy-done.2
  36.1 0.0 copy-done.3
  36.1 0.0 copy-done.4
  36.1 0.0 copy-done.5
  36.1 0.0 copy-done.6
  36.1 0.0 copy-done.7
  36.1 0.0 copy-done.8
  36.1 0.7 copy-done.9
  36.9 16.8 %pairs.2 = (bf16[1,512,1536]{2,1,0:T(8,128)(2,1)}, bf16[1,512,1536]{2,1,0:T(8,128)(2,1)}, f32[1,1536]{1,0:T(1,128)}, bf16[2,128,1536]{2,1,0:T(8,128)(2,1)}, bf16...) custom-call(s32[1,4,4]{2,1,0:T(4,128)} %pairs.3, ...), custom_call_target="tpu_custom_call" | custom-call | flops 6000000000 | bytes 16000000 | tf_op jit(solution)/shard_map/pairs/pallas_call | solution.py:149
  53.7 1.8 %collective-permute-start.10 = (f32[1,1536]{1,0:T(1,128)}, f32[1,1536]{1,0:T(1,128)S(1)}, u32[]{:S(2)}, u32[]{:S(2)}) collective-permute-start(f32[1,1536]{1,0:T(1,128)} %get-tuple-element.20), channel_id=1, source_target_pairs={{0,192},{64,128},{128,64},{192,0},{1,193},{65,129},{129,65},{193,1... | collective-permute-start | bytes 18440 | tf_op jit(solution)/shard_map/ppermute | solution.py:186
  55.4 1.1 %collective-permute-start.9 = (f32[1,1536]{1,0:T(1,128)}, f32[1,1536]{1,0:T(1,128)S(1)}, u32[]{:S(2)}, u32[]{:S(2)}) collective-permute-start(f32[1,1536]{1,0:T(1,128)} %get-tuple-element.20), channel_id=1, source_target_pairs={{0,128},{64,192},{128,0},{192,64},{1,129},{65,193},{129,1},{193,65... | collective-permute-start | bytes 18440 | tf_op jit(solution)/shard_map/ppermute | solution.py:186
  56.5 1.5 %collective-permute-start.8 = (f32[1,1536]{1,0:T(1,128)}, f32[1,1536]{1,0:T(1,128)S(1)}, u32[]{:S(2)}, u32[]{:S(2)}) collective-permute-start(f32[1,1536]{1,0:T(1,128)} %get-tuple-element.20), channel_id=1, source_target_pairs={{0,64},{64,0},{128,192},{192,128},{1,65},{65,1},{129,193},{193,129... | collective-permute-start | bytes 18440 | tf_op jit(solution)/shard_map/ppermute | solution.py:186
  58.0 3.7 %collective-permute-start.14 = (bf16[2,128,1536]{2,1,0:T(8,128)(2,1)}, bf16[2,128,1536]{2,1,0:T(8,128)(2,1)S(1)}, u32[]{:S(2)}, u32[]{:S(2)}) collective-permute-start(bf16[2,128,1536]{2,1,0:T(8,128)(2,1)} %get-tuple-element.21), channel_id=1, source_target_pairs={{0,63},{1,0},{2,1},{3,2},{4,3},{5,4},{6,5},{7,6},{8,7},{9,8},{10,9... | collective-permute-start | bytes 2359304 | tf_op jit(solution)/shard_map/ppermute | solution.py:176
  61.8 0.0 collective-permute-start.15
  61.8 0.0 collective-permute-done.10
  61.8 0.0 collective-permute-done.9
  61.8 0.0 collective-permute-done.8
  61.8 0.7 add_add_fusion.2
  62.5 5.9 %collective-permute-start.13 = (f32[1,1536]{1,0:T(1,128)S(1)}, f32[1,1536]{1,0:T(1,128)S(1)}, u32[]{:S(2)}, u32[]{:S(2)}) collective-permute-start(f32[1,1536]{1,0:T(1,128)S(1)} %add_add_fusion.2), channel_id=1, source_target_pairs={{0,48},{4,52},{8,56},{12,60},{16,32},{20,36},{24,40},{28,44},{32,1... | collective-permute-start | bytes 18440 | tf_op jit(solution)/shard_map/ppermute | solution.py:186
  68.4 1.0 collective-permute-start.12
  69.4 1.5 %collective-permute-start.11 = (f32[1,1536]{1,0:T(1,128)S(1)}, f32[1,1536]{1,0:T(1,128)S(1)}, u32[]{:S(2)}, u32[]{:S(2)}) collective-permute-start(f32[1,1536]{1,0:T(1,128)S(1)} %add_add_fusion.2), channel_id=1, source_target_pairs={{0,16},{4,20},{8,24},{12,28},{16,0},{20,4},{24,8},{28,12},{32,48},... | collective-permute-start | bytes 18440 | tf_op jit(solution)/shard_map/ppermute | solution.py:186
  70.9 0.8 collective-permute-done.13
  71.7 4.2 %collective-permute-done.12 = f32[1,1536]{1,0:T(1,128)S(1)} collective-permute-done((f32[1,1536]{1,0:T(1,128)S(1)}, f32[1,1536]{1,0:T(1,128)S(1)}, u32[]{:S(2)}, u32[]{:S(2)}) %collective-permute-start.12) | collective-permute-done | bytes 6176 | tf_op jit(solution)/shard_map/ppermute | solution.py:186
  75.9 0.0 collective-permute-done.11
  76.0 0.7 collective-permute-done.14
  76.6 0.9 collective-permute-done.15
  77.6 1.3 %add_convert_fusion.1 = bf16[2,128,1536]{2,1,0:T(8,128)(2,1)S(1)} fusion(bf16[2,128,1536]{2,1,0:T(8,128)(2,1)S(1)} %collective-permute-done.15, bf16[2,128,1536]{2,1,0:T(8,128)(2,1)} %get-tuple-element.24), kind=kLoop, calls=%fused_computation.1 | loop fusion | flops 1572864 | bytes 2359296 | tf_op jit(solution)/shard_map/convert_element_type | solution.py:180
  78.9 3.8 %collective-permute-start.17 = (bf16[2,128,1536]{2,1,0:T(8,128)(2,1)S(1)}, bf16[2,128,1536]{2,1,0:T(8,128)(2,1)S(1)}, u32[]{:S(2)}, u32[]{:S(2)}) collective-permute-start(bf16[2,128,1536]{2,1,0:T(8,128)(2,1)S(1)} %add_convert_fusion.1), channel_id=1, source_target_pairs={{0,1},{1,2},{2,3},{3,4},{4,5},{5,6},{6,7},{7,8},{8,9},{9,10},{10,1... | collective-permute-start | bytes 2359304 | tf_op jit(solution)/shard_map/ppermute | solution.py:176
  82.7 0.2 add_convert_fusion.2
  82.9 2.4 %collective-permute-start.16 = (bf16[2,128,1536]{2,1,0:T(8,128)(2,1)S(1)}, bf16[2,128,1536]{2,1,0:T(8,128)(2,1)S(1)}, u32[]{:S(2)}, u32[]{:S(2)}) collective-permute-start(bf16[2,128,1536]{2,1,0:T(8,128)(2,1)S(1)} %add_convert_fusion.2), channel_id=1, source_target_pairs={{0,63},{1,0},{2,1},{3,2},{4,3},{5,4},{6,5},{7,6},{8,7},{9,8},{10,9... | collective-permute-start | bytes 2359304 | tf_op jit(solution)/shard_map/ppermute | solution.py:176
  85.3 0.6 collective-permute-start.20
  85.9 5.4 %collective-permute-start.19 = (f32[1,1536]{1,0:T(1,128)S(1)}, f32[1,1536]{1,0:T(1,128)S(1)}, u32[]{:S(2)}, u32[]{:S(2)}) collective-permute-start(f32[1,1536]{1,0:T(1,128)S(1)} %add_add_fusion.1), channel_id=1, source_target_pairs={{0,8},{4,12},{8,0},{12,4},{16,24},{20,28},{24,16},{28,20},{32,40},... | collective-permute-start | bytes 18440 | tf_op jit(solution)/shard_map/ppermute | solution.py:186
  91.2 0.0 collective-permute-start.18
  91.3 0.0 collective-permute-done.20
  91.3 3.8 %collective-permute-done.19 = f32[1,1536]{1,0:T(1,128)S(1)} collective-permute-done((f32[1,1536]{1,0:T(1,128)S(1)}, f32[1,1536]{1,0:T(1,128)S(1)}, u32[]{:S(2)}, u32[]{:S(2)}) %collective-permute-start.19) | collective-permute-done | bytes 6176 | tf_op jit(solution)/shard_map/ppermute | solution.py:186
  95.1 0.0 collective-permute-done.18
  95.1 0.1 collective-permute-start.23
  95.2 0.1 collective-permute-start.22
  95.3 4.0 %collective-permute-start.21 = (f32[1,1536]{1,0:T(1,128)S(1)}, f32[1,1536]{1,0:T(1,128)S(1)}, u32[]{:S(2)}, u32[]{:S(2)}) collective-permute-start(f32[1,1536]{1,0:T(1,128)S(1)} %add_add_fusion), channel_id=1, source_target_pairs={{0,1},{1,0},{2,3},{3,2},{4,5},{5,4},{6,7},{7,6},{8,9},{9,8},{10,11... | collective-permute-start | bytes 18440 | tf_op jit(solution)/shard_map/ppermute | solution.py:186
  99.3 4.1 %collective-permute-done.23 = f32[1,1536]{1,0:T(1,128)S(1)} collective-permute-done((f32[1,1536]{1,0:T(1,128)S(1)}, f32[1,1536]{1,0:T(1,128)S(1)}, u32[]{:S(2)}, u32[]{:S(2)}) %collective-permute-start.23) | collective-permute-done | bytes 6176 | tf_op jit(solution)/shard_map/ppermute | solution.py:186
  103.3 0.0 collective-permute-done.22
  103.3 0.0 collective-permute-done.21
  103.3 0.6 add_reduce_fusion
  104.0 0.0 collective-permute-done.17
  104.0 0.0 collective-permute-done.16
  104.0 0.3 add_convert_fusion
  104.3 0.9 fusion
  (14 shorter events, 0.0 us)
Async XLA Ops:
  0.6 13.5 %collective-permute-start.2 = (bf16[128,1536]{1,0:T(8,128)(2,1)}, bf16[128,1536]{1,0:T(8,128)(2,1)S(1)}, u32[]{:S(2)}, u32[]{:S(2)}) collective-permute-start(bf16[128,1536]{1,0:T(8,128)(2,1)} %bitcast.2), channel_id=1, source_target_pairs={{0,63},{1,0},{2,1},{3,2},{4,3},{5,4},{6,5},{7,6},{8,7},{9,8},{10,9... | collective-permute-start | bytes 1179656 | tf_op jit(solution)/shard_map/ppermute | solution.py:176
  8.5 10.8 %collective-permute-start = (bf16[128,1536]{1,0:T(8,128)(2,1)}, bf16[128,1536]{1,0:T(8,128)(2,1)S(1)}, u32[]{:S(2)}, u32[]{:S(2)}) collective-permute-start(bf16[128,1536]{1,0:T(8,128)(2,1)} %bitcast.3), channel_id=1, source_target_pairs={{0,1},{1,2},{2,3},{3,4},{4,5},{5,6},{6,7},{7,8},{8,9},{9,10},{10,1... | collective-permute-start | bytes 1179656 | tf_op jit(solution)/shard_map/ppermute | solution.py:176
  8.5 11.7 %collective-permute-start.6 = (bf16[128,1536]{1,0:T(8,128)(2,1)}, bf16[128,1536]{1,0:T(8,128)(2,1)S(1)}, u32[]{:S(2)}, u32[]{:S(2)}) collective-permute-start(bf16[128,1536]{1,0:T(8,128)(2,1)} %bitcast.5), channel_id=1, source_target_pairs={{0,63},{1,0},{2,1},{3,2},{4,3},{5,4},{6,5},{7,6},{8,7},{9,8},{10,9... | collective-permute-start | bytes 1179656 | tf_op jit(solution)/shard_map/ppermute | solution.py:176
  13.5 11.9 %collective-permute-start.4 = (bf16[128,1536]{1,0:T(8,128)(2,1)}, bf16[128,1536]{1,0:T(8,128)(2,1)S(1)}, u32[]{:S(2)}, u32[]{:S(2)}) collective-permute-start(bf16[128,1536]{1,0:T(8,128)(2,1)} %bitcast.6), channel_id=1, source_target_pairs={{0,1},{1,2},{2,3},{3,4},{4,5},{5,6},{6,7},{7,8},{8,9},{9,10},{10,1... | collective-permute-start | bytes 1179656 | tf_op jit(solution)/shard_map/ppermute | solution.py:176
  14.1 22.0 %copy-start.2 = (bf16[128,1536]{1,0:T(8,128)(2,1)}, bf16[128,1536]{1,0:T(8,128)(2,1)S(1)}, u32[]{:S(2)}) copy-start(bf16[128,1536]{1,0:T(8,128)(2,1)S(1)} %collective-permute-done.2.refs_3_) | copy-start | bytes 1179652
  14.1 12.7 %collective-permute-start.3 = (bf16[128,1536]{1,0:T(8,128)(2,1)S(1)}, bf16[128,1536]{1,0:T(8,128)(2,1)S(1)}, u32[]{:S(2)}, u32[]{:S(2)}) collective-permute-start(bf16[128,1536]{1,0:T(8,128)(2,1)S(1)} %collective-permute-done.2.refs_3_), channel_id=1, source_target_pairs={{0,63},{1,0},{2,1},{3,2},{4,3},{5,4},{6,5},{7,6},{8,7},{9,8},{10,9... | collective-permute-start | bytes 1179656 | tf_op jit(solution)/shard_map/ppermute | solution.py:176
  19.3 16.8 %copy-start.3 = (bf16[128,1536]{1,0:T(8,128)(2,1)}, bf16[128,1536]{1,0:T(8,128)(2,1)S(1)}, u32[]{:S(2)}) copy-start(bf16[128,1536]{1,0:T(8,128)(2,1)S(1)} %collective-permute-done.refs_1_) | copy-start | bytes 1179652
  19.3 10.6 %collective-permute-start.1 = (bf16[128,1536]{1,0:T(8,128)(2,1)S(1)}, bf16[128,1536]{1,0:T(8,128)(2,1)S(1)}, u32[]{:S(2)}, u32[]{:S(2)}) collective-permute-start(bf16[128,1536]{1,0:T(8,128)(2,1)S(1)} %collective-permute-done.refs_1_), channel_id=1, source_target_pairs={{0,1},{1,2},{2,3},{3,4},{4,5},{5,6},{6,7},{7,8},{8,9},{9,10},{10,1... | collective-permute-start | bytes 1179656 | tf_op jit(solution)/shard_map/ppermute | solution.py:176
  20.2 15.9 %copy-start.4 = (bf16[128,1536]{1,0:T(8,128)(2,1)}, bf16[128,1536]{1,0:T(8,128)(2,1)S(1)}, u32[]{:S(2)}) copy-start(bf16[128,1536]{1,0:T(8,128)(2,1)S(1)} %collective-permute-done.6.refs_8_) | copy-start | bytes 1179652
  20.2 12.9 %collective-permute-start.7 = (bf16[128,1536]{1,0:T(8,128)(2,1)S(1)}, bf16[128,1536]{1,0:T(8,128)(2,1)S(1)}, u32[]{:S(2)}, u32[]{:S(2)}) collective-permute-start(bf16[128,1536]{1,0:T(8,128)(2,1)S(1)} %collective-permute-done.6.refs_8_), channel_id=1, source_target_pairs={{0,63},{1,0},{2,1},{3,2},{4,3},{5,4},{6,5},{7,6},{8,7},{9,8},{10,9... | collective-permute-start | bytes 1179656 | tf_op jit(solution)/shard_map/ppermute | solution.py:176
  25.5 10.6 %copy-start.5 = (bf16[128,1536]{1,0:T(8,128)(2,1)}, bf16[128,1536]{1,0:T(8,128)(2,1)S(1)}, u32[]{:S(2)}) copy-start(bf16[128,1536]{1,0:T(8,128)(2,1)S(1)} %collective-permute-done.4.refs_6_) | copy-start | bytes 1179652
  25.5 10.6 %collective-permute-start.5 = (bf16[128,1536]{1,0:T(8,128)(2,1)S(1)}, bf16[128,1536]{1,0:T(8,128)(2,1)S(1)}, u32[]{:S(2)}, u32[]{:S(2)}) collective-permute-start(bf16[128,1536]{1,0:T(8,128)(2,1)S(1)} %collective-permute-done.4.refs_6_), channel_id=1, source_target_pairs={{0,1},{1,2},{2,3},{3,4},{4,5},{5,6},{6,7},{7,8},{8,9},{9,10},{10,1... | collective-permute-start | bytes 1179656 | tf_op jit(solution)/shard_map/ppermute | solution.py:176
  26.8 9.3 %copy-start.6 = (bf16[128,1536]{1,0:T(8,128)(2,1)}, bf16[128,1536]{1,0:T(8,128)(2,1)S(1)}, u32[]{:S(2)}) copy-start(bf16[128,1536]{1,0:T(8,128)(2,1)S(1)} %collective-permute-done.3.refs_4_) | copy-start | bytes 1179652
  29.9 6.3 %copy-start.7 = (bf16[128,1536]{1,0:T(8,128)(2,1)}, bf16[128,1536]{1,0:T(8,128)(2,1)S(1)}, u32[]{:S(2)}) copy-start(bf16[128,1536]{1,0:T(8,128)(2,1)S(1)} %collective-permute-done.1.refs_0_) | copy-start | bytes 1179652
  33.1 3.0 %copy-start.8 = (bf16[128,1536]{1,0:T(8,128)(2,1)}, bf16[128,1536]{1,0:T(8,128)(2,1)S(1)}, u32[]{:S(2)}) copy-start(bf16[128,1536]{1,0:T(8,128)(2,1)S(1)} %collective-permute-done.7.refs_9_) | copy-start | bytes 1179652
  36.1 0.7 copy-start.9
  53.7 29.0 %copy-start.1 = (bf16[2,128,1536]{2,1,0:T(8,128)(2,1)S(1)}, bf16[2,128,1536]{2,1,0:T(8,128)(2,1)}, u32[]{:S(2)}) copy-start(bf16[2,128,1536]{2,1,0:T(8,128)(2,1)} %get-tuple-element.19) | copy-start | bytes 2359300
  53.7 8.1 %collective-permute-start.10 = (f32[1,1536]{1,0:T(1,128)}, f32[1,1536]{1,0:T(1,128)S(1)}, u32[]{:S(2)}, u32[]{:S(2)}) collective-permute-start(f32[1,1536]{1,0:T(1,128)} %get-tuple-element.20), channel_id=1, source_target_pairs={{0,192},{64,128},{128,64},{192,0},{1,193},{65,129},{129,65},{193,1... | collective-permute-start | bytes 18440 | tf_op jit(solution)/shard_map/ppermute | solution.py:186
  55.4 6.3 %collective-permute-start.9 = (f32[1,1536]{1,0:T(1,128)}, f32[1,1536]{1,0:T(1,128)S(1)}, u32[]{:S(2)}, u32[]{:S(2)}) collective-permute-start(f32[1,1536]{1,0:T(1,128)} %get-tuple-element.20), channel_id=1, source_target_pairs={{0,128},{64,192},{128,0},{192,64},{1,129},{65,193},{129,1},{193,65... | collective-permute-start | bytes 18440 | tf_op jit(solution)/shard_map/ppermute | solution.py:186
  56.5 5.2 %collective-permute-start.8 = (f32[1,1536]{1,0:T(1,128)}, f32[1,1536]{1,0:T(1,128)S(1)}, u32[]{:S(2)}, u32[]{:S(2)}) collective-permute-start(f32[1,1536]{1,0:T(1,128)} %get-tuple-element.20), channel_id=1, source_target_pairs={{0,64},{64,0},{128,192},{192,128},{1,65},{65,1},{129,193},{193,129... | collective-permute-start | bytes 18440 | tf_op jit(solution)/shard_map/ppermute | solution.py:186
  58.0 18.6 %collective-permute-start.14 = (bf16[2,128,1536]{2,1,0:T(8,128)(2,1)}, bf16[2,128,1536]{2,1,0:T(8,128)(2,1)S(1)}, u32[]{:S(2)}, u32[]{:S(2)}) collective-permute-start(bf16[2,128,1536]{2,1,0:T(8,128)(2,1)} %get-tuple-element.21), channel_id=1, source_target_pairs={{0,63},{1,0},{2,1},{3,2},{4,3},{5,4},{6,5},{7,6},{8,7},{9,8},{10,9... | collective-permute-start | bytes 2359304 | tf_op jit(solution)/shard_map/ppermute | solution.py:176
  61.8 15.8 %collective-permute-start.15 = (bf16[2,128,1536]{2,1,0:T(8,128)(2,1)}, bf16[2,128,1536]{2,1,0:T(8,128)(2,1)S(1)}, u32[]{:S(2)}, u32[]{:S(2)}) collective-permute-start(bf16[2,128,1536]{2,1,0:T(8,128)(2,1)} %get-tuple-element.22), channel_id=1, source_target_pairs={{0,1},{1,2},{2,3},{3,4},{4,5},{5,6},{6,7},{7,8},{8,9},{9,10},{10,1... | collective-permute-start | bytes 2359304 | tf_op jit(solution)/shard_map/ppermute | solution.py:176
  62.5 9.2 %collective-permute-start.13 = (f32[1,1536]{1,0:T(1,128)S(1)}, f32[1,1536]{1,0:T(1,128)S(1)}, u32[]{:S(2)}, u32[]{:S(2)}) collective-permute-start(f32[1,1536]{1,0:T(1,128)S(1)} %add_add_fusion.2), channel_id=1, source_target_pairs={{0,48},{4,52},{8,56},{12,60},{16,32},{20,36},{24,40},{28,44},{32,1... | collective-permute-start | bytes 18440 | tf_op jit(solution)/shard_map/ppermute | solution.py:186
  68.4 7.5 %collective-permute-start.12 = (f32[1,1536]{1,0:T(1,128)S(1)}, f32[1,1536]{1,0:T(1,128)S(1)}, u32[]{:S(2)}, u32[]{:S(2)}) collective-permute-start(f32[1,1536]{1,0:T(1,128)S(1)} %add_add_fusion.2), channel_id=1, source_target_pairs={{0,32},{4,36},{8,40},{12,44},{16,48},{20,52},{24,56},{28,60},{32,0... | collective-permute-start | bytes 18440 | tf_op jit(solution)/shard_map/ppermute | solution.py:186
  69.4 6.6 %collective-permute-start.11 = (f32[1,1536]{1,0:T(1,128)S(1)}, f32[1,1536]{1,0:T(1,128)S(1)}, u32[]{:S(2)}, u32[]{:S(2)}) collective-permute-start(f32[1,1536]{1,0:T(1,128)S(1)} %add_add_fusion.2), channel_id=1, source_target_pairs={{0,16},{4,20},{8,24},{12,28},{16,0},{20,4},{24,8},{28,12},{32,48},... | collective-permute-start | bytes 18440 | tf_op jit(solution)/shard_map/ppermute | solution.py:186
  78.9 25.1 %copy-start = (f32[2,128,1536]{2,1,0:T(8,128)S(1)}, f32[2,128,1536]{2,1,0:T(8,128)}, u32[]{:S(2)}) copy-start(f32[2,128,1536]{2,1,0:T(8,128)} %get-tuple-element.18) | copy-start | bytes 4718596
  78.9 25.1 %collective-permute-start.17 = (bf16[2,128,1536]{2,1,0:T(8,128)(2,1)S(1)}, bf16[2,128,1536]{2,1,0:T(8,128)(2,1)S(1)}, u32[]{:S(2)}, u32[]{:S(2)}) collective-permute-start(bf16[2,128,1536]{2,1,0:T(8,128)(2,1)S(1)} %add_convert_fusion.1), channel_id=1, source_target_pairs={{0,1},{1,2},{2,3},{3,4},{4,5},{5,6},{6,7},{7,8},{8,9},{9,10},{10,1... | collective-permute-start | bytes 2359304 | tf_op jit(solution)/shard_map/ppermute | solution.py:176
  82.9 21.1 %collective-permute-start.16 = (bf16[2,128,1536]{2,1,0:T(8,128)(2,1)S(1)}, bf16[2,128,1536]{2,1,0:T(8,128)(2,1)S(1)}, u32[]{:S(2)}, u32[]{:S(2)}) collective-permute-start(bf16[2,128,1536]{2,1,0:T(8,128)(2,1)S(1)} %add_convert_fusion.2), channel_id=1, source_target_pairs={{0,63},{1,0},{2,1},{3,2},{4,3},{5,4},{6,5},{7,6},{8,7},{9,8},{10,9... | collective-permute-start | bytes 2359304 | tf_op jit(solution)/shard_map/ppermute | solution.py:176
  85.3 6.0 %collective-permute-start.20 = (f32[1,1536]{1,0:T(1,128)S(1)}, f32[1,1536]{1,0:T(1,128)S(1)}, u32[]{:S(2)}, u32[]{:S(2)}) collective-permute-start(f32[1,1536]{1,0:T(1,128)S(1)} %add_add_fusion.1), channel_id=1, source_target_pairs={{0,12},{4,8},{8,4},{12,0},{16,28},{20,24},{24,20},{28,16},{32,44},... | collective-permute-start | bytes 18440 | tf_op jit(solution)/shard_map/ppermute | solution.py:186
  85.9 9.2 %collective-permute-start.19 = (f32[1,1536]{1,0:T(1,128)S(1)}, f32[1,1536]{1,0:T(1,128)S(1)}, u32[]{:S(2)}, u32[]{:S(2)}) collective-permute-start(f32[1,1536]{1,0:T(1,128)S(1)} %add_add_fusion.1), channel_id=1, source_target_pairs={{0,8},{4,12},{8,0},{12,4},{16,24},{20,28},{24,16},{28,20},{32,40},... | collective-permute-start | bytes 18440 | tf_op jit(solution)/shard_map/ppermute | solution.py:186
  91.2 3.8 %collective-permute-start.18 = (f32[1,1536]{1,0:T(1,128)S(1)}, f32[1,1536]{1,0:T(1,128)S(1)}, u32[]{:S(2)}, u32[]{:S(2)}) collective-permute-start(f32[1,1536]{1,0:T(1,128)S(1)} %add_add_fusion.1), channel_id=1, source_target_pairs={{0,4},{4,0},{8,12},{12,8},{16,20},{20,16},{24,28},{28,24},{32,36},... | collective-permute-start | bytes 18440 | tf_op jit(solution)/shard_map/ppermute | solution.py:186
  95.1 8.2 %collective-permute-start.23 = (f32[1,1536]{1,0:T(1,128)S(1)}, f32[1,1536]{1,0:T(1,128)S(1)}, u32[]{:S(2)}, u32[]{:S(2)}) collective-permute-start(f32[1,1536]{1,0:T(1,128)S(1)} %add_add_fusion), channel_id=1, source_target_pairs={{0,3},{1,2},{2,1},{3,0},{4,7},{5,6},{6,5},{7,4},{8,11},{9,10},{10,... | collective-permute-start | bytes 18440 | tf_op jit(solution)/shard_map/ppermute | solution.py:186
  95.2 8.1 %collective-permute-start.22 = (f32[1,1536]{1,0:T(1,128)S(1)}, f32[1,1536]{1,0:T(1,128)S(1)}, u32[]{:S(2)}, u32[]{:S(2)}) collective-permute-start(f32[1,1536]{1,0:T(1,128)S(1)} %add_add_fusion), channel_id=1, source_target_pairs={{0,2},{1,3},{2,0},{3,1},{4,6},{5,7},{6,4},{7,5},{8,10},{9,11},{10,... | collective-permute-start | bytes 18440 | tf_op jit(solution)/shard_map/ppermute | solution.py:186
  95.3 8.0 %collective-permute-start.21 = (f32[1,1536]{1,0:T(1,128)S(1)}, f32[1,1536]{1,0:T(1,128)S(1)}, u32[]{:S(2)}, u32[]{:S(2)}) collective-permute-start(f32[1,1536]{1,0:T(1,128)S(1)} %add_add_fusion), channel_id=1, source_target_pairs={{0,1},{1,0},{2,3},{3,2},{4,5},{5,4},{6,7},{7,6},{8,9},{9,8},{10,11... | collective-permute-start | bytes 18440 | tf_op jit(solution)/shard_map/ppermute | solution.py:186

commit v3 on v2

--- a/solution.py
+++ b/solution.py
@@ -188,6 +188,11 @@
     return (part + a) + (b + c)
 
 
+def paired(part, axis, mask):
+    count = lax.axis_size(axis)
+    return part + lax.ppermute(part, axis, [(i, i ^ mask) for i in range(count)])
+
+
 def shards(video_query, audio_key, audio_value, cross_gate, grad_out, pair_blocks, pair_count):
     width = cross_gate.shape[0]
     key, value = audio_key[0], audio_value[0]
@@ -200,10 +205,11 @@
         (km2, km1, key, kp1, kp2), (vm2, vm1, value, vp1, vp2),
     )
     m2, p2 = moved(m2, -1), moved(p2, 1)
-    gate_part = summed(gate_part, "clip", (1, 2, 3))
+    gate_part = paired(gate_part, "clip", 1)
     gate_part = summed(gate_part, "vid", (4, 8, 12))
     gate_part, m2, p2 = lax.optimization_barrier((gate_part, m2, p2))
     m1, p1 = moved(joined(m1, m2), -1), moved(joined(p1, p2), 1)
+    gate_part = paired(gate_part, "clip", 2)
     gate_part = summed(gate_part, "vid", (1, 2, 3))
     gate_part = summed(gate_part, "aud", (1, 2, 3))
     grads = (own + m1.astype(F32) + p1.astype(F32)).astype(BF16)

time: 107 us -> 104 us (0.972)
  starting transfers between devices: 56.4 us -> 52.8 us
    ppermute x12 -> x9, starting transfers between devices: 22.9 us -> 16.2 us  [summed(): lax.ppermute(part, axis, [(i, i ^ mask) for i in range(count)])]
    ppermute x0 -> x2, waiting for transfers between devices: none -> 6.31 us  [paired(): lax.ppermute(part, axis, [(i, i ^ mask) for i in range(count)])]
    ppermute x12 -> x9, waiting for transfers between devices: 13 us -> 9.34 us  [summed(): lax.ppermute(part, axis, [(i, i ^ mask) for i in range(count)])]
    ppermute x0 -> x2, starting transfers between devices: none -> 2.66 us  [paired(): lax.ppermute(part, axis, [(i, i ^ mask) for i in range(count)])]
    ppermute x12, waiting for transfers between devices: 12.1 us -> 10.5 us  [moved(): lax.ppermute(shard, TIME, [(i, (i + by) % count) for i in range(count)])]
  transfers between devices with their start and end apart: 24 -> 23, of which waited for: 11 -> 10; matrix products, arithmetic and copies ran while one was open for 3% -> 3% of each run, Pallas kernels for 0% -> 0%
where the time goes in v3:
time: 104 us; the launch traced here: 103 us
  starting transfers between devices  52.8 us (51%)
  waiting for transfers between devices  26.1 us (25%)
  Pallas kernels  16.8 us (16%)
  other arithmetic  3.18 us (3%)
  local copies, waits for them, and re-layouts  3.01 us (3%)
    ppermute x12, starting transfers between devices, moved(): lax.ppermute(shard, TIME, [(i, (i + by) % count) for i in range(count)])  34 us
    pallas_call x1, Pallas kernels, attend_pairs(): pl.pallas_call(pair_kernel, grid=(HEADS // GROUP,), in_specs=[smem, smem,...  16.8 us
    ppermute x9, starting transfers between devices, summed(): lax.ppermute(part, axis, [(i, i ^ mask) for i in range(count)])  16.2 us
    ppermute x12, waiting for transfers between devices, moved(): lax.ppermute(shard, TIME, [(i, (i + by) % count) for i in range(count)])  10.5 us
    ppermute x9, waiting for transfers between devices, summed(): lax.ppermute(part, axis, [(i, i ^ mask) for i in range(count)])  9.34 us
    ppermute x2, waiting for transfers between devices, paired(): lax.ppermute(part, axis, [(i, i ^ mask) for i in range(count)])  6.31 us
    ppermute x2, starting transfers between devices, paired(): lax.ppermute(part, axis, [(i, i ^ mask) for i in range(count)])  2.66 us
  transfers between devices with their start and end apart: 23, of which 10 were waited for; matrix products, arithmetic and copies ran while one was open for 3% of the time, Pallas kernels for 0%

profile of v3, /device:TPU:2, one launch (start us, length us, event | category | flops | bytes accessed | tf_op | source)
XLA Modules:
  0.0 102.7 jit_solution(17179804753230406860)
XLA Ops:
  0.6 7.8 %collective-permute-start.2 = (bf16[128,1536]{1,0:T(8,128)(2,1)}, bf16[128,1536]{1,0:T(8,128)(2,1)S(1)}, u32[]{:S(2)}, u32[]{:S(2)}) collective-permute-start(bf16[128,1536]{1,0:T(8,128)(2,1)} %bitcast.2), channel_id=1, source_target_pairs={{0,63},{1,0},{2,1},{3,2},{4,3},{5,4},{6,5},{7,6},{8,7},{9,8},{10,9... | collective-permute-start | bytes 1179656 | tf_op jit(solution)/shard_map/ppermute | solution.py:176
  8.5 0.0 collective-permute-start
  8.5 5.1 %collective-permute-start.6 = (bf16[128,1536]{1,0:T(8,128)(2,1)}, bf16[128,1536]{1,0:T(8,128)(2,1)S(1)}, u32[]{:S(2)}, u32[]{:S(2)}) collective-permute-start(bf16[128,1536]{1,0:T(8,128)(2,1)} %bitcast.5), channel_id=1, source_target_pairs={{0,63},{1,0},{2,1},{3,2},{4,3},{5,4},{6,5},{7,6},{8,7},{9,8},{10,9... | collective-permute-start | bytes 1179656 | tf_op jit(solution)/shard_map/ppermute | solution.py:176
  13.5 0.0 collective-permute-start.4
  13.5 0.6 collective-permute-done.2.refs_3_
  14.1 5.2 %collective-permute-start.3 = (bf16[128,1536]{1,0:T(8,128)(2,1)S(1)}, bf16[128,1536]{1,0:T(8,128)(2,1)S(1)}, u32[]{:S(2)}, u32[]{:S(2)}) collective-permute-start(bf16[128,1536]{1,0:T(8,128)(2,1)S(1)} %collective-permute-done.2.refs_3_), channel_id=1, source_target_pairs={{0,63},{1,0},{2,1},{3,2},{4,3},{5,4},{6,5},{7,6},{8,7},{9,8},{10,9... | collective-permute-start | bytes 1179656 | tf_op jit(solution)/shard_map/ppermute | solution.py:176
  19.3 0.0 collective-permute-done.refs_1_
  19.3 0.3 collective-permute-start.1
  19.6 0.6 collective-permute-done.6.refs_8_
  20.2 5.2 %collective-permute-start.7 = (bf16[128,1536]{1,0:T(8,128)(2,1)S(1)}, bf16[128,1536]{1,0:T(8,128)(2,1)S(1)}, u32[]{:S(2)}, u32[]{:S(2)}) collective-permute-start(bf16[128,1536]{1,0:T(8,128)(2,1)S(1)} %collective-permute-done.6.refs_8_), channel_id=1, source_target_pairs={{0,63},{1,0},{2,1},{3,2},{4,3},{5,4},{6,5},{7,6},{8,7},{9,8},{10,9... | collective-permute-start | bytes 1179656 | tf_op jit(solution)/shard_map/ppermute | solution.py:176
  25.5 0.0 collective-permute-done.4.refs_6_
  25.5 0.0 collective-permute-start.5
  25.5 1.3 %reshape.16.gate_ref = f32[1,1536]{1,0:T(1,128)} reshape(f32[1536]{0:T(1024)} %param.10) | data formatting | bytes 12288 | tf_op jit(solution)/shard_map/reshape | solution.py:204
  26.8 0.0 collective-permute-done.3.refs_4_
  26.8 3.1 %collective-permute-done.1.refs_0_ = bf16[128,1536]{1,0:T(8,128)(2,1)S(1)} collective-permute-done((bf16[128,1536]{1,0:T(8,128)(2,1)S(1)}, bf16[128,1536]{1,0:T(8,128)(2,1)S(1)}, u32[]{:S(2)}, u32[]{:S(2)}) %collective-permute-start.1) | collective-permute-done | bytes 393248 | tf_op jit(solution)/shard_map/ppermute | solution.py:176
  29.9 3.2 %collective-permute-done.7.refs_9_ = bf16[128,1536]{1,0:T(8,128)(2,1)S(1)} collective-permute-done((bf16[128,1536]{1,0:T(8,128)(2,1)S(1)}, bf16[128,1536]{1,0:T(8,128)(2,1)S(1)}, u32[]{:S(2)}, u32[]{:S(2)}) %collective-permute-start.7) | collective-permute-done | bytes 393248 | tf_op jit(solution)/shard_map/ppermute | solution.py:176
  33.1 3.0 %collective-permute-done.5.refs_5_ = bf16[128,1536]{1,0:T(8,128)(2,1)S(1)} collective-permute-done((bf16[128,1536]{1,0:T(8,128)(2,1)S(1)}, bf16[128,1536]{1,0:T(8,128)(2,1)S(1)}, u32[]{:S(2)}, u32[]{:S(2)}) %collective-permute-start.5) | collective-permute-done | bytes 393248 | tf_op jit(solution)/shard_map/ppermute | solution.py:176
  36.1 0.0 copy-done.2
  36.1 0.0 copy-done.3
  36.1 0.0 copy-done.4
  36.1 0.0 copy-done.5
  36.1 0.0 copy-done.6
  36.1 0.0 copy-done.7
  36.1 0.0 copy-done.8
  36.1 0.0 copy-start.9
  36.1 0.7 copy-done.9
  36.9 16.8 %pairs.2 = (bf16[1,512,1536]{2,1,0:T(8,128)(2,1)}, bf16[1,512,1536]{2,1,0:T(8,128)(2,1)}, f32[1,1536]{1,0:T(1,128)}, bf16[2,128,1536]{2,1,0:T(8,128)(2,1)}, bf16...) custom-call(s32[1,4,4]{2,1,0:T(4,128)} %pairs.3, ...), custom_call_target="tpu_custom_call" | custom-call | flops 6000000000 | bytes 16000000 | tf_op jit(solution)/shard_map/pairs/pallas_call | solution.py:149
  53.7 4.8 %collective-permute-start.12 = (bf16[2,128,1536]{2,1,0:T(8,128)(2,1)}, bf16[2,128,1536]{2,1,0:T(8,128)(2,1)S(1)}, u32[]{:S(2)}, u32[]{:S(2)}) collective-permute-start(bf16[2,128,1536]{2,1,0:T(8,128)(2,1)} %get-tuple-element.21), channel_id=1, source_target_pairs={{0,63},{1,0},{2,1},{3,2},{4,3},{5,4},{6,5},{7,6},{8,7},{9,8},{10,9... | collective-permute-start | bytes 2359304 | tf_op jit(solution)/shard_map/ppermute | solution.py:176
  58.5 0.0 collective-permute-start.13
  58.5 0.5 collective-permute-start.8
  59.1 3.3 %collective-permute-done.8 = f32[1,1536]{1,0:T(1,128)S(1)} collective-permute-done((f32[1,1536]{1,0:T(1,128)}, f32[1,1536]{1,0:T(1,128)S(1)}, u32[]{:S(2)}, u32[]{:S(2)}) %collective-permute-start.8) | collective-permute-done | bytes 6176 | tf_op jit(solution)/shard_map/ppermute | solution.py:193
  62.4 0.7 add.45
  63.1 5.1 %collective-permute-start.11 = (f32[1,1536]{1,0:T(1,128)S(1)}, f32[1,1536]{1,0:T(1,128)S(1)}, u32[]{:S(2)}, u32[]{:S(2)}) collective-permute-start(f32[1,1536]{1,0:T(1,128)S(1)} %add.45), channel_id=1, source_target_pairs={{0,48},{4,52},{8,56},{12,60},{16,32},{20,36},{24,40},{28,44},{32,1... | collective-permute-start | bytes 18440 | tf_op jit(solution)/shard_map/ppermute | solution.py:186
  68.1 1.0 collective-permute-start.10
  69.1 1.5 %collective-permute-start.9 = (f32[1,1536]{1,0:T(1,128)S(1)}, f32[1,1536]{1,0:T(1,128)S(1)}, u32[]{:S(2)}, u32[]{:S(2)}) collective-permute-start(f32[1,1536]{1,0:T(1,128)S(1)} %add.45), channel_id=1, source_target_pairs={{0,16},{4,20},{8,24},{12,28},{16,0},{20,4},{24,8},{28,12},{32,48},... | collective-permute-start | bytes 18440 | tf_op jit(solution)/shard_map/ppermute | solution.py:186
  70.6 0.0 collective-permute-done.11
  70.6 5.1 %collective-permute-done.10 = f32[1,1536]{1,0:T(1,128)S(1)} collective-permute-done((f32[1,1536]{1,0:T(1,128)S(1)}, f32[1,1536]{1,0:T(1,128)S(1)}, u32[]{:S(2)}, u32[]{:S(2)}) %collective-permute-start.10) | collective-permute-done | bytes 6176 | tf_op jit(solution)/shard_map/ppermute | solution.py:186
  75.7 0.0 collective-permute-done.9
  75.7 0.0 collective-permute-done.12
  75.7 0.0 collective-permute-done.13
  75.7 1.3 %add_convert_fusion.1 = bf16[2,128,1536]{2,1,0:T(8,128)(2,1)S(1)} fusion(bf16[2,128,1536]{2,1,0:T(8,128)(2,1)S(1)} %collective-permute-done.13, bf16[2,128,1536]{2,1,0:T(8,128)(2,1)} %get-tuple-element.24), kind=kLoop, calls=%fused_computation.1 | loop fusion | flops 1572864 | bytes 2359296 | tf_op jit(solution)/shard_map/convert_element_type | solution.py:180
  77.0 0.0 copy-start
  77.0 2.1 %collective-permute-start.15 = (bf16[2,128,1536]{2,1,0:T(8,128)(2,1)S(1)}, bf16[2,128,1536]{2,1,0:T(8,128)(2,1)S(1)}, u32[]{:S(2)}, u32[]{:S(2)}) collective-permute-start(bf16[2,128,1536]{2,1,0:T(8,128)(2,1)S(1)} %add_convert_fusion.1), channel_id=1, source_target_pairs={{0,1},{1,2},{2,3},{3,4},{4,5},{5,6},{6,7},{7,8},{8,9},{9,10},{10,1... | collective-permute-start | bytes 2359304 | tf_op jit(solution)/shard_map/ppermute | solution.py:176
  79.1 0.2 add_convert_fusion.2
  79.3 3.5 %collective-permute-start.14 = (bf16[2,128,1536]{2,1,0:T(8,128)(2,1)S(1)}, bf16[2,128,1536]{2,1,0:T(8,128)(2,1)S(1)}, u32[]{:S(2)}, u32[]{:S(2)}) collective-permute-start(bf16[2,128,1536]{2,1,0:T(8,128)(2,1)S(1)} %add_convert_fusion.2), channel_id=1, source_target_pairs={{0,63},{1,0},{2,1},{3,2},{4,3},{5,4},{6,5},{7,6},{8,7},{9,8},{10,9... | collective-permute-start | bytes 2359304 | tf_op jit(solution)/shard_map/ppermute | solution.py:176
  82.8 2.1 %collective-permute-start.16 = (f32[1,1536]{1,0:T(1,128)S(1)}, f32[1,1536]{1,0:T(1,128)S(1)}, u32[]{:S(2)}, u32[]{:S(2)}) collective-permute-start(f32[1,1536]{1,0:T(1,128)S(1)} %add_add_fusion.1), channel_id=1, source_target_pairs={{0,128},{64,192},{128,0},{192,64},{1,129},{65,193},{129,1},{193,65... | collective-permute-start | bytes 18440 | tf_op jit(solution)/shard_map/ppermute | solution.py:193
  84.9 3.0 %collective-permute-done.16 = f32[1,1536]{1,0:T(1,128)S(1)} collective-permute-done((f32[1,1536]{1,0:T(1,128)S(1)}, f32[1,1536]{1,0:T(1,128)S(1)}, u32[]{:S(2)}, u32[]{:S(2)}) %collective-permute-start.16) | collective-permute-done | bytes 6176 | tf_op jit(solution)/shard_map/ppermute | solution.py:193
  87.9 0.7 collective-permute-start.19
  88.6 3.8 %collective-permute-start.18 = (f32[1,1536]{1,0:T(1,128)S(1)}, f32[1,1536]{1,0:T(1,128)S(1)}, u32[]{:S(2)}, u32[]{:S(2)}) collective-permute-start(f32[1,1536]{1,0:T(1,128)S(1)} %add.53), channel_id=1, source_target_pairs={{0,8},{4,12},{8,0},{12,4},{16,24},{20,28},{24,16},{28,20},{32,40},... | collective-permute-start | bytes 18440 | tf_op jit(solution)/shard_map/ppermute | solution.py:186
  92.4 0.0 collective-permute-start.17
  92.4 0.0 collective-permute-done.19
  92.4 1.7 %collective-permute-done.18 = f32[1,1536]{1,0:T(1,128)S(1)} collective-permute-done((f32[1,1536]{1,0:T(1,128)S(1)}, f32[1,1536]{1,0:T(1,128)S(1)}, u32[]{:S(2)}, u32[]{:S(2)}) %collective-permute-start.18) | collective-permute-done | bytes 6176 | tf_op jit(solution)/shard_map/ppermute | solution.py:186
  94.0 0.0 collective-permute-done.17
  94.1 1.4 %collective-permute-start.22 = (f32[1,1536]{1,0:T(1,128)S(1)}, f32[1,1536]{1,0:T(1,128)S(1)}, u32[]{:S(2)}, u32[]{:S(2)}) collective-permute-start(f32[1,1536]{1,0:T(1,128)S(1)} %add_add_fusion), channel_id=1, source_target_pairs={{0,3},{1,2},{2,1},{3,0},{4,7},{5,6},{6,5},{7,4},{8,11},{9,10},{10,... | collective-permute-start | bytes 18440 | tf_op jit(solution)/shard_map/ppermute | solution.py:186
  95.4 0.0 collective-permute-start.21
  95.4 2.8 %collective-permute-start.20 = (f32[1,1536]{1,0:T(1,128)S(1)}, f32[1,1536]{1,0:T(1,128)S(1)}, u32[]{:S(2)}, u32[]{:S(2)}) collective-permute-start(f32[1,1536]{1,0:T(1,128)S(1)} %add_add_fusion), channel_id=1, source_target_pairs={{0,1},{1,0},{2,3},{3,2},{4,5},{5,4},{6,7},{7,6},{8,9},{9,8},{10,11... | collective-permute-start | bytes 18440 | tf_op jit(solution)/shard_map/ppermute | solution.py:186
  98.2 2.6 %collective-permute-done.22 = f32[1,1536]{1,0:T(1,128)S(1)} collective-permute-done((f32[1,1536]{1,0:T(1,128)S(1)}, f32[1,1536]{1,0:T(1,128)S(1)}, u32[]{:S(2)}, u32[]{:S(2)}) %collective-permute-start.22) | collective-permute-done | bytes 6176 | tf_op jit(solution)/shard_map/ppermute | solution.py:186
  100.8 0.0 collective-permute-done.21
  100.8 0.0 collective-permute-done.20
  100.8 0.6 add_reduce_fusion
  101.5 0.0 collective-permute-done.15
  101.5 0.0 collective-permute-done.14
  101.5 0.3 add_convert_fusion
  101.8 0.9 fusion
  (13 shorter events, 0.1 us)
Async XLA Ops:
  0.6 13.5 %collective-permute-start.2 = (bf16[128,1536]{1,0:T(8,128)(2,1)}, bf16[128,1536]{1,0:T(8,128)(2,1)S(1)}, u32[]{:S(2)}, u32[]{:S(2)}) collective-permute-start(bf16[128,1536]{1,0:T(8,128)(2,1)} %bitcast.2), channel_id=1, source_target_pairs={{0,63},{1,0},{2,1},{3,2},{4,3},{5,4},{6,5},{7,6},{8,7},{9,8},{10,9... | collective-permute-start | bytes 1179656 | tf_op jit(solution)/shard_map/ppermute | solution.py:176
  8.5 10.8 %collective-permute-start = (bf16[128,1536]{1,0:T(8,128)(2,1)}, bf16[128,1536]{1,0:T(8,128)(2,1)S(1)}, u32[]{:S(2)}, u32[]{:S(2)}) collective-permute-start(bf16[128,1536]{1,0:T(8,128)(2,1)} %bitcast.3), channel_id=1, source_target_pairs={{0,1},{1,2},{2,3},{3,4},{4,5},{5,6},{6,7},{7,8},{8,9},{9,10},{10,1... | collective-permute-start | bytes 1179656 | tf_op jit(solution)/shard_map/ppermute | solution.py:176
  8.5 11.7 %collective-permute-start.6 = (bf16[128,1536]{1,0:T(8,128)(2,1)}, bf16[128,1536]{1,0:T(8,128)(2,1)S(1)}, u32[]{:S(2)}, u32[]{:S(2)}) collective-permute-start(bf16[128,1536]{1,0:T(8,128)(2,1)} %bitcast.5), channel_id=1, source_target_pairs={{0,63},{1,0},{2,1},{3,2},{4,3},{5,4},{6,5},{7,6},{8,7},{9,8},{10,9... | collective-permute-start | bytes 1179656 | tf_op jit(solution)/shard_map/ppermute | solution.py:176
  13.5 11.9 %collective-permute-start.4 = (bf16[128,1536]{1,0:T(8,128)(2,1)}, bf16[128,1536]{1,0:T(8,128)(2,1)S(1)}, u32[]{:S(2)}, u32[]{:S(2)}) collective-permute-start(bf16[128,1536]{1,0:T(8,128)(2,1)} %bitcast.6), channel_id=1, source_target_pairs={{0,1},{1,2},{2,3},{3,4},{4,5},{5,6},{6,7},{7,8},{8,9},{9,10},{10,1... | collective-permute-start | bytes 1179656 | tf_op jit(solution)/shard_map/ppermute | solution.py:176
  14.1 22.0 %copy-start.2 = (bf16[128,1536]{1,0:T(8,128)(2,1)}, bf16[128,1536]{1,0:T(8,128)(2,1)S(1)}, u32[]{:S(2)}) copy-start(bf16[128,1536]{1,0:T(8,128)(2,1)S(1)} %collective-permute-done.2.refs_3_) | copy-start | bytes 1179652
  14.1 12.7 %collective-permute-start.3 = (bf16[128,1536]{1,0:T(8,128)(2,1)S(1)}, bf16[128,1536]{1,0:T(8,128)(2,1)S(1)}, u32[]{:S(2)}, u32[]{:S(2)}) collective-permute-start(bf16[128,1536]{1,0:T(8,128)(2,1)S(1)} %collective-permute-done.2.refs_3_), channel_id=1, source_target_pairs={{0,63},{1,0},{2,1},{3,2},{4,3},{5,4},{6,5},{7,6},{8,7},{9,8},{10,9... | collective-permute-start | bytes 1179656 | tf_op jit(solution)/shard_map/ppermute | solution.py:176
  19.3 16.8 %copy-start.3 = (bf16[128,1536]{1,0:T(8,128)(2,1)}, bf16[128,1536]{1,0:T(8,128)(2,1)S(1)}, u32[]{:S(2)}) copy-start(bf16[128,1536]{1,0:T(8,128)(2,1)S(1)} %collective-permute-done.refs_1_) | copy-start | bytes 1179652
  19.3 10.6 %collective-permute-start.1 = (bf16[128,1536]{1,0:T(8,128)(2,1)S(1)}, bf16[128,1536]{1,0:T(8,128)(2,1)S(1)}, u32[]{:S(2)}, u32[]{:S(2)}) collective-permute-start(bf16[128,1536]{1,0:T(8,128)(2,1)S(1)} %collective-permute-done.refs_1_), channel_id=1, source_target_pairs={{0,1},{1,2},{2,3},{3,4},{4,5},{5,6},{6,7},{7,8},{8,9},{9,10},{10,1... | collective-permute-start | bytes 1179656 | tf_op jit(solution)/shard_map/ppermute | solution.py:176
  20.2 15.9 %copy-start.4 = (bf16[128,1536]{1,0:T(8,128)(2,1)}, bf16[128,1536]{1,0:T(8,128)(2,1)S(1)}, u32[]{:S(2)}) copy-start(bf16[128,1536]{1,0:T(8,128)(2,1)S(1)} %collective-permute-done.6.refs_8_) | copy-start | bytes 1179652
  20.2 12.9 %collective-permute-start.7 = (bf16[128,1536]{1,0:T(8,128)(2,1)S(1)}, bf16[128,1536]{1,0:T(8,128)(2,1)S(1)}, u32[]{:S(2)}, u32[]{:S(2)}) collective-permute-start(bf16[128,1536]{1,0:T(8,128)(2,1)S(1)} %collective-permute-done.6.refs_8_), channel_id=1, source_target_pairs={{0,63},{1,0},{2,1},{3,2},{4,3},{5,4},{6,5},{7,6},{8,7},{9,8},{10,9... | collective-permute-start | bytes 1179656 | tf_op jit(solution)/shard_map/ppermute | solution.py:176
  25.5 10.6 %copy-start.5 = (bf16[128,1536]{1,0:T(8,128)(2,1)}, bf16[128,1536]{1,0:T(8,128)(2,1)S(1)}, u32[]{:S(2)}) copy-start(bf16[128,1536]{1,0:T(8,128)(2,1)S(1)} %collective-permute-done.4.refs_6_) | copy-start | bytes 1179652
  25.5 10.6 %collective-permute-start.5 = (bf16[128,1536]{1,0:T(8,128)(2,1)S(1)}, bf16[128,1536]{1,0:T(8,128)(2,1)S(1)}, u32[]{:S(2)}, u32[]{:S(2)}) collective-permute-start(bf16[128,1536]{1,0:T(8,128)(2,1)S(1)} %collective-permute-done.4.refs_6_), channel_id=1, source_target_pairs={{0,1},{1,2},{2,3},{3,4},{4,5},{5,6},{6,7},{7,8},{8,9},{9,10},{10,1... | collective-permute-start | bytes 1179656 | tf_op jit(solution)/shard_map/ppermute | solution.py:176
  26.8 9.3 %copy-start.6 = (bf16[128,1536]{1,0:T(8,128)(2,1)}, bf16[128,1536]{1,0:T(8,128)(2,1)S(1)}, u32[]{:S(2)}) copy-start(bf16[128,1536]{1,0:T(8,128)(2,1)S(1)} %collective-permute-done.3.refs_4_) | copy-start | bytes 1179652
  29.9 6.3 %copy-start.7 = (bf16[128,1536]{1,0:T(8,128)(2,1)}, bf16[128,1536]{1,0:T(8,128)(2,1)S(1)}, u32[]{:S(2)}) copy-start(bf16[128,1536]{1,0:T(8,128)(2,1)S(1)} %collective-permute-done.1.refs_0_) | copy-start | bytes 1179652
  33.1 3.0 %copy-start.8 = (bf16[128,1536]{1,0:T(8,128)(2,1)}, bf16[128,1536]{1,0:T(8,128)(2,1)S(1)}, u32[]{:S(2)}) copy-start(bf16[128,1536]{1,0:T(8,128)(2,1)S(1)} %collective-permute-done.7.refs_9_) | copy-start | bytes 1179652
  36.1 0.7 copy-start.9
  53.7 25.4 %copy-start.1 = (bf16[2,128,1536]{2,1,0:T(8,128)(2,1)S(1)}, bf16[2,128,1536]{2,1,0:T(8,128)(2,1)}, u32[]{:S(2)}) copy-start(bf16[2,128,1536]{2,1,0:T(8,128)(2,1)} %get-tuple-element.19) | copy-start | bytes 2359300
  53.7 22.0 %collective-permute-start.12 = (bf16[2,128,1536]{2,1,0:T(8,128)(2,1)}, bf16[2,128,1536]{2,1,0:T(8,128)(2,1)S(1)}, u32[]{:S(2)}, u32[]{:S(2)}) collective-permute-start(bf16[2,128,1536]{2,1,0:T(8,128)(2,1)} %get-tuple-element.21), channel_id=1, source_target_pairs={{0,63},{1,0},{2,1},{3,2},{4,3},{5,4},{6,5},{7,6},{8,7},{9,8},{10,9... | collective-permute-start | bytes 2359304 | tf_op jit(solution)/shard_map/ppermute | solution.py:176
  58.5 17.2 %collective-permute-start.13 = (bf16[2,128,1536]{2,1,0:T(8,128)(2,1)}, bf16[2,128,1536]{2,1,0:T(8,128)(2,1)S(1)}, u32[]{:S(2)}, u32[]{:S(2)}) collective-permute-start(bf16[2,128,1536]{2,1,0:T(8,128)(2,1)} %get-tuple-element.22), channel_id=1, source_target_pairs={{0,1},{1,2},{2,3},{3,4},{4,5},{5,6},{6,7},{7,8},{8,9},{9,10},{10,1... | collective-permute-start | bytes 2359304 | tf_op jit(solution)/shard_map/ppermute | solution.py:176
  58.5 3.8 %collective-permute-start.8 = (f32[1,1536]{1,0:T(1,128)}, f32[1,1536]{1,0:T(1,128)S(1)}, u32[]{:S(2)}, u32[]{:S(2)}) collective-permute-start(f32[1,1536]{1,0:T(1,128)} %get-tuple-element.20), channel_id=1, source_target_pairs={{0,64},{64,0},{128,192},{192,128},{1,65},{65,1},{129,193},{193,129... | collective-permute-start | bytes 18440 | tf_op jit(solution)/shard_map/ppermute | solution.py:193
  63.1 7.5 %collective-permute-start.11 = (f32[1,1536]{1,0:T(1,128)S(1)}, f32[1,1536]{1,0:T(1,128)S(1)}, u32[]{:S(2)}, u32[]{:S(2)}) collective-permute-start(f32[1,1536]{1,0:T(1,128)S(1)} %add.45), channel_id=1, source_target_pairs={{0,48},{4,52},{8,56},{12,60},{16,32},{20,36},{24,40},{28,44},{32,1... | collective-permute-start | bytes 18440 | tf_op jit(solution)/shard_map/ppermute | solution.py:186
  68.1 7.5 %collective-permute-start.10 = (f32[1,1536]{1,0:T(1,128)S(1)}, f32[1,1536]{1,0:T(1,128)S(1)}, u32[]{:S(2)}, u32[]{:S(2)}) collective-permute-start(f32[1,1536]{1,0:T(1,128)S(1)} %add.45), channel_id=1, source_target_pairs={{0,32},{4,36},{8,40},{12,44},{16,48},{20,52},{24,56},{28,60},{32,0... | collective-permute-start | bytes 18440 | tf_op jit(solution)/shard_map/ppermute | solution.py:186
  69.1 6.6 %collective-permute-start.9 = (f32[1,1536]{1,0:T(1,128)S(1)}, f32[1,1536]{1,0:T(1,128)S(1)}, u32[]{:S(2)}, u32[]{:S(2)}) collective-permute-start(f32[1,1536]{1,0:T(1,128)S(1)} %add.45), channel_id=1, source_target_pairs={{0,16},{4,20},{8,24},{12,28},{16,0},{20,4},{24,8},{28,12},{32,48},... | collective-permute-start | bytes 18440 | tf_op jit(solution)/shard_map/ppermute | solution.py:186
  77.0 24.4 %copy-start = (f32[2,128,1536]{2,1,0:T(8,128)S(1)}, f32[2,128,1536]{2,1,0:T(8,128)}, u32[]{:S(2)}) copy-start(f32[2,128,1536]{2,1,0:T(8,128)} %get-tuple-element.18) | copy-start | bytes 4718596
  77.0 24.4 %collective-permute-start.15 = (bf16[2,128,1536]{2,1,0:T(8,128)(2,1)S(1)}, bf16[2,128,1536]{2,1,0:T(8,128)(2,1)S(1)}, u32[]{:S(2)}, u32[]{:S(2)}) collective-permute-start(bf16[2,128,1536]{2,1,0:T(8,128)(2,1)S(1)} %add_convert_fusion.1), channel_id=1, source_target_pairs={{0,1},{1,2},{2,3},{3,4},{4,5},{5,6},{6,7},{7,8},{8,9},{9,10},{10,1... | collective-permute-start | bytes 2359304 | tf_op jit(solution)/shard_map/ppermute | solution.py:176
  79.3 22.2 %collective-permute-start.14 = (bf16[2,128,1536]{2,1,0:T(8,128)(2,1)S(1)}, bf16[2,128,1536]{2,1,0:T(8,128)(2,1)S(1)}, u32[]{:S(2)}, u32[]{:S(2)}) collective-permute-start(bf16[2,128,1536]{2,1,0:T(8,128)(2,1)S(1)} %add_convert_fusion.2), channel_id=1, source_target_pairs={{0,63},{1,0},{2,1},{3,2},{4,3},{5,4},{6,5},{7,6},{8,7},{9,8},{10,9... | collective-permute-start | bytes 2359304 | tf_op jit(solution)/shard_map/ppermute | solution.py:176
  82.8 5.1 %collective-permute-start.16 = (f32[1,1536]{1,0:T(1,128)S(1)}, f32[1,1536]{1,0:T(1,128)S(1)}, u32[]{:S(2)}, u32[]{:S(2)}) collective-permute-start(f32[1,1536]{1,0:T(1,128)S(1)} %add_add_fusion.1), channel_id=1, source_target_pairs={{0,128},{64,192},{128,0},{192,64},{1,129},{65,193},{129,1},{193,65... | collective-permute-start | bytes 18440 | tf_op jit(solution)/shard_map/ppermute | solution.py:193
  87.9 4.5 %collective-permute-start.19 = (f32[1,1536]{1,0:T(1,128)S(1)}, f32[1,1536]{1,0:T(1,128)S(1)}, u32[]{:S(2)}, u32[]{:S(2)}) collective-permute-start(f32[1,1536]{1,0:T(1,128)S(1)} %add.53), channel_id=1, source_target_pairs={{0,12},{4,8},{8,4},{12,0},{16,28},{20,24},{24,20},{28,16},{32,44},... | collective-permute-start | bytes 18440 | tf_op jit(solution)/shard_map/ppermute | solution.py:186
  88.6 5.4 %collective-permute-start.18 = (f32[1,1536]{1,0:T(1,128)S(1)}, f32[1,1536]{1,0:T(1,128)S(1)}, u32[]{:S(2)}, u32[]{:S(2)}) collective-permute-start(f32[1,1536]{1,0:T(1,128)S(1)} %add.53), channel_id=1, source_target_pairs={{0,8},{4,12},{8,0},{12,4},{16,24},{20,28},{24,16},{28,20},{32,40},... | collective-permute-start | bytes 18440 | tf_op jit(solution)/shard_map/ppermute | solution.py:186
  92.4 1.7 %collective-permute-start.17 = (f32[1,1536]{1,0:T(1,128)S(1)}, f32[1,1536]{1,0:T(1,128)S(1)}, u32[]{:S(2)}, u32[]{:S(2)}) collective-permute-start(f32[1,1536]{1,0:T(1,128)S(1)} %add.53), channel_id=1, source_target_pairs={{0,4},{4,0},{8,12},{12,8},{16,20},{20,16},{24,28},{28,24},{32,36},... | collective-permute-start | bytes 18440 | tf_op jit(solution)/shard_map/ppermute | solution.py:186
  94.1 6.8 %collective-permute-start.22 = (f32[1,1536]{1,0:T(1,128)S(1)}, f32[1,1536]{1,0:T(1,128)S(1)}, u32[]{:S(2)}, u32[]{:S(2)}) collective-permute-start(f32[1,1536]{1,0:T(1,128)S(1)} %add_add_fusion), channel_id=1, source_target_pairs={{0,3},{1,2},{2,1},{3,0},{4,7},{5,6},{6,5},{7,4},{8,11},{9,10},{10,... | collective-permute-start | bytes 18440 | tf_op jit(solution)/shard_map/ppermute | solution.py:186
  95.4 5.4 %collective-permute-start.21 = (f32[1,1536]{1,0:T(1,128)S(1)}, f32[1,1536]{1,0:T(1,128)S(1)}, u32[]{:S(2)}, u32[]{:S(2)}) collective-permute-start(f32[1,1536]{1,0:T(1,128)S(1)} %add_add_fusion), channel_id=1, source_target_pairs={{0,2},{1,3},{2,0},{3,1},{4,6},{5,7},{6,4},{7,5},{8,10},{9,11},{10,... | collective-permute-start | bytes 18440 | tf_op jit(solution)/shard_map/ppermute | solution.py:186
  95.4 5.4 %collective-permute-start.20 = (f32[1,1536]{1,0:T(1,128)S(1)}, f32[1,1536]{1,0:T(1,128)S(1)}, u32[]{:S(2)}, u32[]{:S(2)}) collective-permute-start(f32[1,1536]{1,0:T(1,128)S(1)} %add_add_fusion), channel_id=1, source_target_pairs={{0,1},{1,0},{2,3},{3,2},{4,5},{5,4},{6,7},{7,6},{8,9},{9,8},{10,11... | collective-permute-start | bytes 18440 | tf_op jit(solution)/shard_map/ppermute | solution.py:186

commit v4 on v3

--- a/solution.py
+++ b/solution.py
@@ -162,7 +162,7 @@
             pltpu.VMEM((GROUP, WINDOW * BLOCK, vrows), BF16),
         ],
         compiler_params=pltpu.CompilerParams(
-            vmem_limit_bytes=60 * 2**20, dimension_semantics=("arbitrary",)
+            vmem_limit_bytes=64 * 2**20 - 2**18, dimension_semantics=("arbitrary",)
         ),
         cost_estimate=pl.CostEstimate(
             flops=6 * 10**9, bytes_accessed=16 * 10**6, transcendentals=4 * 10**6

time: 104 us -> 103 us (level)
    ppermute x12, waiting for transfers between devices: 10.5 us -> 9.39 us  [moved(): lax.ppermute(shard, TIME, [(i, (i + by) % count) for i in range(count)])]
where the time goes in v4:
time: 103 us; the launch traced here: 102 us
  starting transfers between devices  52.4 us (51%)
  waiting for transfers between devices  25.2 us (24%)
  Pallas kernels  16.8 us (16%)
  local copies, waits for them, and re-layouts  3.76 us (4%)
  other arithmetic  3.18 us (3%)
    ppermute x12, starting transfers between devices, moved(): lax.ppermute(shard, TIME, [(i, (i + by) % count) for i in range(count)])  33.7 us
    pallas_call x1, Pallas kernels, attend_pairs(): pl.pallas_call(pair_kernel, grid=(HEADS // GROUP,), in_specs=[smem, smem,...  16.8 us
    ppermute x9, starting transfers between devices, summed(): lax.ppermute(part, axis, [(i, i ^ mask) for i in range(count)])  16.1 us
    ppermute x9, waiting for transfers between devices, summed(): lax.ppermute(part, axis, [(i, i ^ mask) for i in range(count)])  9.48 us
    ppermute x12, waiting for transfers between devices, moved(): lax.ppermute(shard, TIME, [(i, (i + by) % count) for i in range(count)])  9.39 us
    ppermute x2, waiting for transfers between devices, paired(): lax.ppermute(part, axis, [(i, i ^ mask) for i in range(count)])  6.31 us
    ppermute x2, starting transfers between devices, paired(): lax.ppermute(part, axis, [(i, i ^ mask) for i in range(count)])  2.66 us
  transfers between devices with their start and end apart: 23, of which 10 were waited for; matrix products, arithmetic and copies ran while one was open for 3% of the time, Pallas kernels for 0%

profile of v4, /device:TPU:2, one launch (start us, length us, event | category | flops | bytes accessed | tf_op | source)
XLA Modules:
  0.0 102.0 jit_solution(14631686313395353170)
XLA Ops:
  0.6 7.8 %collective-permute-start.2 = (bf16[128,1536]{1,0:T(8,128)(2,1)}, bf16[128,1536]{1,0:T(8,128)(2,1)S(1)}, u32[]{:S(2)}, u32[]{:S(2)}) collective-permute-start(bf16[128,1536]{1,0:T(8,128)(2,1)} %bitcast.2), channel_id=1, source_target_pairs={{0,63},{1,0},{2,1},{3,2},{4,3},{5,4},{6,5},{7,6},{8,7},{9,8},{10,9... | collective-permute-start | bytes 1179656 | tf_op jit(solution)/shard_map/ppermute | solution.py:176
  8.5 0.0 collective-permute-start
  8.5 5.1 %collective-permute-start.6 = (bf16[128,1536]{1,0:T(8,128)(2,1)}, bf16[128,1536]{1,0:T(8,128)(2,1)S(1)}, u32[]{:S(2)}, u32[]{:S(2)}) collective-permute-start(bf16[128,1536]{1,0:T(8,128)(2,1)} %bitcast.5), channel_id=1, source_target_pairs={{0,63},{1,0},{2,1},{3,2},{4,3},{5,4},{6,5},{7,6},{8,7},{9,8},{10,9... | collective-permute-start | bytes 1179656 | tf_op jit(solution)/shard_map/ppermute | solution.py:176
  13.5 0.0 collective-permute-start.4
  13.5 0.6 collective-permute-done.2.refs_3_
  14.1 0.7 copy-done.2
  14.9 5.2 %collective-permute-start.3 = (bf16[128,1536]{1,0:T(8,128)(2,1)S(1)}, bf16[128,1536]{1,0:T(8,128)(2,1)S(1)}, u32[]{:S(2)}, u32[]{:S(2)}) collective-permute-start(bf16[128,1536]{1,0:T(8,128)(2,1)S(1)} %collective-permute-done.2.refs_3_), channel_id=1, source_target_pairs={{0,63},{1,0},{2,1},{3,2},{4,3},{5,4},{6,5},{7,6},{8,7},{9,8},{10,9... | collective-permute-start | bytes 1179656 | tf_op jit(solution)/shard_map/ppermute | solution.py:176
  20.0 0.0 collective-permute-done.refs_1_
  20.1 0.0 collective-permute-start.1
  20.1 0.1 collective-permute-done.6.refs_8_
  20.2 5.2 %collective-permute-start.7 = (bf16[128,1536]{1,0:T(8,128)(2,1)S(1)}, bf16[128,1536]{1,0:T(8,128)(2,1)S(1)}, u32[]{:S(2)}, u32[]{:S(2)}) collective-permute-start(bf16[128,1536]{1,0:T(8,128)(2,1)S(1)} %collective-permute-done.6.refs_8_), channel_id=1, source_target_pairs={{0,63},{1,0},{2,1},{3,2},{4,3},{5,4},{6,5},{7,6},{8,7},{9,8},{10,9... | collective-permute-start | bytes 1179656 | tf_op jit(solution)/shard_map/ppermute | solution.py:176
  25.5 0.0 collective-permute-done.4.refs_6_
  25.5 0.0 collective-permute-start.5
  25.5 1.3 %reshape.16.gate_ref = f32[1,1536]{1,0:T(1,128)} reshape(f32[1536]{0:T(1024)} %param.10) | data formatting | bytes 12288 | tf_op jit(solution)/shard_map/reshape | solution.py:204
  26.8 0.0 collective-permute-done.3.refs_4_
  26.8 0.0 copy-done.3
  26.8 3.8 %collective-permute-done.1.refs_0_ = bf16[128,1536]{1,0:T(8,128)(2,1)S(1)} collective-permute-done((bf16[128,1536]{1,0:T(8,128)(2,1)S(1)}, bf16[128,1536]{1,0:T(8,128)(2,1)S(1)}, u32[]{:S(2)}, u32[]{:S(2)}) %collective-permute-start.1) | collective-permute-done | bytes 393248 | tf_op jit(solution)/shard_map/ppermute | solution.py:176
  30.6 0.0 copy-done.4
  30.6 1.9 %collective-permute-done.7.refs_9_ = bf16[128,1536]{1,0:T(8,128)(2,1)S(1)} collective-permute-done((bf16[128,1536]{1,0:T(8,128)(2,1)S(1)}, bf16[128,1536]{1,0:T(8,128)(2,1)S(1)}, u32[]{:S(2)}, u32[]{:S(2)}) %collective-permute-start.7) | collective-permute-done | bytes 393248 | tf_op jit(solution)/shard_map/ppermute | solution.py:176
  32.6 0.0 copy-done.5
  32.6 0.0 copy-done.6
  32.6 0.0 copy-done.7
  32.6 0.0 copy-start.8
  32.6 0.7 copy-done.8
  33.3 2.9 %collective-permute-done.5.refs_5_ = bf16[128,1536]{1,0:T(8,128)(2,1)} collective-permute-done((bf16[128,1536]{1,0:T(8,128)(2,1)S(1)}, bf16[128,1536]{1,0:T(8,128)(2,1)}, u32[]{:S(2)}, u32[]{:S(2)}) %collective-permute-start.5) | collective-permute-done | bytes 393248 | tf_op jit(solution)/shard_map/ppermute | solution.py:176
  36.2 16.8 %pairs.2 = (bf16[1,512,1536]{2,1,0:T(8,128)(2,1)}, bf16[1,512,1536]{2,1,0:T(8,128)(2,1)}, f32[1,1536]{1,0:T(1,128)}, bf16[2,128,1536]{2,1,0:T(8,128)(2,1)}, bf16...) custom-call(s32[1,4,4]{2,1,0:T(4,128)} %pairs.3, ...), custom_call_target="tpu_custom_call" | custom-call | flops 6000000000 | bytes 16000000 | tf_op jit(solution)/shard_map/pairs/pallas_call | solution.py:149
  53.0 0.0 copy-start.1
  53.0 4.7 %collective-permute-start.12 = (bf16[2,128,1536]{2,1,0:T(8,128)(2,1)}, bf16[2,128,1536]{2,1,0:T(8,128)(2,1)S(1)}, u32[]{:S(2)}, u32[]{:S(2)}) collective-permute-start(bf16[2,128,1536]{2,1,0:T(8,128)(2,1)} %get-tuple-element.21), channel_id=1, source_target_pairs={{0,63},{1,0},{2,1},{3,2},{4,3},{5,4},{6,5},{7,6},{8,7},{9,8},{10,9... | collective-permute-start | bytes 2359304 | tf_op jit(solution)/shard_map/ppermute | solution.py:176
  57.7 0.0 collective-permute-start.13
  57.7 0.5 collective-permute-start.8
  58.2 3.3 %collective-permute-done.8 = f32[1,1536]{1,0:T(1,128)S(1)} collective-permute-done((f32[1,1536]{1,0:T(1,128)}, f32[1,1536]{1,0:T(1,128)S(1)}, u32[]{:S(2)}, u32[]{:S(2)}) %collective-permute-start.8) | collective-permute-done | bytes 6176 | tf_op jit(solution)/shard_map/ppermute | solution.py:193
  61.6 0.7 add.45
  62.3 5.1 %collective-permute-start.11 = (f32[1,1536]{1,0:T(1,128)S(1)}, f32[1,1536]{1,0:T(1,128)S(1)}, u32[]{:S(2)}, u32[]{:S(2)}) collective-permute-start(f32[1,1536]{1,0:T(1,128)S(1)} %add.45), channel_id=1, source_target_pairs={{0,48},{4,52},{8,56},{12,60},{16,32},{20,36},{24,40},{28,44},{32,1... | collective-permute-start | bytes 18440 | tf_op jit(solution)/shard_map/ppermute | solution.py:186
  67.4 1.0 collective-permute-start.10
  68.4 1.5 %collective-permute-start.9 = (f32[1,1536]{1,0:T(1,128)S(1)}, f32[1,1536]{1,0:T(1,128)S(1)}, u32[]{:S(2)}, u32[]{:S(2)}) collective-permute-start(f32[1,1536]{1,0:T(1,128)S(1)} %add.45), channel_id=1, source_target_pairs={{0,16},{4,20},{8,24},{12,28},{16,0},{20,4},{24,8},{28,12},{32,48},... | collective-permute-start | bytes 18440 | tf_op jit(solution)/shard_map/ppermute | solution.py:186
  69.9 0.0 collective-permute-done.11
  69.9 5.1 %collective-permute-done.10 = f32[1,1536]{1,0:T(1,128)S(1)} collective-permute-done((f32[1,1536]{1,0:T(1,128)S(1)}, f32[1,1536]{1,0:T(1,128)S(1)}, u32[]{:S(2)}, u32[]{:S(2)}) %collective-permute-start.10) | collective-permute-done | bytes 6176 | tf_op jit(solution)/shard_map/ppermute | solution.py:186
  74.9 0.0 collective-permute-done.9
  75.0 0.0 collective-permute-done.12
  75.0 0.0 collective-permute-done.13
  75.0 1.3 %add_convert_fusion.1 = bf16[2,128,1536]{2,1,0:T(8,128)(2,1)S(1)} fusion(bf16[2,128,1536]{2,1,0:T(8,128)(2,1)S(1)} %collective-permute-done.13, bf16[2,128,1536]{2,1,0:T(8,128)(2,1)} %get-tuple-element.24), kind=kLoop, calls=%fused_computation.1 | loop fusion | flops 1572864 | bytes 2359296 | tf_op jit(solution)/shard_map/convert_element_type | solution.py:180
  76.3 2.0 %collective-permute-start.15 = (bf16[2,128,1536]{2,1,0:T(8,128)(2,1)S(1)}, bf16[2,128,1536]{2,1,0:T(8,128)(2,1)S(1)}, u32[]{:S(2)}, u32[]{:S(2)}) collective-permute-start(bf16[2,128,1536]{2,1,0:T(8,128)(2,1)S(1)} %add_convert_fusion.1), channel_id=1, source_target_pairs={{0,1},{1,2},{2,3},{3,4},{4,5},{5,6},{6,7},{7,8},{8,9},{9,10},{10,1... | collective-permute-start | bytes 2359304 | tf_op jit(solution)/shard_map/ppermute | solution.py:176
  78.4 0.2 add_convert_fusion.2
  78.5 3.6 %collective-permute-start.14 = (bf16[2,128,1536]{2,1,0:T(8,128)(2,1)S(1)}, bf16[2,128,1536]{2,1,0:T(8,128)(2,1)S(1)}, u32[]{:S(2)}, u32[]{:S(2)}) collective-permute-start(bf16[2,128,1536]{2,1,0:T(8,128)(2,1)S(1)} %add_convert_fusion.2), channel_id=1, source_target_pairs={{0,63},{1,0},{2,1},{3,2},{4,3},{5,4},{6,5},{7,6},{8,7},{9,8},{10,9... | collective-permute-start | bytes 2359304 | tf_op jit(solution)/shard_map/ppermute | solution.py:176
  82.1 2.1 %collective-permute-start.16 = (f32[1,1536]{1,0:T(1,128)S(1)}, f32[1,1536]{1,0:T(1,128)S(1)}, u32[]{:S(2)}, u32[]{:S(2)}) collective-permute-start(f32[1,1536]{1,0:T(1,128)S(1)} %add_add_fusion.1), channel_id=1, source_target_pairs={{0,128},{64,192},{128,0},{192,64},{1,129},{65,193},{129,1},{193,65... | collective-permute-start | bytes 18440 | tf_op jit(solution)/shard_map/ppermute | solution.py:193
  84.2 3.0 %collective-permute-done.16 = f32[1,1536]{1,0:T(1,128)S(1)} collective-permute-done((f32[1,1536]{1,0:T(1,128)S(1)}, f32[1,1536]{1,0:T(1,128)S(1)}, u32[]{:S(2)}, u32[]{:S(2)}) %collective-permute-start.16) | collective-permute-done | bytes 6176 | tf_op jit(solution)/shard_map/ppermute | solution.py:193
  87.2 0.6 collective-permute-start.19
  87.9 3.7 %collective-permute-start.18 = (f32[1,1536]{1,0:T(1,128)S(1)}, f32[1,1536]{1,0:T(1,128)S(1)}, u32[]{:S(2)}, u32[]{:S(2)}) collective-permute-start(f32[1,1536]{1,0:T(1,128)S(1)} %add.53), channel_id=1, source_target_pairs={{0,8},{4,12},{8,0},{12,4},{16,24},{20,28},{24,16},{28,20},{32,40},... | collective-permute-start | bytes 18440 | tf_op jit(solution)/shard_map/ppermute | solution.py:186
  91.6 0.0 collective-permute-start.17
  91.6 0.0 collective-permute-done.19
  91.6 1.7 %collective-permute-done.18 = f32[1,1536]{1,0:T(1,128)S(1)} collective-permute-done((f32[1,1536]{1,0:T(1,128)S(1)}, f32[1,1536]{1,0:T(1,128)S(1)}, u32[]{:S(2)}, u32[]{:S(2)}) %collective-permute-start.18) | collective-permute-done | bytes 6176 | tf_op jit(solution)/shard_map/ppermute | solution.py:186
  93.2 0.0 collective-permute-done.17
  93.3 1.4 %collective-permute-start.22 = (f32[1,1536]{1,0:T(1,128)S(1)}, f32[1,1536]{1,0:T(1,128)S(1)}, u32[]{:S(2)}, u32[]{:S(2)}) collective-permute-start(f32[1,1536]{1,0:T(1,128)S(1)} %add_add_fusion), channel_id=1, source_target_pairs={{0,3},{1,2},{2,1},{3,0},{4,7},{5,6},{6,5},{7,4},{8,11},{9,10},{10,... | collective-permute-start | bytes 18440 | tf_op jit(solution)/shard_map/ppermute | solution.py:186
  94.6 0.0 collective-permute-start.21
  94.6 2.8 %collective-permute-start.20 = (f32[1,1536]{1,0:T(1,128)S(1)}, f32[1,1536]{1,0:T(1,128)S(1)}, u32[]{:S(2)}, u32[]{:S(2)}) collective-permute-start(f32[1,1536]{1,0:T(1,128)S(1)} %add_add_fusion), channel_id=1, source_target_pairs={{0,1},{1,0},{2,3},{3,2},{4,5},{5,4},{6,7},{7,6},{8,9},{9,8},{10,11... | collective-permute-start | bytes 18440 | tf_op jit(solution)/shard_map/ppermute | solution.py:186
  97.4 2.7 %collective-permute-done.22 = f32[1,1536]{1,0:T(1,128)S(1)} collective-permute-done((f32[1,1536]{1,0:T(1,128)S(1)}, f32[1,1536]{1,0:T(1,128)S(1)}, u32[]{:S(2)}, u32[]{:S(2)}) %collective-permute-start.22) | collective-permute-done | bytes 6176 | tf_op jit(solution)/shard_map/ppermute | solution.py:186
  100.2 0.0 collective-permute-done.21
  100.2 0.0 collective-permute-done.20
  100.2 0.6 add_reduce_fusion
  100.8 0.0 collective-permute-done.15
  100.8 0.0 collective-permute-done.14
  100.8 0.0 copy-done
  100.8 0.3 add_convert_fusion
  101.1 0.9 fusion
  (11 shorter events, 0.0 us)
Async XLA Ops:
  0.6 13.5 %collective-permute-start.2 = (bf16[128,1536]{1,0:T(8,128)(2,1)}, bf16[128,1536]{1,0:T(8,128)(2,1)S(1)}, u32[]{:S(2)}, u32[]{:S(2)}) collective-permute-start(bf16[128,1536]{1,0:T(8,128)(2,1)} %bitcast.2), channel_id=1, source_target_pairs={{0,63},{1,0},{2,1},{3,2},{4,3},{5,4},{6,5},{7,6},{8,7},{9,8},{10,9... | collective-permute-start | bytes 1179656 | tf_op jit(solution)/shard_map/ppermute | solution.py:176
  8.5 11.6 %collective-permute-start = (bf16[128,1536]{1,0:T(8,128)(2,1)}, bf16[128,1536]{1,0:T(8,128)(2,1)S(1)}, u32[]{:S(2)}, u32[]{:S(2)}) collective-permute-start(bf16[128,1536]{1,0:T(8,128)(2,1)} %bitcast.3), channel_id=1, source_target_pairs={{0,1},{1,2},{2,3},{3,4},{4,5},{5,6},{6,7},{7,8},{8,9},{9,10},{10,1... | collective-permute-start | bytes 1179656 | tf_op jit(solution)/shard_map/ppermute | solution.py:176
  8.5 11.7 %collective-permute-start.6 = (bf16[128,1536]{1,0:T(8,128)(2,1)}, bf16[128,1536]{1,0:T(8,128)(2,1)S(1)}, u32[]{:S(2)}, u32[]{:S(2)}) collective-permute-start(bf16[128,1536]{1,0:T(8,128)(2,1)} %bitcast.5), channel_id=1, source_target_pairs={{0,63},{1,0},{2,1},{3,2},{4,3},{5,4},{6,5},{7,6},{8,7},{9,8},{10,9... | collective-permute-start | bytes 1179656 | tf_op jit(solution)/shard_map/ppermute | solution.py:176
  13.5 11.9 %collective-permute-start.4 = (bf16[128,1536]{1,0:T(8,128)(2,1)}, bf16[128,1536]{1,0:T(8,128)(2,1)S(1)}, u32[]{:S(2)}, u32[]{:S(2)}) collective-permute-start(bf16[128,1536]{1,0:T(8,128)(2,1)} %bitcast.6), channel_id=1, source_target_pairs={{0,1},{1,2},{2,3},{3,4},{4,5},{5,6},{6,7},{7,8},{8,9},{9,10},{10,1... | collective-permute-start | bytes 1179656 | tf_op jit(solution)/shard_map/ppermute | solution.py:176
  14.1 0.7 copy-start.2
  14.9 11.9 %collective-permute-start.3 = (bf16[128,1536]{1,0:T(8,128)(2,1)S(1)}, bf16[128,1536]{1,0:T(8,128)(2,1)S(1)}, u32[]{:S(2)}, u32[]{:S(2)}) collective-permute-start(bf16[128,1536]{1,0:T(8,128)(2,1)S(1)} %collective-permute-done.2.refs_3_), channel_id=1, source_target_pairs={{0,63},{1,0},{2,1},{3,2},{4,3},{5,4},{6,5},{7,6},{8,7},{9,8},{10,9... | collective-permute-start | bytes 1179656 | tf_op jit(solution)/shard_map/ppermute | solution.py:176
  20.0 6.7 %copy-start.3 = (bf16[128,1536]{1,0:T(8,128)(2,1)}, bf16[128,1536]{1,0:T(8,128)(2,1)S(1)}, u32[]{:S(2)}) copy-start(bf16[128,1536]{1,0:T(8,128)(2,1)S(1)} %collective-permute-done.refs_1_) | copy-start | bytes 1179652
  20.1 10.6 %collective-permute-start.1 = (bf16[128,1536]{1,0:T(8,128)(2,1)S(1)}, bf16[128,1536]{1,0:T(8,128)(2,1)S(1)}, u32[]{:S(2)}, u32[]{:S(2)}) collective-permute-start(bf16[128,1536]{1,0:T(8,128)(2,1)S(1)} %collective-permute-done.refs_1_), channel_id=1, source_target_pairs={{0,1},{1,2},{2,3},{3,4},{4,5},{5,6},{6,7},{7,8},{8,9},{9,10},{10,1... | collective-permute-start | bytes 1179656 | tf_op jit(solution)/shard_map/ppermute | solution.py:176
  20.2 10.4 %copy-start.4 = (bf16[128,1536]{1,0:T(8,128)(2,1)}, bf16[128,1536]{1,0:T(8,128)(2,1)S(1)}, u32[]{:S(2)}) copy-start(bf16[128,1536]{1,0:T(8,128)(2,1)S(1)} %collective-permute-done.6.refs_8_) | copy-start | bytes 1179652
  20.2 12.4 %collective-permute-start.7 = (bf16[128,1536]{1,0:T(8,128)(2,1)S(1)}, bf16[128,1536]{1,0:T(8,128)(2,1)S(1)}, u32[]{:S(2)}, u32[]{:S(2)}) collective-permute-start(bf16[128,1536]{1,0:T(8,128)(2,1)S(1)} %collective-permute-done.6.refs_8_), channel_id=1, source_target_pairs={{0,63},{1,0},{2,1},{3,2},{4,3},{5,4},{6,5},{7,6},{8,7},{9,8},{10,9... | collective-permute-start | bytes 1179656 | tf_op jit(solution)/shard_map/ppermute | solution.py:176
  25.5 7.1 %copy-start.5 = (bf16[128,1536]{1,0:T(8,128)(2,1)}, bf16[128,1536]{1,0:T(8,128)(2,1)S(1)}, u32[]{:S(2)}) copy-start(bf16[128,1536]{1,0:T(8,128)(2,1)S(1)} %collective-permute-done.4.refs_6_) | copy-start | bytes 1179652
  25.5 10.7 %collective-permute-start.5 = (bf16[128,1536]{1,0:T(8,128)(2,1)S(1)}, bf16[128,1536]{1,0:T(8,128)(2,1)}, u32[]{:S(2)}, u32[]{:S(2)}) collective-permute-start(bf16[128,1536]{1,0:T(8,128)(2,1)S(1)} %collective-permute-done.4.refs_6_), channel_id=1, source_target_pairs={{0,1},{1,2},{2,3},{3,4},{4,5},{5,6},{6,7},{7,8},{8,9},{9,10},{10,1... | collective-permute-start | bytes 1179656 | tf_op jit(solution)/shard_map/ppermute | solution.py:176
  26.8 5.8 %copy-start.6 = (bf16[128,1536]{1,0:T(8,128)(2,1)}, bf16[128,1536]{1,0:T(8,128)(2,1)S(1)}, u32[]{:S(2)}) copy-start(bf16[128,1536]{1,0:T(8,128)(2,1)S(1)} %collective-permute-done.3.refs_4_) | copy-start | bytes 1179652
  30.6 2.0 %copy-start.7 = (bf16[128,1536]{1,0:T(8,128)(2,1)}, bf16[128,1536]{1,0:T(8,128)(2,1)S(1)}, u32[]{:S(2)}) copy-start(bf16[128,1536]{1,0:T(8,128)(2,1)S(1)} %collective-permute-done.1.refs_0_) | copy-start | bytes 1179652
  32.6 0.8 copy-start.8
  53.0 25.4 %copy-start.1 = (bf16[2,128,1536]{2,1,0:T(8,128)(2,1)S(1)}, bf16[2,128,1536]{2,1,0:T(8,128)(2,1)}, u32[]{:S(2)}) copy-start(bf16[2,128,1536]{2,1,0:T(8,128)(2,1)} %get-tuple-element.19) | copy-start | bytes 2359300
  53.0 22.0 %collective-permute-start.12 = (bf16[2,128,1536]{2,1,0:T(8,128)(2,1)}, bf16[2,128,1536]{2,1,0:T(8,128)(2,1)S(1)}, u32[]{:S(2)}, u32[]{:S(2)}) collective-permute-start(bf16[2,128,1536]{2,1,0:T(8,128)(2,1)} %get-tuple-element.21), channel_id=1, source_target_pairs={{0,63},{1,0},{2,1},{3,2},{4,3},{5,4},{6,5},{7,6},{8,7},{9,8},{10,9... | collective-permute-start | bytes 2359304 | tf_op jit(solution)/shard_map/ppermute | solution.py:176
  57.7 17.3 %collective-permute-start.13 = (bf16[2,128,1536]{2,1,0:T(8,128)(2,1)}, bf16[2,128,1536]{2,1,0:T(8,128)(2,1)S(1)}, u32[]{:S(2)}, u32[]{:S(2)}) collective-permute-start(bf16[2,128,1536]{2,1,0:T(8,128)(2,1)} %get-tuple-element.22), channel_id=1, source_target_pairs={{0,1},{1,2},{2,3},{3,4},{4,5},{5,6},{6,7},{7,8},{8,9},{9,10},{10,1... | collective-permute-start | bytes 2359304 | tf_op jit(solution)/shard_map/ppermute | solution.py:176
  57.7 3.8 %collective-permute-start.8 = (f32[1,1536]{1,0:T(1,128)}, f32[1,1536]{1,0:T(1,128)S(1)}, u32[]{:S(2)}, u32[]{:S(2)}) collective-permute-start(f32[1,1536]{1,0:T(1,128)} %get-tuple-element.20), channel_id=1, source_target_pairs={{0,64},{64,0},{128,192},{192,128},{1,65},{65,1},{129,193},{193,129... | collective-permute-start | bytes 18440 | tf_op jit(solution)/shard_map/ppermute | solution.py:193
  62.3 7.6 %collective-permute-start.11 = (f32[1,1536]{1,0:T(1,128)S(1)}, f32[1,1536]{1,0:T(1,128)S(1)}, u32[]{:S(2)}, u32[]{:S(2)}) collective-permute-start(f32[1,1536]{1,0:T(1,128)S(1)} %add.45), channel_id=1, source_target_pairs={{0,48},{4,52},{8,56},{12,60},{16,32},{20,36},{24,40},{28,44},{32,1... | collective-permute-start | bytes 18440 | tf_op jit(solution)/shard_map/ppermute | solution.py:186
  67.4 7.5 %collective-permute-start.10 = (f32[1,1536]{1,0:T(1,128)S(1)}, f32[1,1536]{1,0:T(1,128)S(1)}, u32[]{:S(2)}, u32[]{:S(2)}) collective-permute-start(f32[1,1536]{1,0:T(1,128)S(1)} %add.45), channel_id=1, source_target_pairs={{0,32},{4,36},{8,40},{12,44},{16,48},{20,52},{24,56},{28,60},{32,0... | collective-permute-start | bytes 18440 | tf_op jit(solution)/shard_map/ppermute | solution.py:186
  68.4 6.6 %collective-permute-start.9 = (f32[1,1536]{1,0:T(1,128)S(1)}, f32[1,1536]{1,0:T(1,128)S(1)}, u32[]{:S(2)}, u32[]{:S(2)}) collective-permute-start(f32[1,1536]{1,0:T(1,128)S(1)} %add.45), channel_id=1, source_target_pairs={{0,16},{4,20},{8,24},{12,28},{16,0},{20,4},{24,8},{28,12},{32,48},... | collective-permute-start | bytes 18440 | tf_op jit(solution)/shard_map/ppermute | solution.py:186
  76.3 24.5 %copy-start = (f32[2,128,1536]{2,1,0:T(8,128)S(1)}, f32[2,128,1536]{2,1,0:T(8,128)}, u32[]{:S(2)}) copy-start(f32[2,128,1536]{2,1,0:T(8,128)} %get-tuple-element.18) | copy-start | bytes 4718596
  76.3 24.5 %collective-permute-start.15 = (bf16[2,128,1536]{2,1,0:T(8,128)(2,1)S(1)}, bf16[2,128,1536]{2,1,0:T(8,128)(2,1)S(1)}, u32[]{:S(2)}, u32[]{:S(2)}) collective-permute-start(bf16[2,128,1536]{2,1,0:T(8,128)(2,1)S(1)} %add_convert_fusion.1), channel_id=1, source_target_pairs={{0,1},{1,2},{2,3},{3,4},{4,5},{5,6},{6,7},{7,8},{8,9},{9,10},{10,1... | collective-permute-start | bytes 2359304 | tf_op jit(solution)/shard_map/ppermute | solution.py:176
  78.5 22.3 %collective-permute-start.14 = (bf16[2,128,1536]{2,1,0:T(8,128)(2,1)S(1)}, bf16[2,128,1536]{2,1,0:T(8,128)(2,1)S(1)}, u32[]{:S(2)}, u32[]{:S(2)}) collective-permute-start(bf16[2,128,1536]{2,1,0:T(8,128)(2,1)S(1)} %add_convert_fusion.2), channel_id=1, source_target_pairs={{0,63},{1,0},{2,1},{3,2},{4,3},{5,4},{6,5},{7,6},{8,7},{9,8},{10,9... | collective-permute-start | bytes 2359304 | tf_op jit(solution)/shard_map/ppermute | solution.py:176
  82.1 5.1 %collective-permute-start.16 = (f32[1,1536]{1,0:T(1,128)S(1)}, f32[1,1536]{1,0:T(1,128)S(1)}, u32[]{:S(2)}, u32[]{:S(2)}) collective-permute-start(f32[1,1536]{1,0:T(1,128)S(1)} %add_add_fusion.1), channel_id=1, source_target_pairs={{0,128},{64,192},{128,0},{192,64},{1,129},{65,193},{129,1},{193,65... | collective-permute-start | bytes 18440 | tf_op jit(solution)/shard_map/ppermute | solution.py:193
  87.2 4.3 %collective-permute-start.19 = (f32[1,1536]{1,0:T(1,128)S(1)}, f32[1,1536]{1,0:T(1,128)S(1)}, u32[]{:S(2)}, u32[]{:S(2)}) collective-permute-start(f32[1,1536]{1,0:T(1,128)S(1)} %add.53), channel_id=1, source_target_pairs={{0,12},{4,8},{8,4},{12,0},{16,28},{20,24},{24,20},{28,16},{32,44},... | collective-permute-start | bytes 18440 | tf_op jit(solution)/shard_map/ppermute | solution.py:186
  87.9 5.4 %collective-permute-start.18 = (f32[1,1536]{1,0:T(1,128)S(1)}, f32[1,1536]{1,0:T(1,128)S(1)}, u32[]{:S(2)}, u32[]{:S(2)}) collective-permute-start(f32[1,1536]{1,0:T(1,128)S(1)} %add.53), channel_id=1, source_target_pairs={{0,8},{4,12},{8,0},{12,4},{16,24},{20,28},{24,16},{28,20},{32,40},... | collective-permute-start | bytes 18440 | tf_op jit(solution)/shard_map/ppermute | solution.py:186
  91.6 1.7 %collective-permute-start.17 = (f32[1,1536]{1,0:T(1,128)S(1)}, f32[1,1536]{1,0:T(1,128)S(1)}, u32[]{:S(2)}, u32[]{:S(2)}) collective-permute-start(f32[1,1536]{1,0:T(1,128)S(1)} %add.53), channel_id=1, source_target_pairs={{0,4},{4,0},{8,12},{12,8},{16,20},{20,16},{24,28},{28,24},{32,36},... | collective-permute-start | bytes 18440 | tf_op jit(solution)/shard_map/ppermute | solution.py:186
  93.3 6.9 %collective-permute-start.22 = (f32[1,1536]{1,0:T(1,128)S(1)}, f32[1,1536]{1,0:T(1,128)S(1)}, u32[]{:S(2)}, u32[]{:S(2)}) collective-permute-start(f32[1,1536]{1,0:T(1,128)S(1)} %add_add_fusion), channel_id=1, source_target_pairs={{0,3},{1,2},{2,1},{3,0},{4,7},{5,6},{6,5},{7,4},{8,11},{9,10},{10,... | collective-permute-start | bytes 18440 | tf_op jit(solution)/shard_map/ppermute | solution.py:186
  94.6 5.6 %collective-permute-start.21 = (f32[1,1536]{1,0:T(1,128)S(1)}, f32[1,1536]{1,0:T(1,128)S(1)}, u32[]{:S(2)}, u32[]{:S(2)}) collective-permute-start(f32[1,1536]{1,0:T(1,128)S(1)} %add_add_fusion), channel_id=1, source_target_pairs={{0,2},{1,3},{2,0},{3,1},{4,6},{5,7},{6,4},{7,5},{8,10},{9,11},{10,... | collective-permute-start | bytes 18440 | tf_op jit(solution)/shard_map/ppermute | solution.py:186
  94.6 5.6 %collective-permute-start.20 = (f32[1,1536]{1,0:T(1,128)S(1)}, f32[1,1536]{1,0:T(1,128)S(1)}, u32[]{:S(2)}, u32[]{:S(2)}) collective-permute-start(f32[1,1536]{1,0:T(1,128)S(1)} %add_add_fusion), channel_id=1, source_target_pairs={{0,1},{1,0},{2,3},{3,2},{4,5},{5,4},{6,7},{7,6},{8,9},{9,8},{10,11... | collective-permute-start | bytes 18440 | tf_op jit(solution)/shard_map/ppermute | solution.py:186
